TPU v7x, 128 devices: a whole 4x4x4 slice. The times are simulated.
128 devices in a mesh: wide: 16 (over z, x), narrow: 8 (over y, core).
Axes of the slice: x: 4, y: 4, z: 4, core: 2. Of those that a mesh axis runs over, the one named last changes fastest.
Arguments:
- queries: bfloat16 [4096, 4096], P('wide'), may hold values from -256 to 256
- span_keys: bfloat16 [4096, 1024], P('wide'), may hold values from -6 to 6
- span_values: bfloat16 [4096, 1024], P('wide'), may hold values from -6 to 6
- cache_keys: bfloat16 [524288, 128], P(('wide', 'narrow')), may hold values from -6 to 6
- cache_values: bfloat16 [524288, 128], P(('wide', 'narrow')), may hold values from -6 to 6
- chosen: int32 [8, 3], replicated, may hold values from 0 to 15, all different within a row; in each aligned block of 8 rows (0 to 7, 8 to 15, ...) at most 4 rows name the same one
- out_weight: bfloat16 [4096, 4096], P('wide', 'narrow'), may hold values from -0.09375 to 0.09375
Outputs:
- projected: bfloat16 [4096, 4096], P('wide', 'narrow')
Inputs may be any that keep to these rules, and one draw needn't show every extreme that they name: `chosen`: each row names 3 different key blocks; each key block is named by at most 4 rows and some block by exactly 4; every block is named by some row.
All inputs are finite; a program needn't handle non-finite values.
Results may differ from a plain program's by a relative error of at most 0.019.
Values may be sent and summed in bfloat16 or wider, within the bound.
A program may use at most 128 MiB of HBM per device.

v0:
```python
import math

import jax
import jax.numpy as jnp
from jax import lax
from jax.sharding import PartitionSpec as P

HEADS_DEV = 2
GROUP = 4
QB = 512
MOST = 4


FLOOR_SCORE = -1e30


def partner(value, axis, distance):
    mask = 2**distance
    pairs = [(source, source ^ mask) for source in range(lax.axis_size(axis))]
    return lax.ppermute(value, axis, pairs)


def combined_all(part, axis, combine):
    gathered = jax.tree.map(lambda a: lax.all_gather(a, axis), part)

    def take(source):
        return jax.tree.map(lambda a: lax.dynamic_index_in_dim(a, source, 0, False), gathered)

    return lax.fori_loop(
        1, lax.axis_size(axis), lambda source, state: combine(state, take(source)), take(0)
    )


def combine_parts(first_part, second_part):
    peak_first, total_first, sum_first = first_part
    peak_second, total_second, sum_second = second_part
    row_peak = jnp.maximum(peak_first, peak_second)
    weight_first = jnp.exp(peak_first - row_peak)
    weight_second = jnp.exp(peak_second - row_peak)
    row_total = total_first * weight_first + total_second * weight_second
    summed = sum_first * weight_first[..., None] + sum_second * weight_second[..., None]
    return (row_peak, row_total, summed)


def segment_terms(query_rows, key_rows, value_rows, score_scale, key_mask):
    scores = (
        jnp.einsum("hqd,kd->hqk", query_rows, key_rows, preferred_element_type=jnp.float32)
        * score_scale
    )
    if key_mask is not None:
        scores = jnp.where(key_mask, scores, FLOOR_SCORE)
    row_peak = jnp.max(scores, axis=-1)
    weights = jnp.exp(scores - row_peak[..., None])
    row_total = jnp.sum(weights, axis=-1)
    summed = jnp.einsum(
        "hqk,kd->hqd", weights.astype(jnp.bfloat16), value_rows, preferred_element_type=jnp.float32
    )
    return (row_peak, row_total, summed)


def block_partials(block_id, chosen, block_queries, key_rows, value_rows, score_scale):
    query_blocks, block_len, head_count, head_dim = block_queries.shape
    block_hits = jnp.any(chosen == block_id, axis=1).astype(jnp.int32)
    hit_rank = jnp.cumsum(block_hits)
    slot_numbers = jnp.arange(MOST, dtype=jnp.int32)
    slot_taken = (block_hits[None, :] == 1) & (hit_rank[None, :] == slot_numbers[:, None] + 1)
    slot_valid = jnp.any(slot_taken, axis=1)
    picked = jnp.sum(
        slot_taken.astype(jnp.int32) * jnp.arange(query_blocks, dtype=jnp.int32)[None, :], axis=1
    )
    slot_queries = jnp.transpose(jnp.take(block_queries, picked, axis=0), (0, 2, 1, 3)).reshape(
        MOST * head_count, block_len, head_dim
    )

    def one_slot(slot_query):
        row_peak, row_total, summed = segment_terms(
            slot_query[None], key_rows, value_rows, score_scale, None
        )
        return (row_peak[0], row_total[0], summed[0])

    slot_peaks, slot_totals, slot_sums = lax.map(one_slot, slot_queries)
    slot_peaks = slot_peaks.reshape(MOST, head_count, block_len)
    slot_totals = slot_totals.reshape(MOST, head_count, block_len)
    slot_sums = slot_sums.reshape(MOST, head_count, block_len, head_dim)
    dense_peak = jnp.full((query_blocks, head_count, block_len), FLOOR_SCORE, jnp.float32)
    dense_total = jnp.zeros((query_blocks, head_count, block_len), jnp.float32)
    dense_sum = jnp.zeros((query_blocks, head_count, block_len, head_dim), jnp.float32)
    for slot_index in range(MOST):
        target = picked[slot_index]
        live = slot_valid[slot_index]
        dense_peak = dense_peak.at[target].max(jnp.where(live, slot_peaks[slot_index], FLOOR_SCORE))
        dense_total = dense_total.at[target].add(jnp.where(live, slot_totals[slot_index], 0.0))
        dense_sum = dense_sum.at[target].add(jnp.where(live, slot_sums[slot_index], 0.0))
    return (dense_peak, dense_total, dense_sum)


def shards(queries, span_keys, span_values, cache_keys, cache_values, chosen, out_weight):
    axis_width = lax.axis_size("wide")
    part_count = lax.axis_size("narrow")
    wide_rows, columns = queries.shape
    head_dim = cache_keys.shape[1]
    kv_count = span_keys.shape[1] // head_dim
    score_scale = 1.0 / math.sqrt(head_dim)
    stacked = jnp.stack(
        [
            span_keys.reshape(wide_rows, kv_count, head_dim),
            span_values.reshape(wide_rows, kv_count, head_dim),
        ],
        axis=2,
    )
    stacked = jnp.repeat(stacked, axis_width // kv_count, axis=1).reshape(
        1, wide_rows, axis_width * 2 * head_dim
    )
    lifted = queries.reshape(1, wide_rows, columns)
    own_queries, span_pairs = (
        lax.all_to_all(lifted, "wide", split_axis=2, concat_axis=0, tiled=True),
        lax.all_to_all(stacked, "wide", split_axis=2, concat_axis=0, tiled=True),
    )
    tokens = axis_width * wide_rows
    query_blocks = tokens // QB
    own_queries = own_queries.reshape(tokens, HEADS_DEV, head_dim)
    span_pairs = span_pairs.reshape(tokens, 2, head_dim)
    parity = lax.axis_index("wide") % 2
    is_lower = parity == 0
    block_id = parity * part_count + lax.axis_index("narrow")
    partner_q = partner(own_queries, "wide", 0)
    grouped = jnp.where(
        is_lower,
        jnp.concatenate([own_queries, partner_q], 1),
        jnp.concatenate([partner_q, own_queries], 1),
    )
    dense_peak, dense_total, dense_sum = block_partials(
        block_id,
        chosen,
        grouped.reshape(query_blocks, QB, GROUP, head_dim),
        cache_keys,
        cache_values,
        score_scale,
    )

    def split_heads(array):
        first_half = array[:, :HEADS_DEV]
        second_half = array[:, HEADS_DEV:]
        return (
            jnp.where(is_lower, first_half, second_half),
            jnp.where(is_lower, second_half, first_half),
        )

    kept_peak, given_peak = split_heads(dense_peak)
    kept_total, given_total = split_heads(dense_total)
    kept_sum, given_sum = split_heads(dense_sum)
    received = partner((given_peak, given_total, given_sum), "wide", 0)
    merged = combine_parts((kept_peak, kept_total, kept_sum), received)
    blocks_each = query_blocks // part_count
    first_block = lax.axis_index("narrow") * blocks_each
    own_rows = lax.dynamic_slice_in_dim(
        own_queries.reshape(query_blocks, QB, HEADS_DEV, head_dim), first_block, blocks_each, 0
    )
    own_pairs = lax.dynamic_slice_in_dim(
        span_pairs.reshape(query_blocks, QB, 2, head_dim), first_block, blocks_each, 0
    )
    causal = jnp.arange(QB)[:, None] >= jnp.arange(QB)[None, :]

    def own_block(rows_and_pairs):
        query_rows, pair_rows = rows_and_pairs
        return segment_terms(
            jnp.transpose(query_rows, (1, 0, 2)),
            pair_rows[:, 0],
            pair_rows[:, 1],
            score_scale,
            causal[None],
        )

    own_parts = lax.map(own_block, (own_rows, own_pairs))
    current = tuple(
        (lax.dynamic_slice_in_dim(array, first_block, blocks_each, 0) for array in merged)
    )
    updated = combine_parts(current, own_parts)
    merged = tuple(
        (
            lax.dynamic_update_slice_in_dim(array, fresh, first_block, 0)
            for array, fresh in zip(merged, updated)
        )
    )
    row_peak, row_total, summed = combined_all(merged, "narrow", combine_parts)
    attended = (
        jnp.transpose(summed / row_total[..., None], (0, 2, 1, 3))
        .reshape(tokens, HEADS_DEV * head_dim)
        .astype(jnp.bfloat16)
    )
    projected = lax.psum_scatter(
        jnp.dot(attended, out_weight, preferred_element_type=jnp.float32).astype(jnp.bfloat16),
        "wide",
        scatter_dimension=0,
        tiled=True,
    )
    return projected


def solution(mesh):
    return jax.shard_map(
        shards,
        mesh=mesh,
        in_specs=(
            P("wide", None),
            P("wide", None),
            P("wide", None),
            P(("wide", "narrow"), None),
            P(("wide", "narrow"), None),
            P(),
            P("wide", "narrow"),
        ),
        out_specs=P("wide", "narrow"),
        check_vma=False,
    )
```

profile of v0, /device:TPU:1, one launch (start us, length us, event | category | flops | bytes accessed | tf_op | source)
XLA Modules:
  0.0 709.4 jit_solution(17999265716348660386)
XLA Ops:
  6.5 10.1 %copy.88 = bf16[1,256,4096]{1,0,2:T(2,128)(2,1)} copy(bf16[1,256,4096]{2,1,0:T(8,128)(2,1)} %bitcast.187) | data formatting | bytes 4194304 | tf_op jit(solution)/shard_map/reshape | solution.py:114
  17.1 21.6 %reduce.76 = bf16[4096,256]{1,0:T(8,128)(2,1)S(1)} reduce(bf16[4096,1,256]{2,1,0:T(2,128)(2,1)} %bitcast.175, bf16[]{:T(256)} %broadcast.316), dimensions={1}, to_apply=%bitcast.138.reduce_sub_computation | reduce | bytes 4194306
  40.8 35.8 %all_to_all.30 = bf16[16,2,32768]{2,1,0:T(2,128)(2,1)S(1)} all-to-all(bf16[16,2,32768]{2,1,0:T(2,128)(2,1)} %reshape.569), channel_id=1, replica_groups=mesh['wide'=16,'narrow'=8] {'wide'}, dimensions={0} | all-to-all | bytes 4194304 | tf_op jit(solution)/shard_map/all_to_all | solution.py:116
  76.6 6.8 reshape.570
  83.3 2.5 copy.123
  87.1 2.4 reshape.543
  91.5 25.1 %copy.153 = bf16[1,256,4096]{1,0,2:T(2,128)(2,1)} copy(bf16[1,256,4096]{1,2,0:T(8,128)(2,1)S(1)} %bitcast.181) | data formatting | bytes 4194304 | tf_op jit(solution)/shard_map/reshape;reshape | solution.py:111
  116.5 22.9 %reduce.77 = bf16[4096,256]{1,0:T(8,128)(2,1)} reduce(bf16[4096,1,256]{2,1,0:T(2,128)(2,1)} %bitcast.176, bf16[]{:T(256)} %broadcast.316), dimensions={1}, to_apply=%bitcast.157.reduce_sub_computation | reduce | bytes 4194306
  139.5 4.0 reshape.571
  143.5 4.4 all-to-all-start.1
  161.1 3.5 copy.92
  164.6 4.1 copy.91
  168.7 4.3 maximum_select_fusion
  173.0 4.4 gather_fusion
  177.5 3.1 broadcast_select_fusion
  180.6 97.0 %while.51 = (s32[]{:T(128)}, f32[16,512]{1,0:T(8,128)S(1)}, f32[16,512]{1,0:T(8,128)S(1)}, f32[16,512,128]{2,1,0:T(8,128)}, bf16[16,512,128]{2,1,0:T(8,128)(2,1)...) while((s32[]{:T(128)}, f32[16,512]{1,0:T(8,128)S(1)}, ...), condition=%wide.region_8.9_spmd, body=%wide.region_5.8_spmd.sunk | while | flops 1090518016 | bytes 27672692 | solution.py:81
  180.6 2.2 multiply_reduce_fusion.2
  186.7 2.2 multiply_reduce_fusion.2
  192.7 2.2 multiply_reduce_fusion.2
  198.8 2.2 multiply_reduce_fusion.2
  202.5 2.2 fusion.71
  204.9 2.2 multiply_reduce_fusion.2
  208.6 2.2 fusion.71
  210.9 2.2 multiply_reduce_fusion.2
  214.7 2.2 fusion.71
  217.0 2.2 multiply_reduce_fusion.2
  223.1 2.2 multiply_reduce_fusion.2
  226.8 2.2 fusion.71
  229.1 2.2 multiply_reduce_fusion.2
  232.9 2.2 fusion.71
  235.2 2.2 multiply_reduce_fusion.2
  241.3 2.2 multiply_reduce_fusion.2
  247.3 2.2 multiply_reduce_fusion.2
  251.1 2.2 fusion.71
  253.4 2.2 multiply_reduce_fusion.2
  257.2 2.2 fusion.71
  259.5 2.2 multiply_reduce_fusion.2
  263.2 2.2 fusion.71
  265.6 2.2 multiply_reduce_fusion.2
  271.6 2.2 multiply_reduce_fusion.2
  275.4 2.2 fusion.71
  285.6 2.7 slice_select_fusion
  292.2 10.5 %reshape.572 = bf16[4096,1,256]{2,1,0:T(2,128)(2,1)} reshape(bf16[16,2,32768]{2,1,0:T(2,128)(2,1)} %all-to-all-done.1) | data formatting | bytes 4194304
  302.6 2.5 copy.124
  306.4 2.2 reshape_reshape.8
  326.7 54.1 %collective-permute-done.1 = f32[8,2,512]{2,0,1:T(8,128)S(1)} collective-permute-done((f32[8,2,512]{2,0,1:T(8,128)S(1)}, f32[8,2,512]{2,0,1:T(8,128)S(1)}, u32[]{:S(2)}, u32[]{:S(2)}) %collective-permute-start.1) | collective-permute-done | bytes 32800 | tf_op jit(solution)/shard_map/ppermute | solution.py:20
  381.7 6.1 multiply_add_fusion
  391.7 16.3 %all_gather.29 = f32[8,8,2,512]{3,1,2,0:T(8,128)S(1)} all-gather(f32[1,8,2,512]{3,1,2,0:T(8,128)S(1)} %dynamic_update_slice.32), channel_id=1, replica_groups=mesh['wide'=16,'narrow'=8] {'narrow'}, dimensions={0}, use_global_device_ids=true | all-gather | bytes 294912 | tf_op jit(solution)/shard_map/all_gather | solution.py:24
  408.1 13.5 %all_gather.26 = f32[8,8,2,512]{3,1,2,0:T(8,128)S(1)} all-gather(f32[1,8,2,512]{3,1,2,0:T(8,128)S(1)} %dynamic_update_slice.31), channel_id=1, replica_groups=mesh['wide'=16,'narrow'=8] {'narrow'}, dimensions={0}, use_global_device_ids=true | all-gather | bytes 294912 | tf_op jit(solution)/shard_map/all_gather | solution.py:24
  421.7 130.9 %all-gather.2.cloned.1.call-done = f32[8,8,2,512,128]{4,3,2,1,0:T(8,128)} async-done(((f32[1,8,2,512,128]{4,3,2,1,0:T(8,128)}), f32[8,8,2,512,128]{4,3,2,1,0:T(8,128)}) %all-gather.2.cloned.1.call-update) | async-done | bytes 33554448 | tf_op jit(solution)/shard_map/all_gather | solution.py:24
  552.6 4.6 slice_bitcast_fusion
  557.2 56.9 %while.52 = (s32[]{:T(128)}, f32[8,2,512]{2,1,0:T(2,128)S(1)}, f32[8,2,512]{2,1,0:T(2,128)S(1)}, f32[8,2,512,128]{3,2,1,0:T(8,128)}, f32[8,8,2,512]{3,1,2,0:T(8,...) while((s32[]{:T(128)}, f32[8,2,512]{2,1,0:T(2,128)S(1)}, ...), condition=%wide.region_19.20_spmd, body=%wide.region_18.19_spmd.sunk | while | flops 3194885 | bytes 13041807 | solution.py:29
  557.3 8.0 %fusion.73 = f32[8,2,512,128]{3,2,1,0:T(8,128)} fusion(f32[8,8,2,512,128]{4,3,2,1,0:T(8,128)} %get-tuple-element.636, s32[]{:T(128)S(6)} %select_n.307, f32[8,2,512,128]{3,2,1,0:T(8,128)} %get-tuple-element.623, f32[8,2,512]{2,1,0:T(2,128)S(1)} %get-tuple-element.581, f32[8,2,512]{2,1,0:T(2,128)S(1)} %get-tuple-element.582), kind=kLoop, calls=%fused_computation.14.clone.1 | loop fusion | flops 3145728 | bytes 12648452 | tf_op jit(solution)/shard_map/while/body/eval_jaxpr/add | solution.py:41
  565.4 8.0 %fusion.73 = f32[8,2,512,128]{3,2,1,0:T(8,128)} fusion(f32[8,8,2,512,128]{4,3,2,1,0:T(8,128)} %get-tuple-element.636, s32[]{:T(128)S(6)} %select_n.307, f32[8,2,512,128]{3,2,1,0:T(8,128)} %get-tuple-element.623, f32[8,2,512]{2,1,0:T(2,128)S(1)} %get-tuple-element.581, f32[8,2,512]{2,1,0:T(2,128)S(1)} %get-tuple-element.582), kind=kLoop, calls=%fused_computation.14.clone.1 | loop fusion | flops 3145728 | bytes 12648452 | tf_op jit(solution)/shard_map/while/body/eval_jaxpr/add | solution.py:41
  573.6 8.0 %fusion.73 = f32[8,2,512,128]{3,2,1,0:T(8,128)} fusion(f32[8,8,2,512,128]{4,3,2,1,0:T(8,128)} %get-tuple-element.636, s32[]{:T(128)S(6)} %select_n.307, f32[8,2,512,128]{3,2,1,0:T(8,128)} %get-tuple-element.623, f32[8,2,512]{2,1,0:T(2,128)S(1)} %get-tuple-element.581, f32[8,2,512]{2,1,0:T(2,128)S(1)} %get-tuple-element.582), kind=kLoop, calls=%fused_computation.14.clone.1 | loop fusion | flops 3145728 | bytes 12648452 | tf_op jit(solution)/shard_map/while/body/eval_jaxpr/add | solution.py:41
  581.7 8.0 %fusion.73 = f32[8,2,512,128]{3,2,1,0:T(8,128)} fusion(f32[8,8,2,512,128]{4,3,2,1,0:T(8,128)} %get-tuple-element.636, s32[]{:T(128)S(6)} %select_n.307, f32[8,2,512,128]{3,2,1,0:T(8,128)} %get-tuple-element.623, f32[8,2,512]{2,1,0:T(2,128)S(1)} %get-tuple-element.581, f32[8,2,512]{2,1,0:T(2,128)S(1)} %get-tuple-element.582), kind=kLoop, calls=%fused_computation.14.clone.1 | loop fusion | flops 3145728 | bytes 12648452 | tf_op jit(solution)/shard_map/while/body/eval_jaxpr/add | solution.py:41
  589.8 8.0 %fusion.73 = f32[8,2,512,128]{3,2,1,0:T(8,128)} fusion(f32[8,8,2,512,128]{4,3,2,1,0:T(8,128)} %get-tuple-element.636, s32[]{:T(128)S(6)} %select_n.307, f32[8,2,512,128]{3,2,1,0:T(8,128)} %get-tuple-element.623, f32[8,2,512]{2,1,0:T(2,128)S(1)} %get-tuple-element.581, f32[8,2,512]{2,1,0:T(2,128)S(1)} %get-tuple-element.582), kind=kLoop, calls=%fused_computation.14.clone.1 | loop fusion | flops 3145728 | bytes 12648452 | tf_op jit(solution)/shard_map/while/body/eval_jaxpr/add | solution.py:41
  598.0 8.0 %fusion.73 = f32[8,2,512,128]{3,2,1,0:T(8,128)} fusion(f32[8,8,2,512,128]{4,3,2,1,0:T(8,128)} %get-tuple-element.636, s32[]{:T(128)S(6)} %select_n.307, f32[8,2,512,128]{3,2,1,0:T(8,128)} %get-tuple-element.623, f32[8,2,512]{2,1,0:T(2,128)S(1)} %get-tuple-element.581, f32[8,2,512]{2,1,0:T(2,128)S(1)} %get-tuple-element.582), kind=kLoop, calls=%fused_computation.14.clone.1 | loop fusion | flops 3145728 | bytes 12648452 | tf_op jit(solution)/shard_map/while/body/eval_jaxpr/add | solution.py:41
  606.1 8.0 %fusion.73 = f32[8,2,512,128]{3,2,1,0:T(8,128)} fusion(f32[8,8,2,512,128]{4,3,2,1,0:T(8,128)} %get-tuple-element.636, s32[]{:T(128)S(6)} %select_n.307, f32[8,2,512,128]{3,2,1,0:T(8,128)} %get-tuple-element.623, f32[8,2,512]{2,1,0:T(2,128)S(1)} %get-tuple-element.581, f32[8,2,512]{2,1,0:T(2,128)S(1)} %get-tuple-element.582), kind=kLoop, calls=%fused_computation.14.clone.1 | loop fusion | flops 3145728 | bytes 12648452 | tf_op jit(solution)/shard_map/while/body/eval_jaxpr/add | solution.py:41
  614.1 2.9 fusion.19
  617.0 3.0 copy.117
  619.9 2.5 copy.127
  622.4 3.2 convolution_convert_fusion
  625.7 76.9 %reduce-scatter.2.cloned.1.call-done = bf16[256,512]{1,0:T(8,128)(2,1)} async-done(((bf16[4096,512]{1,0:T(8,128)(2,1)}), bf16[256,512]{1,0:T(8,128)(2,1)}) %reduce-scatter.2.cloned.1.call-update) | async-done | bytes 262160 | tf_op jit(solution)/shard_map/reduce_scatter | solution.py:191
  (165 shorter events, 89.2 us)
Async XLA Ops:
  6.5 615.9 %copy-start = (bf16[256,512]{1,0:T(8,128)(2,1)S(1)}, bf16[256,512]{1,0:T(8,128)(2,1)}, u32[]{:S(2)}) copy-start(bf16[256,512]{1,0:T(8,128)(2,1)} %param.41) | copy-start | bytes 786436
  85.9 3.8 copy-start.5
  89.5 75.1 %collective-permute-start = (bf16[4096,2,128]{0,2,1:T(8,128)(2,1)}, bf16[4096,2,128]{0,2,1:T(8,128)(2,1)}, u32[]{:S(2)}, u32[]{:S(2)}) collective-permute-start(bf16[4096,2,128]{0,2,1:T(8,128)(2,1)} %reshape.543), channel_id=1, source_target_pairs={{0,8},{8,0},{16,24},{24,16},{32,40},{40,32},{48,56},{56,48},{64,72... | collective-permute-start | bytes 6291464 | tf_op jit(solution)/shard_map/ppermute | solution.py:20
  139.5 8.7 %copy-start.6 = (s32[8,3]{0,1:T(4,128)S(1)}, s32[8,3]{0,1:T(4,128)}, u32[]{:S(2)}) copy-start(s32[8,3]{0,1:T(4,128)} %param.40) | copy-start | bytes 292
  139.5 17.1 %copy-start.7 = (s32[4]{0:T(128)S(1)}, s32[4]{0:T(128)}, u32[]{:S(2)}) copy-start(s32[4]{0:T(128)} %constant.392.clone.1) | copy-start | bytes 52
  143.5 148.7 %all-to-all-start.1 = ((bf16[16,2,32768]{2,1,0:T(2,128)(2,1)}), bf16[16,2,32768]{2,1,0:T(2,128)(2,1)}, u32[]{:S(2)}, u32[]{:S(2)}) async-start(bf16[16,2,32768]{2,1,0:T(2,128)(2,1)} %reshape.571), calls=%async_computation.1 | async-start | bytes 4194304 | tf_op jit(solution)/shard_map/all_to_all | solution.py:117
  147.9 404.7 %all-gather.2.cloned.1.call-start = ((), (), s32[]{:S(2)}) async-start(), calls=%async_computation.3 | async-start | bytes 37748736 | tf_op jit(solution)/shard_map/all_gather | solution.py:24
  173.0 7.6 %copy-start.2 = (bf16[4096,128]{1,0:T(8,128)(2,1)S(1)}, bf16[4096,128]{1,0:T(8,128)(2,1)}, u32[]{:S(2)}) copy-start(bf16[4096,128]{1,0:T(8,128)(2,1)} %param.38) | copy-start | bytes 3145732
  173.0 7.6 %copy-start.3 = (bf16[4096,128]{1,0:T(8,128)(2,1)S(1)}, bf16[4096,128]{1,0:T(8,128)(2,1)}, u32[]{:S(2)}) copy-start(bf16[4096,128]{1,0:T(8,128)(2,1)} %param.39) | copy-start | bytes 3145732
  277.7 2.2 copy-start.4
  285.6 4.5 copy-start.1
  285.6 5.7 copy-start.8
  290.1 91.6 %collective-permute-start.3 = (f32[8,2,512,128]{3,2,1,0:T(8,128)}, f32[8,2,512,128]{3,2,1,0:T(8,128)}, u32[]{:S(2)}, u32[]{:S(2)}) collective-permute-start(f32[8,2,512,128]{3,2,1,0:T(8,128)} %slice_select_fusion), channel_id=1, source_target_pairs={{0,8},{8,0},{16,24},{24,16},{32,40},{40,32},{48,56},{56,48},{64,72... | collective-permute-start | bytes 12582920 | tf_op jit(solution)/shard_map/ppermute | solution.py:20
  319.5 61.4 %collective-permute-start.1 = (f32[8,2,512]{2,0,1:T(8,128)S(1)}, f32[8,2,512]{2,0,1:T(8,128)S(1)}, u32[]{:S(2)}, u32[]{:S(2)}) collective-permute-start(f32[8,2,512]{2,0,1:T(8,128)S(1)} %slice_select_fusion.1), channel_id=1, source_target_pairs={{0,8},{8,0},{16,24},{24,16},{32,40},{40,32},{48,56},{56,48},{64,72... | collective-permute-start | bytes 98312 | tf_op jit(solution)/shard_map/ppermute | solution.py:20
  325.0 56.6 %collective-permute-start.2 = (f32[8,2,512]{2,1,0:T(2,128)S(1)}, f32[8,2,512]{2,1,0:T(2,128)S(1)}, u32[]{:S(2)}, u32[]{:S(2)}) collective-permute-start(f32[8,2,512]{2,1,0:T(2,128)S(1)} %get-tuple-element.464), channel_id=1, source_target_pairs={{0,8},{8,0},{16,24},{24,16},{32,40},{40,32},{48,56},{56,48},{64,72... | collective-permute-start | bytes 98312 | tf_op jit(solution)/shard_map/ppermute | solution.py:20
  391.6 311.0 %reduce-scatter.2.cloned.1.call-start = ((), (), s32[]{:S(2)}) async-start(), calls=%async_computation.4 | async-start | bytes 4456448 | tf_op jit(solution)/shard_map/reduce_scatter | solution.py:191
Sparse Core Ops, SparseCore 0:
  391.7 160.8 all-gather.1
  625.8 76.7 reduce-scatter.1
where the time goes:
time: 713 us; the launch traced here: 709 us
  waiting for transfers between devices  263 us (37%)
  other arithmetic  164 us (23%)
  local copies, waits for them, and re-layouts  111 us (16%)
  matrix products  76.3 us (11%)
  blocking collectives  65.6 us (9%)
  between operations  21.1 us (3%)
  starting transfers between devices  7.76 us (1%)
    all_gather x1, waiting for transfers between devices, combined_all(): gathered = jax.tree.map(lambda a: lax.all_gather(a, axis), part)  131 us
    reduce_scatter x1, waiting for transfers between devices, shards(): lax.psum_scatter(jnp.dot(attended, out_weight, preferred_element_type=jnp...  76.9 us
    add x8, other arithmetic, combine_parts(): sum_first * weight_first[..., None] + sum_second * weight_second[..., None]  62.2 us
    ppermute x4, waiting for transfers between devices, partner(): return lax.ppermute(value, axis, pairs)  54.8 us
    unnamed x2, other arithmetic  44.5 us
    dot_general x17, matrix products, segment_terms(): jnp.einsum('hqk,kd->hqd', weights.astype(jnp.bfloat16), value_rows, prefe...  36.7 us
    unnamed x29, local copies, waits for them, and re-layouts  36.5 us
    dot_general x17, matrix products, segment_terms(): jnp.einsum('hqd,kd->hqk', query_rows, key_rows, preferred_element_type=jn...  36.3 us
  transfers between devices with their start and end apart: 7, of which 4 were waited for; matrix products, arithmetic and copies ran while one was open for 31% of the time, Pallas kernels for 0%

commit v1 on v0

v1 whole, which is shorter than its diff:
```python
import math

import jax
import jax.numpy as jnp
from jax import lax
from jax.experimental import pallas as pl
from jax.experimental.pallas import tpu as pltpu
from jax.sharding import PartitionSpec as P

HD = 128
QB = 512
KB = 4096
NQB = 8
NW = 16
KVH = 8
HALF = 256
ROWS = 2 * QB
CHUNK = 512
FLOOR_SCORE = -1e30
SCALE2 = math.log2(math.e) / math.sqrt(HD)
MESH = pl.DeviceIdType.MESH
MIB = 2**20


def place():
    wide = lax.axis_index("wide")
    narrow = lax.axis_index("narrow")
    return wide, narrow, narrow // 2, narrow % 2


def remote(src, dst, send_sem, recv_sem, device):
    return pltpu.make_async_remote_copy(
        src_ref=src, dst_ref=dst, send_sem=send_sem, recv_sem=recv_sem, device_id=device, device_id_type=MESH
    )


def spread_kernel(
    queries, span_k, span_v, cache_k, cache_v,
    q_out, pk_out, pv_out, sk_out, sv_out,
    q_send, q_recv, kv_send, kv_recv, span_send, span_recv, local_sem, span_local,
):
    wide, narrow, y, core = place()
    buddy = y * 2 + 1 - core
    block, half = wide // 2, wide % 2
    barrier = pltpu.get_barrier_semaphore()

    def greet(step, carry):
        pl.semaphore_signal(
            barrier, inc=1, device_id=((wide + step) % NW, narrow), device_id_type=MESH
        )
        return carry

    lax.fori_loop(1, NW, greet, 0)
    pl.semaphore_signal(barrier, inc=1, device_id=(wide, buddy), device_id_type=MESH)
    pl.semaphore_wait(barrier, NW)

    def q_src(kv, head):
        column = pl.multiple_of(kv * 512 + core * 256 + head * HD, HD)
        return queries.at[:, pl.ds(column, HD)]

    def q_dst(source, head):
        return q_out.at[source // 2, pl.ds(pl.multiple_of(head * QB + source % 2 * HALF, HALF), HALF), :]

    def span_pair(kv, which):
        src = (span_k, span_v)[which].at[:, pl.ds(pl.multiple_of(kv * HD, HD), HD)]
        return src

    def span_dst(part, which):
        return (sk_out, sv_out)[which].at[pl.ds(pl.multiple_of(part * HALF, HALF), HALF), :]

    def q_copy(step, head):
        target = (wide + step) % NW
        return remote(
            q_src(target // 2, head), q_dst(wide, head),
            q_send.at[step, head], q_recv.at[wide, head], (target, narrow),
        )

    kv_copies = [
        remote(src, dst, kv_send.at[i], kv_recv.at[i], (wide, buddy))
        for i, (src, dst) in enumerate(((cache_k, pk_out), (cache_v, pv_out)))
    ]
    span_owner = y == block % 4

    def span_copy(kv, which):
        return remote(
            span_pair(kv, which), span_dst(half, which),
            span_send.at[kv, which], span_recv.at[half, which], (kv * 2 + block // 4, narrow),
        )

    def span_own(kv, which):
        return pltpu.make_async_copy(span_pair(kv, which), span_dst(half, which), span_local.at[which])

    self_span = span_owner & (half == block // 4)

    def start_q(step, carry):
        for head in range(2):
            q_copy(step, head).start()
        return carry

    lax.fori_loop(1, NW, start_q, 0)
    for head in range(2):
        pltpu.make_async_copy(q_src(wide // 2, head), q_dst(wide, head), local_sem.at[head]).start()

    def each_span(kv, carry, act):
        @pl.when(span_owner & (kv * 2 + block // 4 != wide))
        def _():
            for which in range(2):
                act(span_copy(kv, which))

        return carry

    lax.fori_loop(0, KVH, lambda kv, c: each_span(kv, c, lambda copy: copy.start()), 0)

    @pl.when(self_span)
    def _():
        for which in range(2):
            span_own(block, which).start()

    for copy in kv_copies:
        copy.start()

    for head in range(2):
        pltpu.make_async_copy(q_src(wide // 2, head), q_dst(wide, head), local_sem.at[head]).wait()

    def wait_q(step, carry):
        source = (wide + NW - step) % NW
        for head in range(2):
            q_copy(step, head).wait_send()
            remote(
                q_src(0, head), q_dst(source, head), q_send.at[step, head], q_recv.at[source, head], (source, narrow)
            ).wait_recv()
        return carry

    lax.fori_loop(1, NW, wait_q, 0)
    lax.fori_loop(0, KVH, lambda kv, c: each_span(kv, c, lambda copy: copy.wait_send()), 0)

    @pl.when(self_span)
    def _():
        for which in range(2):
            span_own(block, which).wait()

    held = wide % 2 * 4 + y
    for part in range(2):
        @pl.when(held * 2 + part != wide)
        def _():
            for which in range(2):
                remote(
                    span_pair(0, which), span_dst(part, which),
                    span_send.at[0, which], span_recv.at[part, which], (wide, buddy),
                ).wait_recv()

    for copy in kv_copies:
        copy.wait()


def spread(queries, span_k, span_v, cache_k, cache_v):
    anywhere = pl.BlockSpec(memory_space=pl.ANY)
    shape = lambda *dims: jax.ShapeDtypeStruct(dims, jnp.bfloat16)
    dma = pltpu.SemaphoreType.DMA
    return pl.pallas_call(
        spread_kernel,
        out_shape=[shape(NQB, ROWS, HD), shape(KB, HD), shape(KB, HD), shape(QB, HD), shape(QB, HD)],
        in_specs=[anywhere] * 5,
        out_specs=[anywhere] * 5,
        scratch_shapes=[
            dma((NW, 2)), dma((NW, 2)), dma((2,)), dma((2,)), dma((KVH, 2)), dma((2, 2)), dma((2,)), dma((2,)),
        ],
        compiler_params=pltpu.CompilerParams(collective_id=0, has_side_effects=True),
    )(queries, span_k, span_v, cache_k, cache_v)


def attend_kernel(chosen, q, k_own, v_own, k_pair, v_pair, sk, sv, out, lse, k_both, v_wide, s_wide, acc, peak):
    wide, narrow, y, core = place()
    held = wide % 2 * 4 + y
    first = wide % 2 * 8 + y * 2
    k_both[0] = k_own[...]
    k_both[1] = k_pair[...]
    for i, v in enumerate((v_own, v_pair)):
        v_wide[i, :, :HD] = v[...]
        v_wide[i, :, HD:] = jnp.ones((KB, HD), jnp.bfloat16)
    s_wide[:, :HD] = sv[...]
    s_wide[:, HD:] = jnp.ones((QB, HD), jnp.bfloat16)

    def fold(state, queries, keys, values, mask):
        top, total = state
        scores = lax.dot_general(queries, keys, (((1,), (1,)), ((), ())), preferred_element_type=jnp.float32)
        if mask is not None:
            scores = jnp.where(mask, scores, FLOOR_SCORE)
        new_top = jnp.maximum(top, jnp.max(scores, axis=1, keepdims=True))
        decay = jnp.exp2((top - new_top) * SCALE2)
        weights = jnp.exp2((scores - new_top) * SCALE2).astype(jnp.bfloat16)
        total = total * decay + jnp.dot(weights, values, preferred_element_type=jnp.float32)
        return new_top, total

    def load():
        return peak[:, :1], acc[...]

    def save(state):
        peak[...] = jnp.broadcast_to(state[0], (ROWS, HD))
        acc[...] = state[1]

    def one_block(b, carry):
        hits = []
        for i in range(2):
            c = first + jnp.where(core == 0, i, 1 - i)
            hits.append((chosen[b, 0] == c) | (chosen[b, 1] == c) | (chosen[b, 2] == c))
        used = hits[0] | hits[1] | (b == held)

        @pl.when(used)
        def _():
            acc[...] = jnp.zeros((ROWS, 2 * HD), jnp.float32)
            peak[...] = jnp.full((ROWS, HD), FLOOR_SCORE, jnp.float32)

        @pl.when(b == held)
        def _():
            row = lax.broadcasted_iota(jnp.int32, (ROWS, QB), 0) % QB
            mask = row >= lax.broadcasted_iota(jnp.int32, (ROWS, QB), 1)
            save(fold(load(), q[b], sk[...], s_wide[...], mask))

        def cached(i, carry):
            @pl.when(jnp.where(i == 0, hits[0], hits[1]))
            def _():
                queries = q[b]
                state = load()
                for start in range(0, KB, CHUNK):
                    state = fold(
                        state, queries, k_both[i, start:start + CHUNK, :], v_wide[i, start:start + CHUNK, :], None
                    )
                save(state)

            return carry

        lax.fori_loop(0, 2, cached, 0)

        @pl.when(used)
        def _():
            total = acc[:, HD:]
            out[b] = (acc[:, :HD] / total).astype(jnp.bfloat16)
            logs = peak[...] * SCALE2 + jnp.log2(total)
            eye = lax.broadcasted_iota(jnp.int32, (HD, HD), 0) == lax.broadcasted_iota(jnp.int32, (HD, HD), 1)
            for g in range(ROWS // HD):
                lse[b, g:g + 1, :] = jnp.sum(
                    jnp.where(eye, logs[g * HD:(g + 1) * HD], 0.0), axis=0, keepdims=True
                )

        @pl.when(jnp.logical_not(used))
        def _():
            out[b] = jnp.zeros((ROWS, HD), jnp.bfloat16)
            lse[b] = jnp.full((8, HD), FLOOR_SCORE, jnp.float32)

        return carry

    lax.fori_loop(0, NQB, one_block, 0)


def attend(chosen, q, k_own, v_own, k_pair, v_pair, sk, sv):
    vmem = pl.BlockSpec(memory_space=pltpu.VMEM)
    return pl.pallas_call(
        attend_kernel,
        out_shape=[
            jax.ShapeDtypeStruct((NQB, ROWS, HD), jnp.bfloat16),
            jax.ShapeDtypeStruct((NQB, 8, HD), jnp.float32),
        ],
        in_specs=[pl.BlockSpec(memory_space=pltpu.SMEM)] + [vmem] * 7,
        out_specs=[vmem] * 2,
        scratch_shapes=[
            pltpu.VMEM((2, KB, HD), jnp.bfloat16),
            pltpu.VMEM((2, KB, 2 * HD), jnp.bfloat16),
            pltpu.VMEM((QB, 2 * HD), jnp.bfloat16),
            pltpu.VMEM((ROWS, 2 * HD), jnp.float32),
            pltpu.VMEM((ROWS, HD), jnp.float32),
        ],
        compiler_params=pltpu.CompilerParams(vmem_limit_bytes=56 * MIB),
        cost_estimate=pl.CostEstimate(flops=14 * 10**9, bytes_accessed=10 * MIB, transcendentals=25 * 10**6),
    )(chosen, q, k_own, v_own, k_pair, v_pair, sk, sv)


def finish_kernel(
    part, lse, weight, result,
    p_in, l_in, w_in, rows_out, rows_in,
    p_send, p_recv, l_send, l_recv, a_send, a_recv, f_send, f_recv, local_sem,
):
    wide, narrow, y, core = place()
    buddy = y * 2 + 1 - core
    kv = wide // 2
    held = wide % 2 * 4 + y
    mine = wide // 2
    barrier = pltpu.get_barrier_semaphore()

    def combiner(b):
        return kv * 2 + b // 4, b % 4 * 2 + core

    def source(s):
        return s * 2 + mine // 4, mine % 4 * 2 + core

    def target(t):
        return held * 2 + t // 4, t % 4 * 2 + core

    own_target = wide // 2 == held
    fetch = pltpu.make_async_copy(weight, w_in, local_sem.at[0])
    fetch.start()
    keep = [
        pltpu.make_async_copy(part.at[held], p_in.at[held], local_sem.at[1]),
        pltpu.make_async_copy(lse.at[held], l_in.at[held], local_sem.at[2]),
    ]
    for copy in keep:
        copy.start()

    def greet(step, carry):
        pl.semaphore_signal(barrier, inc=1, device_id=combiner((held + step) % 8), device_id_type=MESH)
        return carry

    lax.fori_loop(1, 8, greet, 0)

    def greet_source(s, carry):
        @pl.when(jnp.logical_not(own_target & (s == kv)))
        def _():
            pl.semaphore_signal(barrier, inc=1, device_id=source(s), device_id_type=MESH)

        return carry

    lax.fori_loop(0, 8, greet_source, 0)
    pl.semaphore_signal(barrier, inc=1, device_id=(wide, buddy), device_id_type=MESH)
    pl.semaphore_wait(barrier, 16 - own_target.astype(jnp.int32))

    def part_copies(step):
        b = (held + step) % 8
        return [
            remote(part.at[b], p_in.at[held], p_send.at[step], p_recv.at[held], combiner(b)),
            remote(lse.at[b], l_in.at[held], l_send.at[step], l_recv.at[held], combiner(b)),
        ]

    def start_part(step, carry):
        for copy in part_copies(step):
            copy.start()
        return carry

    lax.fori_loop(1, 8, start_part, 0)
    for copy in keep:
        copy.wait()

    def wait_part(step, carry):
        for copy in part_copies(step):
            copy.wait_send()
        s = (held + step) % 8
        remote(part.at[s], p_in.at[s], p_send.at[step], p_recv.at[s], combiner(s)).wait_recv()
        remote(lse.at[s], l_in.at[s], l_send.at[step], l_recv.at[s], combiner(s)).wait_recv()
        return carry

    lax.fori_loop(1, 8, wait_part, 0)

    logs = l_in[...]
    shares = jnp.exp2(logs - jnp.max(logs, axis=0, keepdims=True))
    shares = shares / jnp.sum(shares, axis=0, keepdims=True)
    turned = jnp.transpose(jnp.concatenate([shares.reshape(64, HD)] * 2, axis=0))
    for g in range(8):
        total = jnp.zeros((HD, HD), jnp.float32)
        for s in range(8):
            rows = p_in[s, g * HD:(g + 1) * HD, :].astype(jnp.float32)
            total = total + rows * turned[:, s * 8 + g:s * 8 + g + 1]
        rows_out[g % 4 * HD:(g % 4 + 1) * HD, g // 4 * HD:(g // 4 + 1) * HD] = total.astype(jnp.bfloat16)

    slot = kv * 2 + core

    def out_part(t):
        return rows_out.at[pl.ds(pl.multiple_of(t // 4 * HALF, HALF), HALF), :]

    def row_copy(t):
        return remote(out_part(t), rows_in.at[slot], a_send.at[t], a_recv.at[slot], target(t))

    own_number = wide % 2 * 4 + y

    def start_row(t, carry):
        away = jnp.logical_not(own_target & (t == own_number))

        @pl.when(away)
        def _():
            row_copy(t).start()

        @pl.when(jnp.logical_not(away))
        def _():
            copy = pltpu.make_async_copy(out_part(t), rows_in.at[slot], local_sem.at[3])
            copy.start()
            copy.wait()

        return carry

    lax.fori_loop(0, 8, start_row, 0)

    def forward(s):
        n = s * 2 + core
        return remote(rows_in.at[n], rows_in.at[n], f_send.at[s], f_recv.at[n], (wide, buddy))

    fetch.wait()

    def product(n):
        return jnp.dot(
            rows_in[n], w_in[pl.ds(pl.multiple_of(n * HALF, HALF), HALF), :], preferred_element_type=jnp.float32
        )

    def arrive(s, total):
        n = s * 2 + core

        @pl.when(jnp.logical_not(own_target & (s == kv)))
        def _():
            remote(rows_in.at[n], rows_in.at[n], f_send.at[s], a_recv.at[n], (wide, buddy)).wait_recv()

        forward(s).start()
        return total + product(n)

    total = lax.fori_loop(0, 8, arrive, jnp.zeros((HALF, 512), jnp.float32))

    def arrive_pair(s, total):
        n = s * 2 + 1 - core
        remote(rows_in.at[n], rows_in.at[n], f_send.at[s], f_recv.at[n], (wide, buddy)).wait_recv()
        return total + product(n)

    total = lax.fori_loop(0, 8, arrive_pair, total)
    result[...] = total.astype(jnp.bfloat16)

    def drain(t, carry):
        @pl.when(jnp.logical_not(own_target & (t == own_number)))
        def _():
            row_copy(t).wait_send()

        forward(t).wait_send()
        return carry

    lax.fori_loop(0, 8, drain, 0)


def finish(part, lse, weight):
    anywhere = pl.BlockSpec(memory_space=pl.ANY)
    dma = pltpu.SemaphoreType.DMA
    return pl.pallas_call(
        finish_kernel,
        out_shape=jax.ShapeDtypeStruct((HALF, 512), jnp.bfloat16),
        in_specs=[anywhere] * 3,
        out_specs=pl.BlockSpec(memory_space=pltpu.VMEM),
        scratch_shapes=[
            pltpu.VMEM((8, ROWS, HD), jnp.bfloat16),
            pltpu.VMEM((8, 8, HD), jnp.float32),
            pltpu.VMEM((4096, 512), jnp.bfloat16),
            pltpu.VMEM((QB, 256), jnp.bfloat16),
            pltpu.VMEM((16, HALF, 256), jnp.bfloat16),
            dma((8,)), dma((8,)), dma((8,)), dma((8,)), dma((8,)), dma((16,)), dma((8,)), dma((16,)), dma((4,)),
        ],
        compiler_params=pltpu.CompilerParams(
            collective_id=1, has_side_effects=True, vmem_limit_bytes=48 * MIB
        ),
    )(part, lse, weight)


def shards(queries, span_keys, span_values, cache_keys, cache_values, chosen, out_weight):
    weight = lax.all_gather(out_weight, "wide", axis=0, tiled=True)
    q, k_pair, v_pair, sk, sv = spread(queries, span_keys, span_values, cache_keys, cache_values)
    part, lse = attend(chosen, q, cache_keys, cache_values, k_pair, v_pair, sk, sv)
    return finish(part, lse, weight)


def solution(mesh):
    return jax.shard_map(
        shards,
        mesh=mesh,
        in_specs=(
            P("wide", None),
            P("wide", None),
            P("wide", None),
            P(("wide", "narrow"), None),
            P(("wide", "narrow"), None),
            P(),
            P("wide", "narrow"),
        ),
        out_specs=P("wide", "narrow"),
        check_vma=False,
    )
```

time: 713 us -> 229 us (0.32)
  the two profiles are of different devices: /device:TPU:1 before, /device:TPU:26 now
where the time goes in v1:
time: 229 us
  Pallas kernels  210 us (92%)
  between operations  13.4 us (6%)
  local copies, waits for them, and re-layouts  4.4 us (2%)
    pallas_call x1, Pallas kernels, finish(): pl.pallas_call(finish_kernel, out_shape=jax.ShapeDtypeStruct((HALF, 512),...  127 us
    pallas_call x1, Pallas kernels, spread(): pl.pallas_call(spread_kernel, out_shape=[shape(NQB, ROWS, HD), shape(KB,...  49.4 us
    pallas_call x1, Pallas kernels, attend(): pl.pallas_call(attend_kernel, out_shape=[jax.ShapeDtypeStruct((NQB, ROWS,...  34 us
  transfers between devices with their start and end apart: 1, of which 0 were waited for; matrix products, arithmetic and copies ran while one was open for 1% of the time, Pallas kernels for 36%

profile of v1, /device:TPU:26, one launch (start us, length us, event | category | flops | bytes accessed | tf_op | source)
XLA Modules:
  0.0 228.6 jit_solution(2034841230701060119)
XLA Ops:
  6.5 0.0 all-gather.2.cloned.1.call-start
  6.5 0.7 all-gather.2.cloned.1.call-update
  7.3 1.3 copy.8.chosen
  8.6 49.4 %shard_map.73 = (bf16[8,1024,128]{2,1,0:T(8,128)(2,1)}, bf16[4096,128]{1,0:T(8,128)(2,1)}, bf16[4096,128]{1,0:T(8,128)(2,1)}, bf16[512,128]{1,0:T(8,128)(2,1)}, bf16[512,128]{1,0:T(8,128)(2,1)}) custom-call(bf16[256,4096]{1,0:T(8,128)(2,1)} %queries.1, bf16[256,1024]{1,0:T(8,128)(2,1)} %span_k.1, bf16[256,1024]{1,0:T(8,128)(2,1)} %span_v.1, ...), custom_call_target="tpu_custom_call" | custom-call | tf_op jit(solution)/shard_map/pallas_call | solution.py:160
  58.0 34.0 %shard_map.74 = (bf16[8,1024,128]{2,1,0:T(8,128)(2,1)}, f32[8,8,128]{2,1,0:T(8,128)}) custom-call(s32[8,3]{1,0:T(8,128)} %copy.8.chosen, bf16[8,1024,128]{2,1,0:T(8,128)(2,1)} %get-tuple-element.12.q, bf16[4096,128]{1,0:T(8,128)(2,1)} %k_own.1, bf16[4096,128]{1,0:T(8,128)(2,1)} %v_own.1, bf16[4096,128]{1,0:T(8,128)(2,1)} %get-tuple-element.13.k_pair, ...), custom_call_target="tpu_custom_call" | custom-call | flops 14000000000 | bytes 10485760 | tf_op jit(solution)/shard_map/pallas_call | solution.py:258
  92.0 0.0 all-gather.2.cloned.1.call-done.weight
  92.0 0.0 copy-start
  92.0 1.6 copy-done
  93.6 0.0 copy-start.1
  93.6 0.8 copy-done.1
  94.4 126.7 %shard_map.75 = bf16[256,512]{1,0:T(8,128)(2,1)S(1)} custom-call(bf16[8,1024,128]{2,1,0:T(8,128)(2,1)S(1)} %copy-done, f32[8,8,128]{2,1,0:T(8,128)S(1)} %copy-done.1, bf16[4096,512]{1,0:T(8,128)(2,1)} %all-gather.2.cloned.1.call-done.weight), custom_call_target="tpu_custom_call" | custom-call | tf_op jit(solution)/shard_map/pallas_call | solution.py:435
  221.0 0.7 copy.10
Async XLA Ops:
  6.5 85.5 %all-gather.2.cloned.1.call-start = ((), (), s32[]{:S(2)}) async-start(), calls=%async_computation | async-start | bytes 4456448 | tf_op jit(solution)/shard_map/all_gather | solution.py:455
  92.0 1.6 copy-start
  93.6 0.8 copy-start.1
Sparse Core Ops, SparseCore 0:
  9.5 76.9 all-gather.1

commit v2 on v1

--- a/solution.py
+++ b/solution.py
@@ -15,7 +15,7 @@
 KVH = 8
 HALF = 256
 ROWS = 2 * QB
-CHUNK = 512
+CHUNK = 256
 FLOOR_SCORE = -1e30
 SCALE2 = math.log2(math.e) / math.sqrt(HD)
 MESH = pl.DeviceIdType.MESH
@@ -165,21 +165,34 @@
         scratch_shapes=[
             dma((NW, 2)), dma((NW, 2)), dma((2,)), dma((2,)), dma((KVH, 2)), dma((2, 2)), dma((2,)), dma((2,)),
         ],
-        compiler_params=pltpu.CompilerParams(collective_id=0, has_side_effects=True),
+        compiler_params=pltpu.CompilerParams(
+            collective_id=0, has_side_effects=True, vmem_limit_bytes=56 * MIB
+        ),
     )(queries, span_k, span_v, cache_k, cache_v)
 
 
-def attend_kernel(chosen, q, k_own, v_own, k_pair, v_pair, sk, sv, out, lse, k_both, v_wide, s_wide, acc, peak):
+def attend_kernel(
+    chosen, q, k_own, v_own, k_pair, v_pair, sk, sv, out, lse,
+    q_in, k_both, v_wide, sk_in, s_wide, out_in, acc, peak, sems, out_sem,
+):
     wide, narrow, y, core = place()
     held = wide % 2 * 4 + y
     first = wide % 2 * 8 + y * 2
-    k_both[0] = k_own[...]
-    k_both[1] = k_pair[...]
-    for i, v in enumerate((v_own, v_pair)):
-        v_wide[i, :, :HD] = v[...]
+    moves = [
+        (q, q_in),
+        (sk, sk_in),
+        (sv, s_wide.at[:, :HD]),
+        (k_own, k_both.at[0]),
+        (v_own, v_wide.at[0, :, :HD]),
+        (k_pair, k_both.at[1]),
+        (v_pair, v_wide.at[1, :, :HD]),
+    ]
+    loads = [pltpu.make_async_copy(src, dst, sems.at[i]) for i, (src, dst) in enumerate(moves)]
+    for copy in loads:
+        copy.start()
+    s_wide[:, HD:] = jnp.ones((QB, HD), jnp.bfloat16)
+    for i in range(2):
         v_wide[i, :, HD:] = jnp.ones((KB, HD), jnp.bfloat16)
-    s_wide[:, :HD] = sv[...]
-    s_wide[:, HD:] = jnp.ones((QB, HD), jnp.bfloat16)
 
     def fold(state, queries, keys, values, mask):
         top, total = state
@@ -193,34 +206,41 @@
         return new_top, total
 
     def load():
-        return peak[:, :1], acc[...]
+        return jnp.max(peak[...], axis=1, keepdims=True), acc[...]
 
     def save(state):
         peak[...] = jnp.broadcast_to(state[0], (ROWS, HD))
         acc[...] = state[1]
 
-    def one_block(b, carry):
+    for copy in loads[:3]:
+        copy.wait()
+    row = lax.broadcasted_iota(jnp.int32, (ROWS, QB), 0) % QB
+    mask = row >= lax.broadcasted_iota(jnp.int32, (ROWS, QB), 1)
+    fresh = jnp.full((ROWS, 1), FLOOR_SCORE, jnp.float32), jnp.zeros((ROWS, 2 * HD), jnp.float32)
+    save(fold(fresh, q_in[held], sk_in[...], s_wide[...], mask))
+    for copy in loads[3:]:
+        copy.wait()
+
+    def send_out(b):
+        return pltpu.make_async_copy(out_in.at[b], out.at[b], out_sem.at[b])
+
+    def one_block(step, carry):
+        b = (held + step) % NQB
         hits = []
         for i in range(2):
             c = first + jnp.where(core == 0, i, 1 - i)
             hits.append((chosen[b, 0] == c) | (chosen[b, 1] == c) | (chosen[b, 2] == c))
-        used = hits[0] | hits[1] | (b == held)
-
-        @pl.when(used)
+        used = hits[0] | hits[1] | (step == 0)
+
+        @pl.when(used & (step != 0))
         def _():
             acc[...] = jnp.zeros((ROWS, 2 * HD), jnp.float32)
             peak[...] = jnp.full((ROWS, HD), FLOOR_SCORE, jnp.float32)
-
-        @pl.when(b == held)
-        def _():
-            row = lax.broadcasted_iota(jnp.int32, (ROWS, QB), 0) % QB
-            mask = row >= lax.broadcasted_iota(jnp.int32, (ROWS, QB), 1)
-            save(fold(load(), q[b], sk[...], s_wide[...], mask))
 
         def cached(i, carry):
             @pl.when(jnp.where(i == 0, hits[0], hits[1]))
             def _():
-                queries = q[b]
+                queries = q_in[b]
                 state = load()
                 for start in range(0, KB, CHUNK):
                     state = fold(
@@ -235,7 +255,7 @@
         @pl.when(used)
         def _():
             total = acc[:, HD:]
-            out[b] = (acc[:, :HD] / total).astype(jnp.bfloat16)
+            out_in[b] = (acc[:, :HD] / total).astype(jnp.bfloat16)
             logs = peak[...] * SCALE2 + jnp.log2(total)
             eye = lax.broadcasted_iota(jnp.int32, (HD, HD), 0) == lax.broadcasted_iota(jnp.int32, (HD, HD), 1)
             for g in range(ROWS // HD):
@@ -245,30 +265,38 @@
 
         @pl.when(jnp.logical_not(used))
         def _():
-            out[b] = jnp.zeros((ROWS, HD), jnp.bfloat16)
+            out_in[b] = jnp.zeros((ROWS, HD), jnp.bfloat16)
             lse[b] = jnp.full((8, HD), FLOOR_SCORE, jnp.float32)
 
+        send_out(b).start()
         return carry
 
     lax.fori_loop(0, NQB, one_block, 0)
+    for b in range(NQB):
+        send_out(b).wait()
 
 
 def attend(chosen, q, k_own, v_own, k_pair, v_pair, sk, sv):
-    vmem = pl.BlockSpec(memory_space=pltpu.VMEM)
+    anywhere = pl.BlockSpec(memory_space=pl.ANY)
+    dma = pltpu.SemaphoreType.DMA
     return pl.pallas_call(
         attend_kernel,
         out_shape=[
             jax.ShapeDtypeStruct((NQB, ROWS, HD), jnp.bfloat16),
             jax.ShapeDtypeStruct((NQB, 8, HD), jnp.float32),
         ],
-        in_specs=[pl.BlockSpec(memory_space=pltpu.SMEM)] + [vmem] * 7,
-        out_specs=[vmem] * 2,
+        in_specs=[pl.BlockSpec(memory_space=pltpu.SMEM)] + [anywhere] * 7,
+        out_specs=[anywhere, pl.BlockSpec(memory_space=pltpu.VMEM)],
         scratch_shapes=[
+            pltpu.VMEM((NQB, ROWS, HD), jnp.bfloat16),
             pltpu.VMEM((2, KB, HD), jnp.bfloat16),
             pltpu.VMEM((2, KB, 2 * HD), jnp.bfloat16),
+            pltpu.VMEM((QB, HD), jnp.bfloat16),
             pltpu.VMEM((QB, 2 * HD), jnp.bfloat16),
+            pltpu.VMEM((NQB, ROWS, HD), jnp.bfloat16),
             pltpu.VMEM((ROWS, 2 * HD), jnp.float32),
             pltpu.VMEM((ROWS, HD), jnp.float32),
+            dma((7,)), dma((NQB,)),
         ],
         compiler_params=pltpu.CompilerParams(vmem_limit_bytes=56 * MIB),
         cost_estimate=pl.CostEstimate(flops=14 * 10**9, bytes_accessed=10 * MIB, transcendentals=25 * 10**6),
@@ -452,8 +480,9 @@
 
 
 def shards(queries, span_keys, span_values, cache_keys, cache_values, chosen, out_weight):
+    q, k_pair, v_pair, sk, sv = spread(queries, span_keys, span_values, cache_keys, cache_values)
+    out_weight, q = lax.optimization_barrier((out_weight, q))
     weight = lax.all_gather(out_weight, "wide", axis=0, tiled=True)
-    q, k_pair, v_pair, sk, sv = spread(queries, span_keys, span_values, cache_keys, cache_values)
     part, lse = attend(chosen, q, cache_keys, cache_values, k_pair, v_pair, sk, sv)
     return finish(part, lse, weight)
 

time: 229 us -> 191 us (0.83)
  the two profiles are of different devices: /device:TPU:26 before, /device:TPU:30 now
where the time goes in v2:
time: 191 us
  Pallas kernels  125 us (65%)
  waiting for transfers between devices  49.4 us (26%)
  between operations  13.4 us (7%)
  local copies, waits for them, and re-layouts  3.72 us (2%)
    pallas_call x1, Pallas kernels, finish(): pl.pallas_call(finish_kernel, out_shape=jax.ShapeDtypeStruct((HALF, 512),...  66.1 us
    all_gather x1, waiting for transfers between devices, shards(): weight = lax.all_gather(out_weight, 'wide', axis=0, tiled=True)  49.4 us
    pallas_call x1, Pallas kernels, spread(): pl.pallas_call(spread_kernel, out_shape=[shape(NQB, ROWS, HD), shape(KB,...  35.8 us
    pallas_call x1, Pallas kernels, attend(): pl.pallas_call(attend_kernel, out_shape=[jax.ShapeDtypeStruct((NQB, ROWS,...  22.6 us
  transfers between devices with their start and end apart: 1, of which 1 were waited for; matrix products, arithmetic and copies ran while one was open for 0% of the time, Pallas kernels for 12%

profile of v2, /device:TPU:30, one launch (start us, length us, event | category | flops | bytes accessed | tf_op | source)
XLA Modules:
  0.0 191.1 jit_solution(10501809455722736864)
XLA Ops:
  6.5 0.0 copy-start.2
  6.5 0.0 all-gather.2.cloned.1.call-start
  6.5 35.8 %shard_map.73 = (bf16[8,1024,128]{2,1,0:T(8,128)(2,1)}, bf16[4096,128]{1,0:T(8,128)(2,1)}, bf16[4096,128]{1,0:T(8,128)(2,1)}, bf16[512,128]{1,0:T(8,128)(2,1)}, bf16[512,128]{1,0:T(8,128)(2,1)}) custom-call(bf16[256,4096]{1,0:T(8,128)(2,1)} %queries.1, bf16[256,1024]{1,0:T(8,128)(2,1)} %span_k.1, bf16[256,1024]{1,0:T(8,128)(2,1)} %span_v.1, ...), custom_call_target="tpu_custom_call" | custom-call | tf_op jit(solution)/shard_map/pallas_call | solution.py:160
  42.4 0.0 all-gather.2.cloned.1.call-update
  42.4 0.0 copy-done.2
  42.4 0.7 copy.8.chosen
  43.1 22.6 %shard_map.74 = (bf16[8,1024,128]{2,1,0:T(8,128)(2,1)}, f32[8,8,128]{2,1,0:T(8,128)}) custom-call(s32[8,3]{1,0:T(8,128)} %copy.8.chosen, bf16[8,1024,128]{2,1,0:T(8,128)(2,1)} %get-tuple-element.15.q, bf16[4096,128]{1,0:T(8,128)(2,1)} %k_own.1, bf16[4096,128]{1,0:T(8,128)(2,1)} %v_own.1, bf16[4096,128]{1,0:T(8,128)(2,1)} %get-tuple-element.16.k_pair, ...), custom_call_target="tpu_custom_call" | custom-call | flops 14000000000 | bytes 10485760 | tf_op jit(solution)/shard_map/pallas_call | solution.py:282
  65.6 49.4 %all-gather.2.cloned.1.call-done.weight = bf16[4096,512]{1,0:T(8,128)(2,1)} async-done(((bf16[256,512]{1,0:T(8,128)(2,1)}), bf16[4096,512]{1,0:T(8,128)(2,1)}) %all-gather.2.cloned.1.call-update) | async-done | bytes 4194320 | tf_op jit(solution)/shard_map/all_gather | solution.py:485
  115.0 0.0 copy-start
  115.0 1.6 copy-done
  116.6 0.0 copy-start.1
  116.6 0.8 copy-done.1
  117.4 66.1 %shard_map.75 = bf16[256,512]{1,0:T(8,128)(2,1)S(1)} custom-call(bf16[8,1024,128]{2,1,0:T(8,128)(2,1)S(1)} %copy-done, f32[8,8,128]{2,1,0:T(8,128)S(1)} %copy-done.1, bf16[4096,512]{1,0:T(8,128)(2,1)} %all-gather.2.cloned.1.call-done.weight), custom_call_target="tpu_custom_call" | custom-call | tf_op jit(solution)/shard_map/pallas_call | solution.py:463
  183.5 0.7 copy.10
Async XLA Ops:
  6.5 35.8 %copy-start.2 = (s32[8,3]{0,1:T(4,128)S(1)}, s32[8,3]{0,1:T(4,128)}, u32[]{:S(2)}) copy-start(s32[8,3]{0,1:T(4,128)} %param.12) | copy-start | bytes 292
  6.5 108.5 %all-gather.2.cloned.1.call-start = ((), (), s32[]{:S(2)}) async-start(), calls=%async_computation | async-start | bytes 4456448 | tf_op jit(solution)/shard_map/all_gather | solution.py:485
  115.0 1.6 copy-start
  116.6 0.8 copy-start.1
Sparse Core Ops, SparseCore 0:
  42.5 72.4 all-gather.1

commit v3 on v2

--- a/solution.py
+++ b/solution.py
@@ -15,6 +15,8 @@
 KVH = 8
 HALF = 256
 ROWS = 2 * QB
+NY = 4
+PIECE = HALF // NY
 CHUNK = 256
 FLOOR_SCORE = -1e30
 SCALE2 = math.log2(math.e) / math.sqrt(HD)
@@ -37,7 +39,8 @@
 def spread_kernel(
     queries, span_k, span_v, cache_k, cache_v,
     q_out, pk_out, pv_out, sk_out, sv_out,
-    q_send, q_recv, kv_send, kv_recv, span_send, span_recv, local_sem, span_local,
+    q_send, q_recv, ring_send, ring_recv, pass_send, pass_recv,
+    kv_send, kv_recv, span_send, span_recv, local_sem, span_local,
 ):
     wide, narrow, y, core = place()
     buddy = y * 2 + 1 - core
@@ -51,15 +54,32 @@
         return carry
 
     lax.fori_loop(1, NW, greet, 0)
-    pl.semaphore_signal(barrier, inc=1, device_id=(wide, buddy), device_id_type=MESH)
-    pl.semaphore_wait(barrier, NW)
+    ring = [(y + 1) % NY * 2 + core, (y + NY - 1) % NY * 2 + core]
+    for neighbour in (buddy, *ring):
+        pl.semaphore_signal(barrier, inc=1, device_id=(wide, neighbour), device_id_type=MESH)
+    pl.semaphore_wait(barrier, NW + 2)
 
     def q_src(kv, head):
         column = pl.multiple_of(kv * 512 + core * 256 + head * HD, HD)
-        return queries.at[:, pl.ds(column, HD)]
+        return queries.at[pl.ds(pl.multiple_of(y * PIECE, PIECE), PIECE), pl.ds(column, HD)]
 
     def q_dst(source, head):
-        return q_out.at[source // 2, pl.ds(pl.multiple_of(head * QB + source % 2 * HALF, HALF), HALF), :]
+        return q_out.at[head, source, y]
+
+    def batch(group, head, piece):
+        return q_out.at[head, pl.ds(group * 4, 4), piece]
+
+    def ring_copy(group, head, direction, piece):
+        return remote(
+            batch(group, head, piece), batch(group, head, piece),
+            ring_send.at[group, head, direction], ring_recv.at[group, head, direction], (wide, ring[direction]),
+        )
+
+    def pass_copy(group, head, piece):
+        return remote(
+            batch(group, head, piece), batch(group, head, piece),
+            pass_send.at[group, head], pass_recv.at[group, head], (wide, ring[head]),
+        )
 
     def span_pair(kv, which):
         src = (span_k, span_v)[which].at[:, pl.ds(pl.multiple_of(kv * HD, HD), HD)]
@@ -121,14 +141,56 @@
 
     for head in range(2):
         pltpu.make_async_copy(q_src(wide // 2, head), q_dst(wide, head), local_sem.at[head]).wait()
+    behind = [(y + NY - 1) % NY, (y + 1) % NY]
+
+    def gather_batch(step, carry):
+        group = (wide // 4 + step) % 4
+
+        def wait_source(i, carry):
+            source = group * 4 + i
+
+            @pl.when(source != wide)
+            def _():
+                for head in range(2):
+                    remote(
+                        q_src(0, head), q_dst(source, head),
+                        q_send.at[0, head], q_recv.at[source, head], (source, narrow),
+                    ).wait_recv()
+
+            return carry
+
+        lax.fori_loop(0, 4, wait_source, 0)
+        for head in range(2):
+            for direction in range(2):
+                ring_copy(group, head, direction, y).start()
+        return carry
+
+    lax.fori_loop(0, 4, gather_batch, 0)
+
+    def pass_batch(step, carry):
+        group = (wide // 4 + step) % 4
+        for head in range(2):
+            ring_copy(group, head, head, behind[head]).wait_recv()
+            pass_copy(group, head, behind[head]).start()
+        return carry
+
+    lax.fori_loop(0, 4, pass_batch, 0)
+
+    def finish_batch(step, carry):
+        group = (wide // 4 + step) % 4
+        for head in range(2):
+            ring_copy(group, head, 1 - head, behind[1 - head]).wait_recv()
+            pass_copy(group, head, (y + 2) % NY).wait_recv()
+            pass_copy(group, head, behind[head]).wait_send()
+            for direction in range(2):
+                ring_copy(group, head, direction, y).wait_send()
+        return carry
+
+    lax.fori_loop(0, 4, finish_batch, 0)
 
     def wait_q(step, carry):
-        source = (wide + NW - step) % NW
         for head in range(2):
             q_copy(step, head).wait_send()
-            remote(
-                q_src(0, head), q_dst(source, head), q_send.at[step, head], q_recv.at[source, head], (source, narrow)
-            ).wait_recv()
         return carry
 
     lax.fori_loop(1, NW, wait_q, 0)
@@ -159,11 +221,12 @@
     dma = pltpu.SemaphoreType.DMA
     return pl.pallas_call(
         spread_kernel,
-        out_shape=[shape(NQB, ROWS, HD), shape(KB, HD), shape(KB, HD), shape(QB, HD), shape(QB, HD)],
+        out_shape=[shape(2, NW, NY, PIECE, HD), shape(KB, HD), shape(KB, HD), shape(QB, HD), shape(QB, HD)],
         in_specs=[anywhere] * 5,
         out_specs=[anywhere] * 5,
         scratch_shapes=[
-            dma((NW, 2)), dma((NW, 2)), dma((2,)), dma((2,)), dma((KVH, 2)), dma((2, 2)), dma((2,)), dma((2,)),
+            dma((NW, 2)), dma((NW, 2)), dma((4, 2, 2)), dma((4, 2, 2)), dma((4, 2)), dma((4, 2)),
+            dma((2,)), dma((2,)), dma((KVH, 2)), dma((2, 2)), dma((2,)), dma((2,)),
         ],
         compiler_params=pltpu.CompilerParams(
             collective_id=0, has_side_effects=True, vmem_limit_bytes=56 * MIB
@@ -205,6 +268,9 @@
         total = total * decay + jnp.dot(weights, values, preferred_element_type=jnp.float32)
         return new_top, total
 
+    def block_queries(b):
+        return q_in[:, pl.ds(b * 2, 2)].reshape(ROWS, HD)
+
     def load():
         return jnp.max(peak[...], axis=1, keepdims=True), acc[...]
 
@@ -217,7 +283,7 @@
     row = lax.broadcasted_iota(jnp.int32, (ROWS, QB), 0) % QB
     mask = row >= lax.broadcasted_iota(jnp.int32, (ROWS, QB), 1)
     fresh = jnp.full((ROWS, 1), FLOOR_SCORE, jnp.float32), jnp.zeros((ROWS, 2 * HD), jnp.float32)
-    save(fold(fresh, q_in[held], sk_in[...], s_wide[...], mask))
+    save(fold(fresh, block_queries(held), sk_in[...], s_wide[...], mask))
     for copy in loads[3:]:
         copy.wait()
 
@@ -240,7 +306,7 @@
         def cached(i, carry):
             @pl.when(jnp.where(i == 0, hits[0], hits[1]))
             def _():
-                queries = q_in[b]
+                queries = block_queries(b)
                 state = load()
                 for start in range(0, KB, CHUNK):
                     state = fold(
@@ -288,7 +354,7 @@
         in_specs=[pl.BlockSpec(memory_space=pltpu.SMEM)] + [anywhere] * 7,
         out_specs=[anywhere, pl.BlockSpec(memory_space=pltpu.VMEM)],
         scratch_shapes=[
-            pltpu.VMEM((NQB, ROWS, HD), jnp.bfloat16),
+            pltpu.VMEM((2, NW, NY, PIECE, HD), jnp.bfloat16),
             pltpu.VMEM((2, KB, HD), jnp.bfloat16),
             pltpu.VMEM((2, KB, 2 * HD), jnp.bfloat16),
             pltpu.VMEM((QB, HD), jnp.bfloat16),
@@ -480,9 +546,8 @@
 
 
 def shards(queries, span_keys, span_values, cache_keys, cache_values, chosen, out_weight):
+    weight = lax.all_gather(out_weight, "wide", axis=0, tiled=True)
     q, k_pair, v_pair, sk, sv = spread(queries, span_keys, span_values, cache_keys, cache_values)
-    out_weight, q = lax.optimization_barrier((out_weight, q))
-    weight = lax.all_gather(out_weight, "wide", axis=0, tiled=True)
     part, lse = attend(chosen, q, cache_keys, cache_values, k_pair, v_pair, sk, sv)
     return finish(part, lse, weight)
 

time: 191 us -> 153 us (0.80)
  the two profiles are of different devices: /device:TPU:30 before, /device:TPU:52 now
where the time goes in v3:
time: 153 us
  Pallas kernels  125 us (82%)
  between operations  13.4 us (9%)
  waiting for transfers between devices  9.9 us (6%)
  local copies, waits for them, and re-layouts  4.4 us (3%)
    pallas_call x1, Pallas kernels, finish(): pl.pallas_call(finish_kernel, out_shape=jax.ShapeDtypeStruct((HALF, 512),...  73.5 us
    pallas_call x1, Pallas kernels, spread(): pl.pallas_call(spread_kernel, out_shape=[shape(2, NW, NY, PIECE, HD), sha...  34.9 us
    pallas_call x1, Pallas kernels, attend(): pl.pallas_call(attend_kernel, out_shape=[jax.ShapeDtypeStruct((NQB, ROWS,...  16.9 us
    all_gather x1, waiting for transfers between devices, shards(): weight = lax.all_gather(out_weight, 'wide', axis=0, tiled=True)  9.19 us
    unnamed x6, local copies, waits for them, and re-layouts  4.4 us
  transfers between devices with their start and end apart: 1, of which 1 were waited for; matrix products, arithmetic and copies ran while one was open for 1% of the time, Pallas kernels for 34%

profile of v3, /device:TPU:52, one launch (start us, length us, event | category | flops | bytes accessed | tf_op | source)
XLA Modules:
  0.0 153.0 jit_solution(17879085498075037742)
XLA Ops:
  6.5 0.0 all-gather.2.cloned.1.call-start
  6.5 0.7 all-gather.2.cloned.1.call-update
  7.3 1.3 copy.8.chosen
  8.6 34.9 %shard_map.73 = (bf16[2,16,4,64,128]{4,3,2,1,0:T(8,128)(2,1)}, bf16[4096,128]{1,0:T(8,128)(2,1)}, bf16[4096,128]{1,0:T(8,128)(2,1)}, bf16[512,128]{1,0:T(8,128)(2,1)}, bf16[512,128]{1,0:T(8,128)(2,1)}) custom-call(bf16[256,4096]{1,0:T(8,128)(2,1)} %queries.1, bf16[256,1024]{1,0:T(8,128)(2,1)} %span_k.1, bf16[256,1024]{1,0:T(8,128)(2,1)} %span_v.1, ...), custom_call_target="tpu_custom_call" | custom-call | tf_op jit(solution)/shard_map/pallas_call | solution.py:222
  43.5 16.9 %shard_map.74 = (bf16[8,1024,128]{2,1,0:T(8,128)(2,1)}, f32[8,8,128]{2,1,0:T(8,128)}) custom-call(s32[8,3]{1,0:T(8,128)} %copy.8.chosen, bf16[2,16,4,64,128]{4,3,2,1,0:T(8,128)(2,1)} %get-tuple-element.12.q, bf16[4096,128]{1,0:T(8,128)(2,1)} %k_own.1, bf16[4096,128]{1,0:T(8,128)(2,1)} %v_own.1, bf16[4096,128]{1,0:T(8,128)(2,1)} %get-tuple-element.13.k_pair, ...), custom_call_target="tpu_custom_call" | custom-call | flops 14000000000 | bytes 10485760 | tf_op jit(solution)/shard_map/pallas_call | solution.py:348
  60.4 9.2 %all-gather.2.cloned.1.call-done.weight = bf16[4096,512]{1,0:T(8,128)(2,1)} async-done(((bf16[256,512]{1,0:T(8,128)(2,1)}), bf16[4096,512]{1,0:T(8,128)(2,1)}) %all-gather.2.cloned.1.call-update) | async-done | bytes 4194320 | tf_op jit(solution)/shard_map/all_gather | solution.py:549
  69.5 0.0 copy-start
  69.5 1.6 %copy-done = bf16[8,1024,128]{2,1,0:T(8,128)(2,1)S(1)} copy-done((bf16[8,1024,128]{2,1,0:T(8,128)(2,1)S(1)}, bf16[8,1024,128]{2,1,0:T(8,128)(2,1)}, u32[]{:S(2)}) %copy-start) | copy-done | bytes 2097176
  71.1 0.0 copy-start.1
  71.1 0.8 copy-done.1
  71.9 73.5 %shard_map.75 = bf16[256,512]{1,0:T(8,128)(2,1)S(1)} custom-call(bf16[8,1024,128]{2,1,0:T(8,128)(2,1)S(1)} %copy-done, f32[8,8,128]{2,1,0:T(8,128)S(1)} %copy-done.1, bf16[4096,512]{1,0:T(8,128)(2,1)} %all-gather.2.cloned.1.call-done.weight), custom_call_target="tpu_custom_call" | custom-call | tf_op jit(solution)/shard_map/pallas_call | solution.py:529
  145.5 0.7 copy.10
Async XLA Ops:
  6.5 63.0 %all-gather.2.cloned.1.call-start = ((), (), s32[]{:S(2)}) async-start(), calls=%async_computation | async-start | bytes 4456448 | tf_op jit(solution)/shard_map/all_gather | solution.py:549
  69.5 1.6 %copy-start = (bf16[8,1024,128]{2,1,0:T(8,128)(2,1)S(1)}, bf16[8,1024,128]{2,1,0:T(8,128)(2,1)}, u32[]{:S(2)}) copy-start(bf16[8,1024,128]{2,1,0:T(8,128)(2,1)} %get-tuple-element.17.part) | copy-start | bytes 6291460
  71.1 0.8 copy-start.1
Sparse Core Ops, SparseCore 0:
  9.5 60.0 all-gather.1

commit v4 on v3

--- a/solution.py
+++ b/solution.py
@@ -236,7 +236,7 @@
 
 def attend_kernel(
     chosen, q, k_own, v_own, k_pair, v_pair, sk, sv, out, lse,
-    q_in, k_both, v_wide, sk_in, s_wide, out_in, acc, peak, sems, out_sem,
+    q_in, k_both, v_wide, sk_in, s_wide, out_in, lse_in, acc, peak, sems, out_sem,
 ):
     wide, narrow, y, core = place()
     held = wide % 2 * 4 + y
@@ -288,7 +288,10 @@
         copy.wait()
 
     def send_out(b):
-        return pltpu.make_async_copy(out_in.at[b], out.at[b], out_sem.at[b])
+        return (
+            pltpu.make_async_copy(out_in.at[b], out.at[b], out_sem.at[b, 0]),
+            pltpu.make_async_copy(lse_in.at[b], lse.at[b], out_sem.at[b, 1]),
+        )
 
     def one_block(step, carry):
         b = (held + step) % NQB
@@ -325,21 +328,23 @@
             logs = peak[...] * SCALE2 + jnp.log2(total)
             eye = lax.broadcasted_iota(jnp.int32, (HD, HD), 0) == lax.broadcasted_iota(jnp.int32, (HD, HD), 1)
             for g in range(ROWS // HD):
-                lse[b, g:g + 1, :] = jnp.sum(
+                lse_in[b, g:g + 1, :] = jnp.sum(
                     jnp.where(eye, logs[g * HD:(g + 1) * HD], 0.0), axis=0, keepdims=True
                 )
 
         @pl.when(jnp.logical_not(used))
         def _():
             out_in[b] = jnp.zeros((ROWS, HD), jnp.bfloat16)
-            lse[b] = jnp.full((8, HD), FLOOR_SCORE, jnp.float32)
-
-        send_out(b).start()
+            lse_in[b] = jnp.full((8, HD), FLOOR_SCORE, jnp.float32)
+
+        for copy in send_out(b):
+            copy.start()
         return carry
 
     lax.fori_loop(0, NQB, one_block, 0)
     for b in range(NQB):
-        send_out(b).wait()
+        for copy in send_out(b):
+            copy.wait()
 
 
 def attend(chosen, q, k_own, v_own, k_pair, v_pair, sk, sv):
@@ -352,7 +357,7 @@
             jax.ShapeDtypeStruct((NQB, 8, HD), jnp.float32),
         ],
         in_specs=[pl.BlockSpec(memory_space=pltpu.SMEM)] + [anywhere] * 7,
-        out_specs=[anywhere, pl.BlockSpec(memory_space=pltpu.VMEM)],
+        out_specs=[anywhere] * 2,
         scratch_shapes=[
             pltpu.VMEM((2, NW, NY, PIECE, HD), jnp.bfloat16),
             pltpu.VMEM((2, KB, HD), jnp.bfloat16),
@@ -360,9 +365,10 @@
             pltpu.VMEM((QB, HD), jnp.bfloat16),
             pltpu.VMEM((QB, 2 * HD), jnp.bfloat16),
             pltpu.VMEM((NQB, ROWS, HD), jnp.bfloat16),
+            pltpu.VMEM((NQB, 8, HD), jnp.float32),
             pltpu.VMEM((ROWS, 2 * HD), jnp.float32),
             pltpu.VMEM((ROWS, HD), jnp.float32),
-            dma((7,)), dma((NQB,)),
+            dma((7,)), dma((NQB, 2)),
         ],
         compiler_params=pltpu.CompilerParams(vmem_limit_bytes=56 * MIB),
         cost_estimate=pl.CostEstimate(flops=14 * 10**9, bytes_accessed=10 * MIB, transcendentals=25 * 10**6),
@@ -371,14 +377,18 @@
 
 def finish_kernel(
     part, lse, weight, result,
-    p_in, l_in, w_in, rows_out, rows_in,
-    p_send, p_recv, l_send, l_recv, a_send, a_recv, f_send, f_recv, local_sem,
+    p_in, l_in, w_in, relay, rows_out, rows_in,
+    p_send, p_recv, l_send, l_recv, relay_send, relay_recv, pass_send,
+    a_send, a_recv, y_send, f_send, f_recv, local_sem,
 ):
     wide, narrow, y, core = place()
     buddy = y * 2 + 1 - core
-    kv = wide // 2
-    held = wide % 2 * 4 + y
+    kv, side = wide // 2, wide % 2
+    held = side * 4 + y
     mine = wide // 2
+    from_y = (y + NY - mine % 4) % NY
+    ahead, behind = (y + 1) % NY, (y + NY - 1) % NY
+    own_target = mine == held
     barrier = pltpu.get_barrier_semaphore()
 
     def combiner(b):
@@ -387,17 +397,12 @@
     def source(s):
         return s * 2 + mine // 4, mine % 4 * 2 + core
 
-    def target(t):
-        return held * 2 + t // 4, t % 4 * 2 + core
-
-    own_target = wide // 2 == held
     fetch = pltpu.make_async_copy(weight, w_in, local_sem.at[0])
-    fetch.start()
     keep = [
         pltpu.make_async_copy(part.at[held], p_in.at[held], local_sem.at[1]),
         pltpu.make_async_copy(lse.at[held], l_in.at[held], local_sem.at[2]),
     ]
-    for copy in keep:
+    for copy in (*keep, fetch):
         copy.start()
 
     def greet(step, carry):
@@ -407,7 +412,7 @@
     lax.fori_loop(1, 8, greet, 0)
 
     def greet_source(s, carry):
-        @pl.when(jnp.logical_not(own_target & (s == kv)))
+        @pl.when((from_y != 2) & jnp.logical_not(own_target & (s == kv)))
         def _():
             pl.semaphore_signal(barrier, inc=1, device_id=source(s), device_id_type=MESH)
 
@@ -415,112 +420,198 @@
 
     lax.fori_loop(0, 8, greet_source, 0)
     pl.semaphore_signal(barrier, inc=1, device_id=(wide, buddy), device_id_type=MESH)
-    pl.semaphore_wait(barrier, 16 - own_target.astype(jnp.int32))
-
-    def part_copies(step):
+    pl.semaphore_wait(barrier, 14 - own_target.astype(jnp.int32))
+
+    def head_rows(h):
+        return pl.ds(h * QB, QB)
+
+    def relay_copy(across):
+        b = (side + across) % 2 * 4 + (y + 2) % NY
+        return remote(
+            part.at[b, head_rows(1)], relay.at[across],
+            relay_send.at[across], relay_recv.at[across], (wide, behind * 2 + core),
+        )
+
+    def pass_copy(across):
+        origin = side * 4 + ahead
+        return remote(
+            relay.at[across], p_in.at[origin, head_rows(1)],
+            pass_send.at[across], p_recv.at[origin, 1], (kv * 2 + (side + across) % 2, behind * 2 + core),
+        )
+
+    def part_copy(step, h):
         b = (held + step) % 8
-        return [
-            remote(part.at[b], p_in.at[held], p_send.at[step], p_recv.at[held], combiner(b)),
-            remote(lse.at[b], l_in.at[held], l_send.at[step], l_recv.at[held], combiner(b)),
-        ]
-
-    def start_part(step, carry):
-        for copy in part_copies(step):
-            copy.start()
-        return carry
-
-    lax.fori_loop(1, 8, start_part, 0)
+        return remote(
+            part.at[b, head_rows(h)], p_in.at[held, head_rows(h)],
+            p_send.at[step, h], p_recv.at[held, h], combiner(b),
+        )
+
+    def lse_copy(step):
+        b = (held + step) % 8
+        return remote(lse.at[b], l_in.at[held], l_send.at[step], l_recv.at[held], combiner(b))
+
+    def straight(step):
+        return (held + step) % 4 != (y + 2) % 4
+
+    for across in range(2):
+        relay_copy(across).start()
+
+    def start_first(step, carry):
+        lse_copy(step).start()
+        part_copy(step, 0).start()
+        return carry
+
+    lax.fori_loop(1, 8, start_first, 0)
+
+    def start_second(step, carry):
+        @pl.when(straight(step))
+        def _():
+            part_copy(step, 1).start()
+
+        return carry
+
+    lax.fori_loop(1, 8, start_second, 0)
+    for across in range(2):
+        relay_copy(across).wait_recv()
+        pass_copy(across).start()
     for copy in keep:
         copy.wait()
 
-    def wait_part(step, carry):
-        for copy in part_copies(step):
-            copy.wait_send()
+    def wait_lse(step, carry):
         s = (held + step) % 8
-        remote(part.at[s], p_in.at[s], p_send.at[step], p_recv.at[s], combiner(s)).wait_recv()
         remote(lse.at[s], l_in.at[s], l_send.at[step], l_recv.at[s], combiner(s)).wait_recv()
         return carry
 
-    lax.fori_loop(1, 8, wait_part, 0)
-
+    lax.fori_loop(1, 8, wait_lse, 0)
     logs = l_in[...]
     shares = jnp.exp2(logs - jnp.max(logs, axis=0, keepdims=True))
     shares = shares / jnp.sum(shares, axis=0, keepdims=True)
     turned = jnp.transpose(jnp.concatenate([shares.reshape(64, HD)] * 2, axis=0))
-    for g in range(8):
-        total = jnp.zeros((HD, HD), jnp.float32)
-        for s in range(8):
-            rows = p_in[s, g * HD:(g + 1) * HD, :].astype(jnp.float32)
-            total = total + rows * turned[:, s * 8 + g:s * 8 + g + 1]
-        rows_out[g % 4 * HD:(g % 4 + 1) * HD, g // 4 * HD:(g // 4 + 1) * HD] = total.astype(jnp.bfloat16)
-
-    slot = kv * 2 + core
-
-    def out_part(t):
-        return rows_out.at[pl.ds(pl.multiple_of(t // 4 * HALF, HALF), HALF), :]
-
-    def row_copy(t):
-        return remote(out_part(t), rows_in.at[slot], a_send.at[t], a_recv.at[slot], target(t))
-
-    own_number = wide % 2 * 4 + y
-
-    def start_row(t, carry):
-        away = jnp.logical_not(own_target & (t == own_number))
-
-        @pl.when(away)
-        def _():
-            row_copy(t).start()
-
-        @pl.when(jnp.logical_not(away))
-        def _():
-            copy = pltpu.make_async_copy(out_part(t), rows_in.at[slot], local_sem.at[3])
-            copy.start()
-            copy.wait()
-
-        return carry
-
-    lax.fori_loop(0, 8, start_row, 0)
-
-    def forward(s):
-        n = s * 2 + core
-        return remote(rows_in.at[n], rows_in.at[n], f_send.at[s], f_recv.at[n], (wide, buddy))
+
+    def row_copy(i, delta, h):
+        head = kv * 4 + core * 2 + h
+        return remote(
+            rows_out.at[h, pl.ds(i * HALF, HALF)], rows_in.at[head],
+            a_send.at[i, delta, h], a_recv.at[head], (held * 2 + i, (y + delta) % NY * 2 + core),
+        )
+
+    def own_copy(i, h):
+        return pltpu.make_async_copy(
+            rows_out.at[h, pl.ds(i * HALF, HALF)], rows_in.at[kv * 4 + core * 2 + h], local_sem.at[3 + h]
+        )
+
+    def each_target(h, act, act_own):
+        for i in range(2):
+            for delta in (0, 1, 3):
+                if delta:
+                    act(row_copy(i, delta, h))
+                else:
+                    here = own_target & (side == i)
+
+                    @pl.when(here)
+                    def _():
+                        act_own(own_copy(i, h))
+
+                    @pl.when(jnp.logical_not(here))
+                    def _():
+                        act(row_copy(i, 0, h))
+
+    for h in range(2):
+        def wait_part(step, carry):
+            s = (held + step) % 8
+            remote(
+                part.at[s, head_rows(h)], p_in.at[s, head_rows(h)], p_send.at[step, h], p_recv.at[s, h], combiner(s)
+            ).wait_recv()
+            return carry
+
+        lax.fori_loop(1, 8, wait_part, 0)
+        for g in range(4):
+            total = jnp.zeros((HD, HD), jnp.float32)
+            for s in range(8):
+                column = s * 8 + h * 4 + g
+                rows = p_in[s, h * QB + g * HD:h * QB + (g + 1) * HD, :].astype(jnp.float32)
+                total = total + rows * turned[:, column:column + 1]
+            rows_out[h, g * HD:(g + 1) * HD, :] = total.astype(jnp.bfloat16)
+        each_target(h, lambda copy: copy.start(), lambda copy: copy.start())
 
     fetch.wait()
-
-    def product(n):
+    duty = ((from_y == 1) & (side == 0)) | ((from_y == 3) & (side == 1))
+    onward = jnp.where(side == 0, ahead, behind) * 2 + core
+
+    def product(head):
         return jnp.dot(
-            rows_in[n], w_in[pl.ds(pl.multiple_of(n * HALF, HALF), HALF), :], preferred_element_type=jnp.float32
-        )
-
-    def arrive(s, total):
-        n = s * 2 + core
-
-        @pl.when(jnp.logical_not(own_target & (s == kv)))
-        def _():
-            remote(rows_in.at[n], rows_in.at[n], f_send.at[s], a_recv.at[n], (wide, buddy)).wait_recv()
-
-        forward(s).start()
-        return total + product(n)
-
-    total = lax.fori_loop(0, 8, arrive, jnp.zeros((HALF, 512), jnp.float32))
-
-    def arrive_pair(s, total):
-        n = s * 2 + 1 - core
-        remote(rows_in.at[n], rows_in.at[n], f_send.at[s], f_recv.at[n], (wide, buddy)).wait_recv()
-        return total + product(n)
-
-    total = lax.fori_loop(0, 8, arrive_pair, total)
+            rows_in[head], w_in[pl.ds(pl.multiple_of(head * HD, HD), HD), :], preferred_element_type=jnp.float32
+        )
+
+    def forward(s, h):
+        head = s * 4 + core * 2 + h
+        return remote(rows_in.at[head], rows_in.at[head], f_send.at[s, h], f_recv.at[head], (wide, buddy))
+
+    def along(s, h):
+        head = s * 4 + core * 2 + h
+        return remote(rows_in.at[head], rows_in.at[head], y_send.at[s, h], a_recv.at[head], (wide, onward))
+
+    total = jnp.zeros((HALF, 512), jnp.float32)
+    for h in range(2):
+        def arrive(s, total):
+            head = s * 4 + core * 2 + h
+            local = own_target & (s == kv)
+
+            @pl.when(local)
+            def _():
+                own_copy(0, h).wait()
+
+            @pl.when(jnp.logical_not(local))
+            def _():
+                remote(
+                    rows_in.at[head], rows_in.at[head], f_send.at[s, h], a_recv.at[head], (wide, buddy)
+                ).wait_recv()
+
+            forward(s, h).start()
+
+            @pl.when(duty)
+            def _():
+                along(s, h).start()
+
+            return total + product(head)
+
+        total = lax.fori_loop(0, 8, arrive, total)
+
+        def arrive_pair(s, total):
+            head = s * 4 + (1 - core) * 2 + h
+            remote(rows_in.at[head], rows_in.at[head], f_send.at[s, h], f_recv.at[head], (wide, buddy)).wait_recv()
+            return total + product(head)
+
+        total = lax.fori_loop(0, 8, arrive_pair, total)
     result[...] = total.astype(jnp.bfloat16)
 
-    def drain(t, carry):
-        @pl.when(jnp.logical_not(own_target & (t == own_number)))
-        def _():
-            row_copy(t).wait_send()
-
-        forward(t).wait_send()
-        return carry
-
-    lax.fori_loop(0, 8, drain, 0)
+    def drain(step, carry):
+        lse_copy(step).wait_send()
+        part_copy(step, 0).wait_send()
+
+        @pl.when(straight(step))
+        def _():
+            part_copy(step, 1).wait_send()
+
+        return carry
+
+    lax.fori_loop(1, 8, drain, 0)
+    for across in range(2):
+        relay_copy(across).wait_send()
+        pass_copy(across).wait_send()
+    for h in range(2):
+        each_target(h, lambda copy: copy.wait_send(), lambda copy: None)
+
+        def drain_rows(s, carry):
+            forward(s, h).wait_send()
+
+            @pl.when(duty)
+            def _():
+                along(s, h).wait_send()
+
+            return carry
+
+        lax.fori_loop(0, 8, drain_rows, 0)
 
 
 def finish(part, lse, weight):
@@ -535,12 +626,14 @@
             pltpu.VMEM((8, ROWS, HD), jnp.bfloat16),
             pltpu.VMEM((8, 8, HD), jnp.float32),
             pltpu.VMEM((4096, 512), jnp.bfloat16),
-            pltpu.VMEM((QB, 256), jnp.bfloat16),
-            pltpu.VMEM((16, HALF, 256), jnp.bfloat16),
-            dma((8,)), dma((8,)), dma((8,)), dma((8,)), dma((8,)), dma((16,)), dma((8,)), dma((16,)), dma((4,)),
+            pltpu.VMEM((2, QB, HD), jnp.bfloat16),
+            pltpu.VMEM((2, QB, HD), jnp.bfloat16),
+            pltpu.VMEM((32, HALF, HD), jnp.bfloat16),
+            dma((8, 2)), dma((8, 2)), dma((8,)), dma((8,)), dma((2,)), dma((2,)), dma((2,)),
+            dma((2, 4, 2)), dma((32,)), dma((8, 2)), dma((8, 2)), dma((32,)), dma((5,)),
         ],
         compiler_params=pltpu.CompilerParams(
-            collective_id=1, has_side_effects=True, vmem_limit_bytes=48 * MIB
+            collective_id=1, has_side_effects=True, vmem_limit_bytes=56 * MIB
         ),
     )(part, lse, weight)
 

time: 153 us -> 160 us (1.046)
  the two profiles are of different devices: /device:TPU:52 before, /device:TPU:82 now
where the time goes in v4:
time: 160 us; the launch traced here: 159 us
  Pallas kernels  134 us (84%)
  between operations  13.4 us (8%)
  waiting for transfers between devices  9.11 us (6%)
  local copies, waits for them, and re-layouts  3.01 us (2%)
    pallas_call x1, Pallas kernels, finish(): pl.pallas_call(finish_kernel, out_shape=jax.ShapeDtypeStruct((HALF, 512),...  81.8 us
    pallas_call x1, Pallas kernels, spread(): pl.pallas_call(spread_kernel, out_shape=[shape(2, NW, NY, PIECE, HD), sha...  30 us
    pallas_call x1, Pallas kernels, attend(): pl.pallas_call(attend_kernel, out_shape=[jax.ShapeDtypeStruct((NQB, ROWS,...  22.1 us
    all_gather x1, waiting for transfers between devices, shards(): weight = lax.all_gather(out_weight, 'wide', axis=0, tiled=True)  8.4 us
  transfers between devices with their start and end apart: 1, of which 1 were waited for; matrix products, arithmetic and copies ran while one was open for 1% of the time, Pallas kernels for 33%

profile of v4, /device:TPU:82, one launch (start us, length us, event | category | flops | bytes accessed | tf_op | source)
XLA Modules:
  0.0 159.4 jit_solution(1643806914216302077)
XLA Ops:
  6.5 0.0 all-gather.2.cloned.1.call-start
  6.5 0.7 all-gather.2.cloned.1.call-update
  7.3 1.3 copy.8.chosen
  8.6 30.0 %shard_map.73 = (bf16[2,16,4,64,128]{4,3,2,1,0:T(8,128)(2,1)}, bf16[4096,128]{1,0:T(8,128)(2,1)}, bf16[4096,128]{1,0:T(8,128)(2,1)}, bf16[512,128]{1,0:T(8,128)(2,1)}, bf16[512,128]{1,0:T(8,128)(2,1)}) custom-call(bf16[256,4096]{1,0:T(8,128)(2,1)} %queries.1, bf16[256,1024]{1,0:T(8,128)(2,1)} %span_k.1, bf16[256,1024]{1,0:T(8,128)(2,1)} %span_v.1, ...), custom_call_target="tpu_custom_call" | custom-call | tf_op jit(solution)/shard_map/pallas_call | solution.py:222
  38.6 22.1 %shard_map.74 = (bf16[8,1024,128]{2,1,0:T(8,128)(2,1)}, f32[8,8,128]{2,1,0:T(8,128)}) custom-call(s32[8,3]{1,0:T(8,128)} %copy.8.chosen, bf16[2,16,4,64,128]{4,3,2,1,0:T(8,128)(2,1)} %get-tuple-element.12.q, bf16[4096,128]{1,0:T(8,128)(2,1)} %k_own.1, bf16[4096,128]{1,0:T(8,128)(2,1)} %v_own.1, bf16[4096,128]{1,0:T(8,128)(2,1)} %get-tuple-element.13.k_pair, ...), custom_call_target="tpu_custom_call" | custom-call | flops 14000000000 | bytes 10485760 | tf_op jit(solution)/shard_map/pallas_call | solution.py:353
  60.7 8.4 %all-gather.2.cloned.1.call-done.weight = bf16[4096,512]{1,0:T(8,128)(2,1)} async-done(((bf16[256,512]{1,0:T(8,128)(2,1)}), bf16[4096,512]{1,0:T(8,128)(2,1)}) %all-gather.2.cloned.1.call-update) | async-done | bytes 4194320 | tf_op jit(solution)/shard_map/all_gather | solution.py:642
  69.1 81.8 %shard_map.75 = bf16[256,512]{1,0:T(8,128)(2,1)} custom-call(bf16[8,1024,128]{2,1,0:T(8,128)(2,1)} %get-tuple-element.17.part, f32[8,8,128]{2,1,0:T(8,128)} %get-tuple-element.18.lse, bf16[4096,512]{1,0:T(8,128)(2,1)} %all-gather.2.cloned.1.call-done.weight), custom_call_target="tpu_custom_call" | custom-call | tf_op jit(solution)/shard_map/pallas_call | solution.py:620
  150.9 1.7 %copy.10 = bf16[256,512]{1,0:T(8,128)(2,1)} copy(bf16[256,512]{1,0:T(8,128)(2,1)} %shard_map.75) | data formatting | bytes 524288
Async XLA Ops:
  6.5 62.6 %all-gather.2.cloned.1.call-start = ((), (), s32[]{:S(2)}) async-start(), calls=%async_computation | async-start | bytes 4456448 | tf_op jit(solution)/shard_map/all_gather | solution.py:642
Sparse Core Ops, SparseCore 0:
  9.5 59.5 all-gather.1

commit v5 on v4

--- a/solution.py
+++ b/solution.py
@@ -254,6 +254,7 @@
     for copy in loads:
         copy.start()
     s_wide[:, HD:] = jnp.ones((QB, HD), jnp.bfloat16)
+    lse_in[...] = jnp.full((NY, 2, 16, HD), FLOOR_SCORE, jnp.float32)
     for i in range(2):
         v_wide[i, :, HD:] = jnp.ones((KB, HD), jnp.bfloat16)
 
@@ -288,9 +289,8 @@
         copy.wait()
 
     def send_out(b):
-        return (
-            pltpu.make_async_copy(out_in.at[b], out.at[b], out_sem.at[b, 0]),
-            pltpu.make_async_copy(lse_in.at[b], lse.at[b], out_sem.at[b, 1]),
+        return pltpu.make_async_copy(
+            out_in.at[:, pl.ds(b * 2, 2)], out.at[:, pl.ds(b * 2, 2)], out_sem.at[b]
         )
 
     def one_block(step, carry):
@@ -324,27 +324,33 @@
         @pl.when(used)
         def _():
             total = acc[:, HD:]
-            out_in[b] = (acc[:, :HD] / total).astype(jnp.bfloat16)
+            out_in[:, pl.ds(b * 2, 2)] = (
+                (acc[:, :HD] / total).astype(jnp.bfloat16).reshape(2, 2, NY, PIECE, HD)
+            )
             logs = peak[...] * SCALE2 + jnp.log2(total)
-            eye = lax.broadcasted_iota(jnp.int32, (HD, HD), 0) == lax.broadcasted_iota(jnp.int32, (HD, HD), 1)
-            for g in range(ROWS // HD):
-                lse_in[b, g:g + 1, :] = jnp.sum(
-                    jnp.where(eye, logs[g * HD:(g + 1) * HD], 0.0), axis=0, keepdims=True
-                )
+            eye = lax.broadcasted_iota(jnp.int32, (PIECE, HD), 0) == lax.broadcasted_iota(
+                jnp.int32, (PIECE, HD), 1
+            )
+            for piece in range(NY):
+                for part in range(4):
+                    start = part * HALF + piece * PIECE
+                    lse_in[piece, b // 4, pl.ds(b % 4 * 4 + part, 1), :] = jnp.sum(
+                        jnp.where(eye, logs[start:start + PIECE], 0.0), axis=0, keepdims=True
+                    )
 
         @pl.when(jnp.logical_not(used))
         def _():
-            out_in[b] = jnp.zeros((ROWS, HD), jnp.bfloat16)
-            lse_in[b] = jnp.full((8, HD), FLOOR_SCORE, jnp.float32)
-
-        for copy in send_out(b):
-            copy.start()
+            out_in[:, pl.ds(b * 2, 2)] = jnp.zeros((2, 2, NY, PIECE, HD), jnp.bfloat16)
+
+        send_out(b).start()
         return carry
 
     lax.fori_loop(0, NQB, one_block, 0)
+    lse_copy = pltpu.make_async_copy(lse_in, lse, sems.at[7])
+    lse_copy.start()
     for b in range(NQB):
-        for copy in send_out(b):
-            copy.wait()
+        send_out(b).wait()
+    lse_copy.wait()
 
 
 def attend(chosen, q, k_own, v_own, k_pair, v_pair, sk, sv):
@@ -353,8 +359,8 @@
     return pl.pallas_call(
         attend_kernel,
         out_shape=[
-            jax.ShapeDtypeStruct((NQB, ROWS, HD), jnp.bfloat16),
-            jax.ShapeDtypeStruct((NQB, 8, HD), jnp.float32),
+            jax.ShapeDtypeStruct((2, NW, NY, PIECE, HD), jnp.bfloat16),
+            jax.ShapeDtypeStruct((NY, 2, 16, HD), jnp.float32),
         ],
         in_specs=[pl.BlockSpec(memory_space=pltpu.SMEM)] + [anywhere] * 7,
         out_specs=[anywhere] * 2,
@@ -364,11 +370,11 @@
             pltpu.VMEM((2, KB, 2 * HD), jnp.bfloat16),
             pltpu.VMEM((QB, HD), jnp.bfloat16),
             pltpu.VMEM((QB, 2 * HD), jnp.bfloat16),
-            pltpu.VMEM((NQB, ROWS, HD), jnp.bfloat16),
-            pltpu.VMEM((NQB, 8, HD), jnp.float32),
+            pltpu.VMEM((2, NW, NY, PIECE, HD), jnp.bfloat16),
+            pltpu.VMEM((NY, 2, 16, HD), jnp.float32),
             pltpu.VMEM((ROWS, 2 * HD), jnp.float32),
             pltpu.VMEM((ROWS, HD), jnp.float32),
-            dma((7,)), dma((NQB, 2)),
+            dma((8,)), dma((NQB,)),
         ],
         compiler_params=pltpu.CompilerParams(vmem_limit_bytes=56 * MIB),
         cost_estimate=pl.CostEstimate(flops=14 * 10**9, bytes_accessed=10 * MIB, transcendentals=25 * 10**6),
@@ -379,30 +385,27 @@
     part, lse, weight, result,
     p_in, l_in, w_in, relay, rows_out, rows_in,
     p_send, p_recv, l_send, l_recv, relay_send, relay_recv, pass_send,
-    a_send, a_recv, y_send, f_send, f_recv, local_sem,
+    a_send, a_recv, ring_send, ring_recv, on_send, on_recv, f_send, f_recv, local_sem,
 ):
     wide, narrow, y, core = place()
     buddy = y * 2 + 1 - core
     kv, side = wide // 2, wide % 2
     held = side * 4 + y
-    mine = wide // 2
-    from_y = (y + NY - mine % 4) % NY
-    ahead, behind = (y + 1) % NY, (y + NY - 1) % NY
-    own_target = mine == held
+    ring = [(y + 1) % NY, (y + NY - 1) % NY]
+    behind = ring[::-1]
+    own_target = wide // 8 == side
     barrier = pltpu.get_barrier_semaphore()
 
     def combiner(b):
         return kv * 2 + b // 4, b % 4 * 2 + core
 
-    def source(s):
-        return s * 2 + mine // 4, mine % 4 * 2 + core
-
-    fetch = pltpu.make_async_copy(weight, w_in, local_sem.at[0])
+    fetches = [pltpu.make_async_copy(weight.at[:, i], w_in.at[i], local_sem.at[i]) for i in range(4)]
     keep = [
-        pltpu.make_async_copy(part.at[held], p_in.at[held], local_sem.at[1]),
-        pltpu.make_async_copy(lse.at[held], l_in.at[held], local_sem.at[2]),
+        pltpu.make_async_copy(part.at[h, pl.ds(side * 8, 8), y], p_in.at[held, h], local_sem.at[4 + h])
+        for h in range(2)
     ]
-    for copy in (*keep, fetch):
+    keep.append(pltpu.make_async_copy(lse.at[y, side], l_in.at[held], local_sem.at[6]))
+    for copy in (*keep, *fetches):
         copy.start()
 
     def greet(step, carry):
@@ -412,43 +415,40 @@
     lax.fori_loop(1, 8, greet, 0)
 
     def greet_source(s, carry):
-        @pl.when((from_y != 2) & jnp.logical_not(own_target & (s == kv)))
-        def _():
-            pl.semaphore_signal(barrier, inc=1, device_id=source(s), device_id_type=MESH)
+        @pl.when(jnp.logical_not(own_target & (s == kv)))
+        def _():
+            pl.semaphore_signal(barrier, inc=1, device_id=(s * 2 + wide // 8, narrow), device_id_type=MESH)
 
         return carry
 
     lax.fori_loop(0, 8, greet_source, 0)
     pl.semaphore_signal(barrier, inc=1, device_id=(wide, buddy), device_id_type=MESH)
-    pl.semaphore_wait(barrier, 14 - own_target.astype(jnp.int32))
-
-    def head_rows(h):
-        return pl.ds(h * QB, QB)
+    pl.semaphore_wait(barrier, 16 - own_target.astype(jnp.int32))
+
+    def share(b, h):
+        return part.at[h, pl.ds(b // 4 * 8, 8), b % 4]
 
     def relay_copy(across):
         b = (side + across) % 2 * 4 + (y + 2) % NY
         return remote(
-            part.at[b, head_rows(1)], relay.at[across],
-            relay_send.at[across], relay_recv.at[across], (wide, behind * 2 + core),
+            share(b, 1), relay.at[across],
+            relay_send.at[across], relay_recv.at[across], (wide, ring[1] * 2 + core),
         )
 
     def pass_copy(across):
-        origin = side * 4 + ahead
-        return remote(
-            relay.at[across], p_in.at[origin, head_rows(1)],
-            pass_send.at[across], p_recv.at[origin, 1], (kv * 2 + (side + across) % 2, behind * 2 + core),
+        origin = side * 4 + ring[0]
+        return remote(
+            relay.at[across], p_in.at[origin, 1],
+            pass_send.at[across], p_recv.at[origin, 1], (kv * 2 + (side + across) % 2, ring[1] * 2 + core),
         )
 
     def part_copy(step, h):
         b = (held + step) % 8
-        return remote(
-            part.at[b, head_rows(h)], p_in.at[held, head_rows(h)],
-            p_send.at[step, h], p_recv.at[held, h], combiner(b),
-        )
+        return remote(share(b, h), p_in.at[held, h], p_send.at[step, h], p_recv.at[held, h], combiner(b))
 
     def lse_copy(step):
         b = (held + step) % 8
-        return remote(lse.at[b], l_in.at[held], l_send.at[step], l_recv.at[held], combiner(b))
+        return remote(lse.at[b % 4, b // 4], l_in.at[held], l_send.at[step], l_recv.at[held], combiner(b))
 
     def straight(step):
         return (held + step) % 4 != (y + 2) % 4
@@ -479,110 +479,119 @@
 
     def wait_lse(step, carry):
         s = (held + step) % 8
-        remote(lse.at[s], l_in.at[s], l_send.at[step], l_recv.at[s], combiner(s)).wait_recv()
+        remote(lse.at[0, 0], l_in.at[s], l_send.at[step], l_recv.at[s], combiner(s)).wait_recv()
         return carry
 
     lax.fori_loop(1, 8, wait_lse, 0)
     logs = l_in[...]
     shares = jnp.exp2(logs - jnp.max(logs, axis=0, keepdims=True))
     shares = shares / jnp.sum(shares, axis=0, keepdims=True)
-    turned = jnp.transpose(jnp.concatenate([shares.reshape(64, HD)] * 2, axis=0))
-
-    def row_copy(i, delta, h):
-        head = kv * 4 + core * 2 + h
-        return remote(
-            rows_out.at[h, pl.ds(i * HALF, HALF)], rows_in.at[head],
-            a_send.at[i, delta, h], a_recv.at[head], (held * 2 + i, (y + delta) % NY * 2 + core),
-        )
-
-    def own_copy(i, h):
-        return pltpu.make_async_copy(
-            rows_out.at[h, pl.ds(i * HALF, HALF)], rows_in.at[kv * 4 + core * 2 + h], local_sem.at[3 + h]
-        )
-
-    def each_target(h, act, act_own):
-        for i in range(2):
-            for delta in (0, 1, 3):
-                if delta:
-                    act(row_copy(i, delta, h))
-                else:
-                    here = own_target & (side == i)
-
-                    @pl.when(here)
-                    def _():
-                        act_own(own_copy(i, h))
-
-                    @pl.when(jnp.logical_not(here))
-                    def _():
-                        act(row_copy(i, 0, h))
+    turned = jnp.transpose(shares.reshape(HD, HD))
+
+    def row_copy(i, h):
+        return remote(
+            rows_out.at[h, i], rows_in.at[core, h, y, kv], a_send.at[i, h], a_recv.at[kv, h], (side * 8 + i, narrow)
+        )
+
+    def own_copy(h):
+        return pltpu.make_async_copy(rows_out.at[h, wide % 8], rows_in.at[core, h, y, kv], local_sem.at[7 + h])
+
+    def local(i):
+        return own_target & (i == wide % 8)
 
     for h in range(2):
         def wait_part(step, carry):
             s = (held + step) % 8
-            remote(
-                part.at[s, head_rows(h)], p_in.at[s, head_rows(h)], p_send.at[step, h], p_recv.at[s, h], combiner(s)
-            ).wait_recv()
+            remote(share(s, h), p_in.at[s, h], p_send.at[step, h], p_recv.at[s, h], combiner(s)).wait_recv()
             return carry
 
         lax.fori_loop(1, 8, wait_part, 0)
-        for g in range(4):
-            total = jnp.zeros((HD, HD), jnp.float32)
+        for i in range(8):
+            total = jnp.zeros((PIECE, HD), jnp.float32)
             for s in range(8):
-                column = s * 8 + h * 4 + g
-                rows = p_in[s, h * QB + g * HD:h * QB + (g + 1) * HD, :].astype(jnp.float32)
-                total = total + rows * turned[:, column:column + 1]
-            rows_out[h, g * HD:(g + 1) * HD, :] = total.astype(jnp.bfloat16)
-        each_target(h, lambda copy: copy.start(), lambda copy: copy.start())
-
-    fetch.wait()
-    duty = ((from_y == 1) & (side == 0)) | ((from_y == 3) & (side == 1))
-    onward = jnp.where(side == 0, ahead, behind) * 2 + core
-
-    def product(head):
+                column = s * 16 + i // 2 * 4 + h * 2 + i % 2
+                total = total + p_in[s, h, i].astype(jnp.float32) * turned[:PIECE, column:column + 1]
+            rows_out[h, i] = total.astype(jnp.bfloat16)
+
+        def start_row(i, carry):
+            @pl.when(local(i))
+            def _():
+                own_copy(h).start()
+
+            @pl.when(jnp.logical_not(local(i)))
+            def _():
+                row_copy(i, h).start()
+
+            return carry
+
+        lax.fori_loop(0, 8, start_row, 0)
+
+    def batch(side_core, h, piece):
+        return rows_in.at[side_core, h, piece]
+
+    def ring_copy(h, direction, piece):
+        return remote(
+            batch(core, h, piece), batch(core, h, piece),
+            ring_send.at[h, direction], ring_recv.at[h, direction], (wide, ring[direction] * 2 + core),
+        )
+
+    def on_copy(h, piece):
+        return remote(
+            batch(core, h, piece), batch(core, h, piece), on_send.at[h], on_recv.at[h], (wide, ring[h] * 2 + core)
+        )
+
+    def forward(h, piece, side_core):
+        return remote(
+            batch(side_core, h, piece), batch(side_core, h, piece),
+            f_send.at[h, piece], f_recv.at[h, piece], (wide, buddy),
+        )
+
+    for h in range(2):
+        def wait_row(k, carry):
+            mine = own_target & (k == kv)
+
+            @pl.when(mine)
+            def _():
+                own_copy(h).wait()
+
+            @pl.when(jnp.logical_not(mine))
+            def _():
+                remote(
+                    rows_out.at[h, 0], rows_in.at[core, h, y, k], a_send.at[0, h], a_recv.at[k, h], (wide, buddy)
+                ).wait_recv()
+
+            return carry
+
+        lax.fori_loop(0, 8, wait_row, 0)
+        for direction in range(2):
+            ring_copy(h, direction, y).start()
+        forward(h, y, core).start()
+
+    for h in range(2):
+        ring_copy(h, h, behind[h]).wait_recv()
+        on_copy(h, behind[h]).start()
+        forward(h, behind[h], core).start()
+
+    for copy in fetches:
+        copy.wait()
+
+    def product(side_core, h):
+        rows = jnp.concatenate([rows_in[side_core, h, :, k].reshape(HALF, HD) for k in range(KVH)], axis=1)
         return jnp.dot(
-            rows_in[head], w_in[pl.ds(pl.multiple_of(head * HD, HD), HD), :], preferred_element_type=jnp.float32
-        )
-
-    def forward(s, h):
-        head = s * 4 + core * 2 + h
-        return remote(rows_in.at[head], rows_in.at[head], f_send.at[s, h], f_recv.at[head], (wide, buddy))
-
-    def along(s, h):
-        head = s * 4 + core * 2 + h
-        return remote(rows_in.at[head], rows_in.at[head], y_send.at[s, h], a_recv.at[head], (wide, onward))
+            rows, w_in[side_core * 2 + h].reshape(KVH * HD, 512), preferred_element_type=jnp.float32
+        )
 
     total = jnp.zeros((HALF, 512), jnp.float32)
     for h in range(2):
-        def arrive(s, total):
-            head = s * 4 + core * 2 + h
-            local = own_target & (s == kv)
-
-            @pl.when(local)
-            def _():
-                own_copy(0, h).wait()
-
-            @pl.when(jnp.logical_not(local))
-            def _():
-                remote(
-                    rows_in.at[head], rows_in.at[head], f_send.at[s, h], a_recv.at[head], (wide, buddy)
-                ).wait_recv()
-
-            forward(s, h).start()
-
-            @pl.when(duty)
-            def _():
-                along(s, h).start()
-
-            return total + product(head)
-
-        total = lax.fori_loop(0, 8, arrive, total)
-
-        def arrive_pair(s, total):
-            head = s * 4 + (1 - core) * 2 + h
-            remote(rows_in.at[head], rows_in.at[head], f_send.at[s, h], f_recv.at[head], (wide, buddy)).wait_recv()
-            return total + product(head)
-
-        total = lax.fori_loop(0, 8, arrive_pair, total)
+        ring_copy(h, 1 - h, behind[1 - h]).wait_recv()
+        forward(h, behind[1 - h], core).start()
+        on_copy(h, (y + 2) % NY).wait_recv()
+        forward(h, (y + 2) % NY, core).start()
+        total = total + product(core, h)
+    for h in range(2):
+        for piece in range(NY):
+            forward(h, piece, 1 - core).wait_recv()
+        total = total + product(1 - core, h)
     result[...] = total.astype(jnp.bfloat16)
 
     def drain(step, carry):
@@ -600,18 +609,19 @@
         relay_copy(across).wait_send()
         pass_copy(across).wait_send()
     for h in range(2):
-        each_target(h, lambda copy: copy.wait_send(), lambda copy: None)
-
-        def drain_rows(s, carry):
-            forward(s, h).wait_send()
-
-            @pl.when(duty)
+        def drain_row(i, carry):
+            @pl.when(jnp.logical_not(local(i)))
             def _():
-                along(s, h).wait_send()
+                row_copy(i, h).wait_send()
 
             return carry
 
-        lax.fori_loop(0, 8, drain_rows, 0)
+        lax.fori_loop(0, 8, drain_row, 0)
+        for direction in range(2):
+            ring_copy(h, direction, y).wait_send()
+        on_copy(h, behind[h]).wait_send()
+        for piece in range(NY):
+            forward(h, piece, core).wait_send()
 
 
 def finish(part, lse, weight):
@@ -623,19 +633,20 @@
         in_specs=[anywhere] * 3,
         out_specs=pl.BlockSpec(memory_space=pltpu.VMEM),
         scratch_shapes=[
-            pltpu.VMEM((8, ROWS, HD), jnp.bfloat16),
-            pltpu.VMEM((8, 8, HD), jnp.float32),
-            pltpu.VMEM((4096, 512), jnp.bfloat16),
-            pltpu.VMEM((2, QB, HD), jnp.bfloat16),
-            pltpu.VMEM((2, QB, HD), jnp.bfloat16),
-            pltpu.VMEM((32, HALF, HD), jnp.bfloat16),
+            pltpu.VMEM((8, 2, 8, PIECE, HD), jnp.bfloat16),
+            pltpu.VMEM((8, 16, HD), jnp.float32),
+            pltpu.VMEM((4, KVH, HD, 512), jnp.bfloat16),
+            pltpu.VMEM((2, 8, PIECE, HD), jnp.bfloat16),
+            pltpu.VMEM((2, 8, PIECE, HD), jnp.bfloat16),
+            pltpu.VMEM((2, 2, NY, KVH, PIECE, HD), jnp.bfloat16),
             dma((8, 2)), dma((8, 2)), dma((8,)), dma((8,)), dma((2,)), dma((2,)), dma((2,)),
-            dma((2, 4, 2)), dma((32,)), dma((8, 2)), dma((8, 2)), dma((32,)), dma((5,)),
+            dma((8, 2)), dma((8, 2)), dma((2, 2)), dma((2, 2)), dma((2,)), dma((2,)),
+            dma((2, NY)), dma((2, NY)), dma((9,)),
         ],
         compiler_params=pltpu.CompilerParams(
             collective_id=1, has_side_effects=True, vmem_limit_bytes=56 * MIB
         ),
-    )(part, lse, weight)
+    )(part, lse, weight.reshape(KVH, 4, HD, 512))
 
 
 def shards(queries, span_keys, span_values, cache_keys, cache_values, chosen, out_weight):

time: 160 us -> 150 us (0.938)
  the two profiles are of different devices: /device:TPU:82 before, /device:TPU:1 now
where the time goes in v5:
time: 150 us
  Pallas kernels  119 us (79%)
  waiting for transfers between devices  14.7 us (10%)
  between operations  13.4 us (9%)
  local copies, waits for them, and re-layouts  3.01 us (2%)
    pallas_call x1, Pallas kernels, finish(): pl.pallas_call(finish_kernel, out_shape=jax.ShapeDtypeStruct((HALF, 512),...  69.2 us
    pallas_call x1, Pallas kernels, spread(): pl.pallas_call(spread_kernel, out_shape=[shape(2, NW, NY, PIECE, HD), sha...  33.3 us
    pallas_call x1, Pallas kernels, attend(): pl.pallas_call(attend_kernel, out_shape=[jax.ShapeDtypeStruct((2, NW, NY,...  16.5 us
    all_gather x1, waiting for transfers between devices, shards(): weight = lax.all_gather(out_weight, 'wide', axis=0, tiled=True)  14 us
    unnamed x2, local copies, waits for them, and re-layouts  3.01 us
  transfers between devices with their start and end apart: 1, of which 1 were waited for; matrix products, arithmetic and copies ran while one was open for 1% of the time, Pallas kernels for 33%

profile of v5, /device:TPU:1, one launch (start us, length us, event | category | flops | bytes accessed | tf_op | source)
XLA Modules:
  0.0 150.1 jit_solution(17610924321202132565)
XLA Ops:
  6.5 0.0 all-gather.2.cloned.1.call-start
  6.5 0.7 all-gather.2.cloned.1.call-update
  7.3 1.3 copy.8.chosen
  8.6 33.3 %shard_map.73 = (bf16[2,16,4,64,128]{4,3,2,1,0:T(8,128)(2,1)}, bf16[4096,128]{1,0:T(8,128)(2,1)}, bf16[4096,128]{1,0:T(8,128)(2,1)}, bf16[512,128]{1,0:T(8,128)(2,1)}, bf16[512,128]{1,0:T(8,128)(2,1)}) custom-call(bf16[256,4096]{1,0:T(8,128)(2,1)} %queries.1, bf16[256,1024]{1,0:T(8,128)(2,1)} %span_k.1, bf16[256,1024]{1,0:T(8,128)(2,1)} %span_v.1, ...), custom_call_target="tpu_custom_call" | custom-call | tf_op jit(solution)/shard_map/pallas_call | solution.py:222
  41.9 16.5 %shard_map.74 = (bf16[2,16,4,64,128]{4,3,2,1,0:T(8,128)(2,1)}, f32[4,2,16,128]{3,2,1,0:T(8,128)}) custom-call(s32[8,3]{1,0:T(8,128)} %copy.8.chosen, bf16[2,16,4,64,128]{4,3,2,1,0:T(8,128)(2,1)} %get-tuple-element.12.q, bf16[4096,128]{1,0:T(8,128)(2,1)} %k_own.1, bf16[4096,128]{1,0:T(8,128)(2,1)} %v_own.1, bf16[4096,128]{1,0:T(8,128)(2,1)} %get-tuple-element.13.k_pair, ...), custom_call_target="tpu_custom_call" | custom-call | flops 14000000000 | bytes 10485760 | tf_op jit(solution)/shard_map/pallas_call | solution.py:359
  58.3 14.0 %all-gather.2.cloned.1.call-done = bf16[4096,512]{1,0:T(8,128)(2,1)} async-done(((bf16[256,512]{1,0:T(8,128)(2,1)}), bf16[4096,512]{1,0:T(8,128)(2,1)}) %all-gather.2.cloned.1.call-update) | async-done | bytes 4194320 | tf_op jit(solution)/shard_map/all_gather | solution.py:653
  72.3 69.2 %shard_map.75 = bf16[256,512]{1,0:T(8,128)(2,1)} custom-call(bf16[2,16,4,64,128]{4,3,2,1,0:T(8,128)(2,1)} %get-tuple-element.17.part, f32[4,2,16,128]{3,2,1,0:T(8,128)} %get-tuple-element.18.lse, bf16[8,4,128,512]{3,2,1,0:T(8,128)(2,1)} %bitcast.1), custom_call_target="tpu_custom_call" | custom-call | tf_op jit(solution)/shard_map/pallas_call | solution.py:630
  141.6 1.7 %copy.10 = bf16[256,512]{1,0:T(8,128)(2,1)} copy(bf16[256,512]{1,0:T(8,128)(2,1)} %shard_map.75) | data formatting | bytes 524288
Async XLA Ops:
  6.5 65.8 %all-gather.2.cloned.1.call-start = ((), (), s32[]{:S(2)}) async-start(), calls=%async_computation | async-start | bytes 4456448 | tf_op jit(solution)/shard_map/all_gather | solution.py:653
Sparse Core Ops, SparseCore 0:
  9.5 62.8 all-gather.1

commit v6 on v5

--- a/solution.py
+++ b/solution.py
@@ -38,13 +38,15 @@
 
 def spread_kernel(
     queries, span_k, span_v, cache_k, cache_v,
-    q_out, pk_out, pv_out, sk_out, sv_out,
-    q_send, q_recv, ring_send, ring_recv, pass_send, pass_recv,
-    kv_send, kv_recv, span_send, span_recv, local_sem, span_local,
+    q_out, pk_out, pv_out, s_out,
+    s_in, q_send, q_recv, ring_send, ring_recv, pass_send, pass_recv,
+    kv_send, kv_recv, s_send, s_recv, turn_send, turn_recv, share_send, share_recv, local_sem,
 ):
     wide, narrow, y, core = place()
     buddy = y * 2 + 1 - core
-    block, half = wide // 2, wide % 2
+    z, x, side = wide // 4, wide % 4, wide % 2
+    ring = [(y + 1) % NY, (y + NY - 1) % NY]
+    behind = ring[::-1]
     barrier = pltpu.get_barrier_semaphore()
 
     def greet(step, carry):
@@ -54,165 +56,158 @@
         return carry
 
     lax.fori_loop(1, NW, greet, 0)
-    ring = [(y + 1) % NY * 2 + core, (y + NY - 1) % NY * 2 + core]
-    for neighbour in (buddy, *ring):
+    for neighbour in (buddy, *((y + step) % NY * 2 + core for step in range(1, NY))):
         pl.semaphore_signal(barrier, inc=1, device_id=(wide, neighbour), device_id_type=MESH)
-    pl.semaphore_wait(barrier, NW + 2)
-
-    def q_src(kv, head):
-        column = pl.multiple_of(kv * 512 + core * 256 + head * HD, HD)
-        return queries.at[pl.ds(pl.multiple_of(y * PIECE, PIECE), PIECE), pl.ds(column, HD)]
-
-    def q_dst(source, head):
-        return q_out.at[head, source, y]
-
-    def batch(group, head, piece):
-        return q_out.at[head, pl.ds(group * 4, 4), piece]
-
-    def ring_copy(group, head, direction, piece):
-        return remote(
-            batch(group, head, piece), batch(group, head, piece),
-            ring_send.at[group, head, direction], ring_recv.at[group, head, direction], (wide, ring[direction]),
-        )
-
-    def pass_copy(group, head, piece):
-        return remote(
-            batch(group, head, piece), batch(group, head, piece),
-            pass_send.at[group, head], pass_recv.at[group, head], (wide, ring[head]),
-        )
-
-    def span_pair(kv, which):
-        src = (span_k, span_v)[which].at[:, pl.ds(pl.multiple_of(kv * HD, HD), HD)]
-        return src
-
-    def span_dst(part, which):
-        return (sk_out, sv_out)[which].at[pl.ds(pl.multiple_of(part * HALF, HALF), HALF), :]
-
-    def q_copy(step, head):
-        target = (wide + step) % NW
-        return remote(
-            q_src(target // 2, head), q_dst(wide, head),
-            q_send.at[step, head], q_recv.at[wide, head], (target, narrow),
-        )
-
+    pl.semaphore_wait(barrier, NW + 3)
+
+    tokens = pl.ds(pl.multiple_of(y * PIECE, PIECE), PIECE)
+
+    def q_src(kv):
+        return queries.at[tokens, pl.ds(pl.multiple_of(kv * 512 + core * 256, 256), 256)]
+
+    def q_copy(dz, dx):
+        target = (z + dz) % 4 * 4 + (x + dx) % 4
+        return remote(
+            q_src(target // 2), q_out.at[wide, y], q_send.at[dz * 4 + dx], q_recv.at[wide], (target, narrow)
+        )
+
+    steps = [(dz, dx) for dz in (0, 1, 3, 2) for dx in (0, 1, 3, 2) if dz or dx]
+    own_q = pltpu.make_async_copy(q_src(wide // 2), q_out.at[wide, y], local_sem.at[0])
+
+    s_home = wide // 8
+    own_s = s_home == side
+
+    def s_src(which, kv):
+        return (span_k, span_v)[which].at[tokens, pl.ds(pl.multiple_of(kv * HD, HD), HD)]
+
+    def s_copy(which, kv):
+        return remote(
+            s_src(which, kv), s_in.at[wide % 8], s_send.at[kv], s_recv.at[wide % 8], (kv * 2 + s_home, narrow)
+        )
+
+    def s_local(which):
+        return pltpu.make_async_copy(s_src(which, wide // 2), s_in.at[wide % 8], local_sem.at[1])
+
+    def s_start(kv, carry):
+        away = jnp.logical_not(own_s & (kv == wide // 2))
+        for which in range(2):
+            @pl.when((core == which) & away)
+            def _():
+                s_copy(which, kv).start()
+
+            @pl.when((core == which) & jnp.logical_not(away))
+            def _():
+                s_local(which).start()
+
+        return carry
+
+    for dz, dx in steps[:3]:
+        q_copy(dz, dx).start()
+    own_q.start()
+    lax.fori_loop(0, KVH, s_start, 0)
+    for dz, dx in steps[3:]:
+        q_copy(dz, dx).start()
     kv_copies = [
         remote(src, dst, kv_send.at[i], kv_recv.at[i], (wide, buddy))
         for i, (src, dst) in enumerate(((cache_k, pk_out), (cache_v, pv_out)))
     ]
-    span_owner = y == block % 4
-
-    def span_copy(kv, which):
-        return remote(
-            span_pair(kv, which), span_dst(half, which),
-            span_send.at[kv, which], span_recv.at[half, which], (kv * 2 + block // 4, narrow),
-        )
-
-    def span_own(kv, which):
-        return pltpu.make_async_copy(span_pair(kv, which), span_dst(half, which), span_local.at[which])
-
-    self_span = span_owner & (half == block // 4)
-
-    def start_q(step, carry):
-        for head in range(2):
-            q_copy(step, head).start()
-        return carry
-
-    lax.fori_loop(1, NW, start_q, 0)
-    for head in range(2):
-        pltpu.make_async_copy(q_src(wide // 2, head), q_dst(wide, head), local_sem.at[head]).start()
-
-    def each_span(kv, carry, act):
-        @pl.when(span_owner & (kv * 2 + block // 4 != wide))
-        def _():
-            for which in range(2):
-                act(span_copy(kv, which))
-
-        return carry
-
-    lax.fori_loop(0, KVH, lambda kv, c: each_span(kv, c, lambda copy: copy.start()), 0)
-
-    @pl.when(self_span)
-    def _():
-        for which in range(2):
-            span_own(block, which).start()
-
     for copy in kv_copies:
         copy.start()
 
-    for head in range(2):
-        pltpu.make_async_copy(q_src(wide // 2, head), q_dst(wide, head), local_sem.at[head]).wait()
-    behind = [(y + NY - 1) % NY, (y + 1) % NY]
-
-    def gather_batch(step, carry):
-        group = (wide // 4 + step) % 4
-
-        def wait_source(i, carry):
+    def ring_copy(group, direction, piece):
+        batch = q_out.at[pl.ds(group * 4, 4), piece]
+        return remote(
+            batch, batch, ring_send.at[group, direction], ring_recv.at[group, direction],
+            (wide, ring[direction] * 2 + core),
+        )
+
+    def pass_copy(group, direction, piece):
+        batch = q_out.at[pl.ds(group * 4 + direction * 2, 2), piece]
+        return remote(
+            batch, batch, pass_send.at[group, direction], pass_recv.at[group, direction],
+            (wide, ring[direction] * 2 + core),
+        )
+
+    own_q.wait()
+    groups = [(z + step) % 4 for step in (0, 3, 1, 2)]
+    for group in groups:
+        for i in range(4):
             source = group * 4 + i
 
             @pl.when(source != wide)
             def _():
-                for head in range(2):
-                    remote(
-                        q_src(0, head), q_dst(source, head),
-                        q_send.at[0, head], q_recv.at[source, head], (source, narrow),
-                    ).wait_recv()
-
-            return carry
-
-        lax.fori_loop(0, 4, wait_source, 0)
-        for head in range(2):
-            for direction in range(2):
-                ring_copy(group, head, direction, y).start()
-        return carry
-
-    lax.fori_loop(0, 4, gather_batch, 0)
-
-    def pass_batch(step, carry):
-        group = (wide // 4 + step) % 4
-        for head in range(2):
-            ring_copy(group, head, head, behind[head]).wait_recv()
-            pass_copy(group, head, behind[head]).start()
-        return carry
-
-    lax.fori_loop(0, 4, pass_batch, 0)
-
-    def finish_batch(step, carry):
-        group = (wide // 4 + step) % 4
-        for head in range(2):
-            ring_copy(group, head, 1 - head, behind[1 - head]).wait_recv()
-            pass_copy(group, head, (y + 2) % NY).wait_recv()
-            pass_copy(group, head, behind[head]).wait_send()
-            for direction in range(2):
-                ring_copy(group, head, direction, y).wait_send()
-        return carry
-
-    lax.fori_loop(0, 4, finish_batch, 0)
-
-    def wait_q(step, carry):
-        for head in range(2):
-            q_copy(step, head).wait_send()
-        return carry
-
-    lax.fori_loop(1, NW, wait_q, 0)
-    lax.fori_loop(0, KVH, lambda kv, c: each_span(kv, c, lambda copy: copy.wait_send()), 0)
-
-    @pl.when(self_span)
-    def _():
-        for which in range(2):
-            span_own(block, which).wait()
-
-    held = wide % 2 * 4 + y
-    for part in range(2):
-        @pl.when(held * 2 + part != wide)
+                remote(
+                    q_src(0), q_out.at[source, y], q_send.at[1], q_recv.at[source], (source, narrow)
+                ).wait_recv()
+
+        for direction in range(2):
+            ring_copy(group, direction, y).start()
+
+    def s_wait(i, carry):
+        mine = own_s & (i == wide % 8)
+
+        @pl.when(mine)
         def _():
-            for which in range(2):
-                remote(
-                    span_pair(0, which), span_dst(part, which),
-                    span_send.at[0, which], span_recv.at[part, which], (wide, buddy),
-                ).wait_recv()
-
+            s_local(0).wait()
+
+        @pl.when(jnp.logical_not(mine))
+        def _():
+            remote(s_src(0, 0), s_in.at[i], s_send.at[0], s_recv.at[i], (wide, buddy)).wait_recv()
+
+        return carry
+
+    lax.fori_loop(0, 8, s_wait, 0)
+
+    def turn_copy(step):
+        to = (y + step) % NY
+        return remote(
+            s_in.at[pl.ds(to * 2, 2)], s_out.at[core, :, y], turn_send.at[step], turn_recv.at[y],
+            (wide, to * 2 + core),
+        )
+
+    keep = pltpu.make_async_copy(s_in.at[pl.ds(y * 2, 2)], s_out.at[core, :, y], local_sem.at[2])
+    keep.start()
+    for step in range(1, NY):
+        turn_copy(step).start()
+
+    for group in groups:
+        for direction in range(2):
+            ring_copy(group, direction, behind[direction]).wait_recv()
+            pass_copy(group, direction, behind[direction]).start()
+
+    keep.wait()
+    for step in range(1, NY):
+        origin = (y + step) % NY
+        remote(
+            s_in.at[pl.ds(0, 2)], s_out.at[core, :, origin], turn_send.at[step], turn_recv.at[origin], (wide, buddy)
+        ).wait_recv()
+    share = remote(s_out.at[core], s_out.at[core], share_send.at[0], share_recv.at[core], (wide, buddy))
+    share.start()
+
+    for group in groups:
+        for direction in range(2):
+            pass_copy(group, direction, (y + 2) % NY).wait_recv()
+    remote(s_out.at[core], s_out.at[1 - core], share_send.at[0], share_recv.at[1 - core], (wide, buddy)).wait_recv()
     for copy in kv_copies:
         copy.wait()
+    share.wait_send()
+    for group in groups:
+        for direction in range(2):
+            ring_copy(group, direction, y).wait_send()
+            pass_copy(group, direction, behind[direction]).wait_send()
+    for step in range(1, NY):
+        turn_copy(step).wait_send()
+    for dz, dx in steps:
+        q_copy(dz, dx).wait_send()
+
+    def s_drain(kv, carry):
+        @pl.when(jnp.logical_not(own_s & (kv == wide // 2)))
+        def _():
+            s_copy(0, kv).wait_send()
+
+        return carry
+
+    lax.fori_loop(0, KVH, s_drain, 0)
 
 
 def spread(queries, span_k, span_v, cache_k, cache_v):
@@ -221,12 +216,13 @@
     dma = pltpu.SemaphoreType.DMA
     return pl.pallas_call(
         spread_kernel,
-        out_shape=[shape(2, NW, NY, PIECE, HD), shape(KB, HD), shape(KB, HD), shape(QB, HD), shape(QB, HD)],
+        out_shape=[shape(NW, NY, PIECE, 2 * HD), shape(KB, HD), shape(KB, HD), shape(2, 2, NY, PIECE, HD)],
         in_specs=[anywhere] * 5,
-        out_specs=[anywhere] * 5,
+        out_specs=[anywhere] * 4,
         scratch_shapes=[
-            dma((NW, 2)), dma((NW, 2)), dma((4, 2, 2)), dma((4, 2, 2)), dma((4, 2)), dma((4, 2)),
-            dma((2,)), dma((2,)), dma((KVH, 2)), dma((2, 2)), dma((2,)), dma((2,)),
+            pltpu.VMEM((8, PIECE, HD), jnp.bfloat16),
+            dma((NW,)), dma((NW,)), dma((4, 2)), dma((4, 2)), dma((4, 2)), dma((4, 2)),
+            dma((2,)), dma((2,)), dma((KVH,)), dma((8,)), dma((NY,)), dma((NY,)), dma((1,)), dma((2,)), dma((3,)),
         ],
         compiler_params=pltpu.CompilerParams(
             collective_id=0, has_side_effects=True, vmem_limit_bytes=56 * MIB
@@ -235,7 +231,7 @@
 
 
 def attend_kernel(
-    chosen, q, k_own, v_own, k_pair, v_pair, sk, sv, out, lse,
+    chosen, q, k_own, v_own, k_pair, v_pair, span, out, lse,
     q_in, k_both, v_wide, sk_in, s_wide, out_in, lse_in, acc, peak, sems, out_sem,
 ):
     wide, narrow, y, core = place()
@@ -243,8 +239,8 @@
     first = wide % 2 * 8 + y * 2
     moves = [
         (q, q_in),
-        (sk, sk_in),
-        (sv, s_wide.at[:, :HD]),
+        (span.at[0], sk_in),
+        (span.at[1], s_wide.at[:, :, :, :HD]),
         (k_own, k_both.at[0]),
         (v_own, v_wide.at[0, :, :HD]),
         (k_pair, k_both.at[1]),
@@ -253,7 +249,7 @@
     loads = [pltpu.make_async_copy(src, dst, sems.at[i]) for i, (src, dst) in enumerate(moves)]
     for copy in loads:
         copy.start()
-    s_wide[:, HD:] = jnp.ones((QB, HD), jnp.bfloat16)
+    s_wide[:, :, :, HD:] = jnp.ones((2, NY, PIECE, HD), jnp.bfloat16)
     lse_in[...] = jnp.full((NY, 2, 16, HD), FLOOR_SCORE, jnp.float32)
     for i in range(2):
         v_wide[i, :, HD:] = jnp.ones((KB, HD), jnp.bfloat16)
@@ -270,7 +266,8 @@
         return new_top, total
 
     def block_queries(b):
-        return q_in[:, pl.ds(b * 2, 2)].reshape(ROWS, HD)
+        rows = q_in[pl.ds(b * 2, 2)].reshape(QB, 2 * HD)
+        return jnp.concatenate([rows[:, :HD], rows[:, HD:]], axis=0)
 
     def load():
         return jnp.max(peak[...], axis=1, keepdims=True), acc[...]
@@ -284,7 +281,7 @@
     row = lax.broadcasted_iota(jnp.int32, (ROWS, QB), 0) % QB
     mask = row >= lax.broadcasted_iota(jnp.int32, (ROWS, QB), 1)
     fresh = jnp.full((ROWS, 1), FLOOR_SCORE, jnp.float32), jnp.zeros((ROWS, 2 * HD), jnp.float32)
-    save(fold(fresh, block_queries(held), sk_in[...], s_wide[...], mask))
+    save(fold(fresh, block_queries(held), sk_in[...].reshape(QB, HD), s_wide[...].reshape(QB, 2 * HD), mask))
     for copy in loads[3:]:
         copy.wait()
 
@@ -353,7 +350,7 @@
     lse_copy.wait()
 
 
-def attend(chosen, q, k_own, v_own, k_pair, v_pair, sk, sv):
+def attend(chosen, q, k_own, v_own, k_pair, v_pair, span):
     anywhere = pl.BlockSpec(memory_space=pl.ANY)
     dma = pltpu.SemaphoreType.DMA
     return pl.pallas_call(
@@ -362,14 +359,14 @@
             jax.ShapeDtypeStruct((2, NW, NY, PIECE, HD), jnp.bfloat16),
             jax.ShapeDtypeStruct((NY, 2, 16, HD), jnp.float32),
         ],
-        in_specs=[pl.BlockSpec(memory_space=pltpu.SMEM)] + [anywhere] * 7,
+        in_specs=[pl.BlockSpec(memory_space=pltpu.SMEM)] + [anywhere] * 6,
         out_specs=[anywhere] * 2,
         scratch_shapes=[
-            pltpu.VMEM((2, NW, NY, PIECE, HD), jnp.bfloat16),
+            pltpu.VMEM((NW, NY, PIECE, 2 * HD), jnp.bfloat16),
             pltpu.VMEM((2, KB, HD), jnp.bfloat16),
             pltpu.VMEM((2, KB, 2 * HD), jnp.bfloat16),
-            pltpu.VMEM((QB, HD), jnp.bfloat16),
-            pltpu.VMEM((QB, 2 * HD), jnp.bfloat16),
+            pltpu.VMEM((2, NY, PIECE, HD), jnp.bfloat16),
+            pltpu.VMEM((2, NY, PIECE, 2 * HD), jnp.bfloat16),
             pltpu.VMEM((2, NW, NY, PIECE, HD), jnp.bfloat16),
             pltpu.VMEM((NY, 2, 16, HD), jnp.float32),
             pltpu.VMEM((ROWS, 2 * HD), jnp.float32),
@@ -378,13 +375,13 @@
         ],
         compiler_params=pltpu.CompilerParams(vmem_limit_bytes=56 * MIB),
         cost_estimate=pl.CostEstimate(flops=14 * 10**9, bytes_accessed=10 * MIB, transcendentals=25 * 10**6),
-    )(chosen, q, k_own, v_own, k_pair, v_pair, sk, sv)
+    )(chosen, q, k_own, v_own, k_pair, v_pair, span)
 
 
 def finish_kernel(
     part, lse, weight, result,
-    p_in, l_in, w_in, relay, rows_out, rows_in,
-    p_send, p_recv, l_send, l_recv, relay_send, relay_recv, pass_send,
+    p_in, l_in, w_in, rows_out, rows_in,
+    p_send, p_recv, l_send, l_recv,
     a_send, a_recv, ring_send, ring_recv, on_send, on_recv, f_send, f_recv, local_sem,
 ):
     wide, narrow, y, core = place()
@@ -428,20 +425,6 @@
     def share(b, h):
         return part.at[h, pl.ds(b // 4 * 8, 8), b % 4]
 
-    def relay_copy(across):
-        b = (side + across) % 2 * 4 + (y + 2) % NY
-        return remote(
-            share(b, 1), relay.at[across],
-            relay_send.at[across], relay_recv.at[across], (wide, ring[1] * 2 + core),
-        )
-
-    def pass_copy(across):
-        origin = side * 4 + ring[0]
-        return remote(
-            relay.at[across], p_in.at[origin, 1],
-            pass_send.at[across], p_recv.at[origin, 1], (kv * 2 + (side + across) % 2, ring[1] * 2 + core),
-        )
-
     def part_copy(step, h):
         b = (held + step) % 8
         return remote(share(b, h), p_in.at[held, h], p_send.at[step, h], p_recv.at[held, h], combiner(b))
@@ -450,30 +433,17 @@
         b = (held + step) % 8
         return remote(lse.at[b % 4, b // 4], l_in.at[held], l_send.at[step], l_recv.at[held], combiner(b))
 
-    def straight(step):
-        return (held + step) % 4 != (y + 2) % 4
-
-    for across in range(2):
-        relay_copy(across).start()
-
-    def start_first(step, carry):
+    def start_lse(step, carry):
         lse_copy(step).start()
-        part_copy(step, 0).start()
-        return carry
-
-    lax.fori_loop(1, 8, start_first, 0)
-
-    def start_second(step, carry):
-        @pl.when(straight(step))
-        def _():
-            part_copy(step, 1).start()
-
-        return carry
-
-    lax.fori_loop(1, 8, start_second, 0)
-    for across in range(2):
-        relay_copy(across).wait_recv()
-        pass_copy(across).start()
+        return carry
+
+    lax.fori_loop(1, 8, start_lse, 0)
+    for h in range(2):
+        def start_part(step, carry):
+            part_copy(step, h).start()
+            return carry
+
+        lax.fori_loop(1, 8, start_part, 0)
     for copy in keep:
         copy.wait()
 
@@ -596,18 +566,11 @@
 
     def drain(step, carry):
         lse_copy(step).wait_send()
-        part_copy(step, 0).wait_send()
-
-        @pl.when(straight(step))
-        def _():
-            part_copy(step, 1).wait_send()
-
+        for h in range(2):
+            part_copy(step, h).wait_send()
         return carry
 
     lax.fori_loop(1, 8, drain, 0)
-    for across in range(2):
-        relay_copy(across).wait_send()
-        pass_copy(across).wait_send()
     for h in range(2):
         def drain_row(i, carry):
             @pl.when(jnp.logical_not(local(i)))
@@ -637,9 +600,8 @@
             pltpu.VMEM((8, 16, HD), jnp.float32),
             pltpu.VMEM((4, KVH, HD, 512), jnp.bfloat16),
             pltpu.VMEM((2, 8, PIECE, HD), jnp.bfloat16),
-            pltpu.VMEM((2, 8, PIECE, HD), jnp.bfloat16),
             pltpu.VMEM((2, 2, NY, KVH, PIECE, HD), jnp.bfloat16),
-            dma((8, 2)), dma((8, 2)), dma((8,)), dma((8,)), dma((2,)), dma((2,)), dma((2,)),
+            dma((8, 2)), dma((8, 2)), dma((8,)), dma((8,)),
             dma((8, 2)), dma((8, 2)), dma((2, 2)), dma((2, 2)), dma((2,)), dma((2,)),
             dma((2, NY)), dma((2, NY)), dma((9,)),
         ],
@@ -651,8 +613,8 @@
 
 def shards(queries, span_keys, span_values, cache_keys, cache_values, chosen, out_weight):
     weight = lax.all_gather(out_weight, "wide", axis=0, tiled=True)
-    q, k_pair, v_pair, sk, sv = spread(queries, span_keys, span_values, cache_keys, cache_values)
-    part, lse = attend(chosen, q, cache_keys, cache_values, k_pair, v_pair, sk, sv)
+    q, k_pair, v_pair, span = spread(queries, span_keys, span_values, cache_keys, cache_values)
+    part, lse = attend(chosen, q, cache_keys, cache_values, k_pair, v_pair, span)
     return finish(part, lse, weight)
 
 

time: 150 us -> 132 us (0.88)
  waiting for transfers between devices: 14.7 us -> 0.76 us
  Pallas kernels: 119 us -> 114 us
    all_gather x1, waiting for transfers between devices: 14 us -> 0.05 us  [shards(): weight = lax.all_gather(out_weight, 'wide', axis=0, tiled=True)]
    pallas_call x1, Pallas kernels: 69.2 us -> 58.6 us  [finish(): pl.pallas_call(finish_kernel, out_shape=jax.ShapeDtypeStruct((HALF, 512),...]
    pallas_call x1, Pallas kernels: 16.5 us -> 22.3 us  [attend(): pl.pallas_call(attend_kernel, out_shape=[jax.ShapeDtypeStruct((2, NW, NY,...]
  transfers between devices with their start and end apart: 1 -> 1, of which waited for: 1 -> 1; matrix products, arithmetic and copies ran while one was open for 1% -> 1% of each run, Pallas kernels for 33% -> 42%
where the time goes in v6:
time: 132 us; the launch traced here: 131 us
  Pallas kernels  114 us (86%)
  between operations  13.4 us (10%)
  local copies, waits for them, and re-layouts  3.01 us (2%)
    pallas_call x1, Pallas kernels, finish(): pl.pallas_call(finish_kernel, out_shape=jax.ShapeDtypeStruct((HALF, 512),...  58.6 us
    pallas_call x1, Pallas kernels, spread(): pl.pallas_call(spread_kernel, out_shape=[shape(NW, NY, PIECE, 2 * HD), sh...  33.5 us
    pallas_call x1, Pallas kernels, attend(): pl.pallas_call(attend_kernel, out_shape=[jax.ShapeDtypeStruct((2, NW, NY,...  22.3 us
    unnamed x2, local copies, waits for them, and re-layouts  3.01 us
  transfers between devices with their start and end apart: 1, of which 1 were waited for; matrix products, arithmetic and copies ran while one was open for 1% of the time, Pallas kernels for 42%

profile of v6, /device:TPU:1, one launch (start us, length us, event | category | flops | bytes accessed | tf_op | source)
XLA Modules:
  0.0 131.5 jit_solution(12065092764402041645)
XLA Ops:
  6.5 0.0 all-gather.2.cloned.1.call-start
  6.5 0.7 all-gather.2.cloned.1.call-update
  7.3 1.3 %copy.8.chosen = s32[8,3]{1,0:T(8,128)} copy(s32[8,3]{0,1:T(4,128)} %param.12) | data formatting | bytes 192 | tf_op args[5]
  8.6 33.5 %shard_map.73 = (bf16[16,4,64,256]{3,2,1,0:T(8,128)(2,1)}, bf16[4096,128]{1,0:T(8,128)(2,1)}, bf16[4096,128]{1,0:T(8,128)(2,1)}, bf16[2,2,4,64,128]{4,3,2,1,0:T(8,128)(2,1)}) custom-call(bf16[256,4096]{1,0:T(8,128)(2,1)} %queries.1, bf16[256,1024]{1,0:T(8,128)(2,1)} %span_k.1, bf16[256,1024]{1,0:T(8,128)(2,1)} %span_v.1, bf16[4096,128]{1,0:T(8,128)(2,1)} %k_own.1, ...), custom_call_target="tpu_custom_call" | custom-call | tf_op jit(solution)/shard_map/pallas_call | solution.py:217
  42.1 22.3 %shard_map.74 = (bf16[2,16,4,64,128]{4,3,2,1,0:T(8,128)(2,1)}, f32[4,2,16,128]{3,2,1,0:T(8,128)}) custom-call(s32[8,3]{1,0:T(8,128)} %copy.8.chosen, bf16[16,4,64,256]{3,2,1,0:T(8,128)(2,1)} %get-tuple-element.11.q, bf16[4096,128]{1,0:T(8,128)(2,1)} %k_own.1, bf16[4096,128]{1,0:T(8,128)(2,1)} %v_own.1, bf16[4096,128]{1,0:T(8,128)(2,1)} %get-tuple-element.12.k_pair, ...), custom_call_target="tpu_custom_call" | custom-call | flops 14000000000 | bytes 10485760 | tf_op jit(solution)/shard_map/pallas_call | solution.py:356
  64.4 0.1 all-gather.2.cloned.1.call-done
  64.4 58.6 %shard_map.75 = bf16[256,512]{1,0:T(8,128)(2,1)} custom-call(bf16[2,16,4,64,128]{4,3,2,1,0:T(8,128)(2,1)} %get-tuple-element.15.part, f32[4,2,16,128]{3,2,1,0:T(8,128)} %get-tuple-element.16.lse, bf16[8,4,128,512]{3,2,1,0:T(8,128)(2,1)} %bitcast.1), custom_call_target="tpu_custom_call" | custom-call | tf_op jit(solution)/shard_map/pallas_call | solution.py:593
  123.0 1.7 %copy.10 = bf16[256,512]{1,0:T(8,128)(2,1)} copy(bf16[256,512]{1,0:T(8,128)(2,1)} %shard_map.75) | data formatting | bytes 524288
Async XLA Ops:
  6.5 57.9 %all-gather.2.cloned.1.call-start = ((), (), s32[]{:S(2)}) async-start(), calls=%async_computation | async-start | bytes 4456448 | tf_op jit(solution)/shard_map/all_gather | solution.py:615
Sparse Core Ops, SparseCore 0:
  9.5 54.8 all-gather.1

commit v7 on v6

--- a/solution.py
+++ b/solution.py
@@ -62,17 +62,24 @@
 
     tokens = pl.ds(pl.multiple_of(y * PIECE, PIECE), PIECE)
 
-    def q_src(kv):
-        return queries.at[tokens, pl.ds(pl.multiple_of(kv * 512 + core * 256, 256), 256)]
+    def columns(kv):
+        return pl.ds(pl.multiple_of(kv * 512 + core * 256, 256), 256)
 
     def q_copy(dz, dx):
         target = (z + dz) % 4 * 4 + (x + dx) % 4
-        return remote(
-            q_src(target // 2), q_out.at[wide, y], q_send.at[dz * 4 + dx], q_recv.at[wide], (target, narrow)
-        )
-
-    steps = [(dz, dx) for dz in (0, 1, 3, 2) for dx in (0, 1, 3, 2) if dz or dx]
-    own_q = pltpu.make_async_copy(q_src(wide // 2), q_out.at[wide, y], local_sem.at[0])
+        rows = tokens if dz else slice(None)
+        return remote(
+            queries.at[rows, columns(target // 2)], q_out.at[wide, rows],
+            q_send.at[dz * 4 + dx], q_recv.at[wide], (target, narrow),
+        )
+
+    def q_wait(source, rows):
+        remote(
+            queries.at[rows, columns(0)], q_out.at[source, rows], q_send.at[1], q_recv.at[source], (source, narrow)
+        ).wait_recv()
+
+    steps = [(dz, dx) for dz in (1, 3, 2, 0) for dx in (0, 1, 3, 2) if dz or dx]
+    own_q = pltpu.make_async_copy(queries.at[:, columns(wide // 2)], q_out.at[wide], local_sem.at[0])
 
     s_home = wide // 8
     own_s = s_home == side
@@ -101,12 +108,12 @@
 
         return carry
 
-    for dz, dx in steps[:3]:
+    for dz, dx in steps[:8]:
+        q_copy(dz, dx).start()
+    lax.fori_loop(0, KVH, s_start, 0)
+    for dz, dx in steps[8:]:
         q_copy(dz, dx).start()
     own_q.start()
-    lax.fori_loop(0, KVH, s_start, 0)
-    for dz, dx in steps[3:]:
-        q_copy(dz, dx).start()
     kv_copies = [
         remote(src, dst, kv_send.at[i], kv_recv.at[i], (wide, buddy))
         for i, (src, dst) in enumerate(((cache_k, pk_out), (cache_v, pv_out)))
@@ -114,32 +121,27 @@
     for copy in kv_copies:
         copy.start()
 
+    def piece_rows(piece):
+        return pl.ds(pl.multiple_of(piece * PIECE, PIECE), PIECE)
+
     def ring_copy(group, direction, piece):
-        batch = q_out.at[pl.ds(group * 4, 4), piece]
+        batch = q_out.at[pl.ds(group * 4, 4), piece_rows(piece)]
         return remote(
             batch, batch, ring_send.at[group, direction], ring_recv.at[group, direction],
             (wide, ring[direction] * 2 + core),
         )
 
     def pass_copy(group, direction, piece):
-        batch = q_out.at[pl.ds(group * 4 + direction * 2, 2), piece]
+        batch = q_out.at[pl.ds(group * 4 + direction * 2, 2), piece_rows(piece)]
         return remote(
             batch, batch, pass_send.at[group, direction], pass_recv.at[group, direction],
             (wide, ring[direction] * 2 + core),
         )
 
-    own_q.wait()
-    groups = [(z + step) % 4 for step in (0, 3, 1, 2)]
+    groups = [(z + step) % 4 for step in (3, 1, 2)]
     for group in groups:
         for i in range(4):
-            source = group * 4 + i
-
-            @pl.when(source != wide)
-            def _():
-                remote(
-                    q_src(0), q_out.at[source, y], q_send.at[1], q_recv.at[source], (source, narrow)
-                ).wait_recv()
-
+            q_wait(group * 4 + i, tokens)
         for direction in range(2):
             ring_copy(group, direction, y).start()
 
@@ -188,6 +190,9 @@
         for direction in range(2):
             pass_copy(group, direction, (y + 2) % NY).wait_recv()
     remote(s_out.at[core], s_out.at[1 - core], share_send.at[0], share_recv.at[1 - core], (wide, buddy)).wait_recv()
+    own_q.wait()
+    for dx in range(1, 4):
+        q_wait(z * 4 + (x + dx) % 4, slice(None))
     for copy in kv_copies:
         copy.wait()
     share.wait_send()
@@ -216,7 +221,7 @@
     dma = pltpu.SemaphoreType.DMA
     return pl.pallas_call(
         spread_kernel,
-        out_shape=[shape(NW, NY, PIECE, 2 * HD), shape(KB, HD), shape(KB, HD), shape(2, 2, NY, PIECE, HD)],
+        out_shape=[shape(NW, HALF, 2 * HD), shape(KB, HD), shape(KB, HD), shape(2, 2, NY, PIECE, HD)],
         in_specs=[anywhere] * 5,
         out_specs=[anywhere] * 4,
         scratch_shapes=[
@@ -250,7 +255,7 @@
     for copy in loads:
         copy.start()
     s_wide[:, :, :, HD:] = jnp.ones((2, NY, PIECE, HD), jnp.bfloat16)
-    lse_in[...] = jnp.full((NY, 2, 16, HD), FLOOR_SCORE, jnp.float32)
+    lse_in[...] = jnp.full((2, NY, 2, 8, HD), FLOOR_SCORE, jnp.float32)
     for i in range(2):
         v_wide[i, :, HD:] = jnp.ones((KB, HD), jnp.bfloat16)
 
@@ -331,7 +336,7 @@
             for piece in range(NY):
                 for part in range(4):
                     start = part * HALF + piece * PIECE
-                    lse_in[piece, b // 4, pl.ds(b % 4 * 4 + part, 1), :] = jnp.sum(
+                    lse_in[part // 2, piece, b // 4, pl.ds(b % 4 * 2 + part % 2, 1), :] = jnp.sum(
                         jnp.where(eye, logs[start:start + PIECE], 0.0), axis=0, keepdims=True
                     )
 
@@ -357,18 +362,18 @@
         attend_kernel,
         out_shape=[
             jax.ShapeDtypeStruct((2, NW, NY, PIECE, HD), jnp.bfloat16),
-            jax.ShapeDtypeStruct((NY, 2, 16, HD), jnp.float32),
+            jax.ShapeDtypeStruct((2, NY, 2, 8, HD), jnp.float32),
         ],
         in_specs=[pl.BlockSpec(memory_space=pltpu.SMEM)] + [anywhere] * 6,
         out_specs=[anywhere] * 2,
         scratch_shapes=[
-            pltpu.VMEM((NW, NY, PIECE, 2 * HD), jnp.bfloat16),
+            pltpu.VMEM((NW, HALF, 2 * HD), jnp.bfloat16),
             pltpu.VMEM((2, KB, HD), jnp.bfloat16),
             pltpu.VMEM((2, KB, 2 * HD), jnp.bfloat16),
             pltpu.VMEM((2, NY, PIECE, HD), jnp.bfloat16),
             pltpu.VMEM((2, NY, PIECE, 2 * HD), jnp.bfloat16),
             pltpu.VMEM((2, NW, NY, PIECE, HD), jnp.bfloat16),
-            pltpu.VMEM((NY, 2, 16, HD), jnp.float32),
+            pltpu.VMEM((2, NY, 2, 8, HD), jnp.float32),
             pltpu.VMEM((ROWS, 2 * HD), jnp.float32),
             pltpu.VMEM((ROWS, HD), jnp.float32),
             dma((8,)), dma((NQB,)),
@@ -380,36 +385,35 @@
 
 def finish_kernel(
     part, lse, weight, result,
-    p_in, l_in, w_in, rows_out, rows_in,
-    p_send, p_recv, l_send, l_recv,
+    x_in, y_in, x_mid, y_mid, x_last, y_last, lx_in, ly_in, lx_mid, ly_mid, lx_last, ly_last,
+    w_in, rows_out, rows_in,
+    x_send, x_recv, y_send, y_recv, xm_send, xm_recv, ym_send, ym_recv,
     a_send, a_recv, ring_send, ring_recv, on_send, on_recv, f_send, f_recv, local_sem,
 ):
     wide, narrow, y, core = place()
     buddy = y * 2 + 1 - core
     kv, side = wide // 2, wide % 2
-    held = side * 4 + y
     ring = [(y + 1) % NY, (y + NY - 1) % NY]
     behind = ring[::-1]
     own_target = wide // 8 == side
     barrier = pltpu.get_barrier_semaphore()
 
-    def combiner(b):
-        return kv * 2 + b // 4, b % 4 * 2 + core
+    across = wide + 1 - side * 2, narrow
+
+    def along(step):
+        return wide, (y + step) % NY * 2 + core
 
     fetches = [pltpu.make_async_copy(weight.at[:, i], w_in.at[i], local_sem.at[i]) for i in range(4)]
     keep = [
-        pltpu.make_async_copy(part.at[h, pl.ds(side * 8, 8), y], p_in.at[held, h], local_sem.at[4 + h])
-        for h in range(2)
+        pltpu.make_async_copy(part.at[0, pl.ds(side * 8, 8)], x_in.at[0], local_sem.at[4]),
+        pltpu.make_async_copy(lse.at[0, :, side], lx_in.at[0], local_sem.at[5]),
+        pltpu.make_async_copy(part.at[1, :, y], y_in.at[y], local_sem.at[6]),
+        pltpu.make_async_copy(lse.at[1, y], ly_in.at[y], local_sem.at[9]),
     ]
-    keep.append(pltpu.make_async_copy(lse.at[y, side], l_in.at[held], local_sem.at[6]))
     for copy in (*keep, *fetches):
         copy.start()
-
-    def greet(step, carry):
-        pl.semaphore_signal(barrier, inc=1, device_id=combiner((held + step) % 8), device_id_type=MESH)
-        return carry
-
-    lax.fori_loop(1, 8, greet, 0)
+    for device in (across, *(along(step) for step in range(1, NY))):
+        pl.semaphore_signal(barrier, inc=1, device_id=device, device_id_type=MESH)
 
     def greet_source(s, carry):
         @pl.when(jnp.logical_not(own_target & (s == kv)))
@@ -420,43 +424,95 @@
 
     lax.fori_loop(0, 8, greet_source, 0)
     pl.semaphore_signal(barrier, inc=1, device_id=(wide, buddy), device_id_type=MESH)
-    pl.semaphore_wait(barrier, 16 - own_target.astype(jnp.int32))
-
-    def share(b, h):
-        return part.at[h, pl.ds(b // 4 * 8, 8), b % 4]
-
-    def part_copy(step, h):
-        b = (held + step) % 8
-        return remote(share(b, h), p_in.at[held, h], p_send.at[step, h], p_recv.at[held, h], combiner(b))
-
-    def lse_copy(step):
-        b = (held + step) % 8
-        return remote(lse.at[b % 4, b // 4], l_in.at[held], l_send.at[step], l_recv.at[held], combiner(b))
-
-    def start_lse(step, carry):
-        lse_copy(step).start()
-        return carry
-
-    lax.fori_loop(1, 8, start_lse, 0)
-    for h in range(2):
-        def start_part(step, carry):
-            part_copy(step, h).start()
-            return carry
-
-        lax.fori_loop(1, 8, start_part, 0)
+    pl.semaphore_wait(barrier, 13 - own_target.astype(jnp.int32))
+
+    x_copies = [
+        remote(part.at[0, pl.ds((1 - side) * 8, 8)], x_in.at[1], x_send.at[0], x_recv.at[0], across),
+        remote(lse.at[0, :, 1 - side], lx_in.at[1], x_send.at[1], x_recv.at[1], across),
+    ]
+
+    def y_copies(step):
+        to = (y + step) % NY
+        return [
+            remote(part.at[1, :, to], y_in.at[y], y_send.at[step, 0], y_recv.at[y, 0], along(step)),
+            remote(lse.at[1, to], ly_in.at[y], y_send.at[step, 1], y_recv.at[y, 1], along(step)),
+        ]
+
+    def y_arrivals(step):
+        origin = (y + step) % NY
+        return [
+            remote(part.at[1, :, 0], y_in.at[origin], y_send.at[step, 0], y_recv.at[origin, 0], across),
+            remote(lse.at[1, 0], ly_in.at[origin], y_send.at[step, 1], y_recv.at[origin, 1], across),
+        ]
+
+    def xm_copies(step):
+        to = (y + step) % NY
+        return [
+            remote(x_mid.at[to], x_last.at[y], xm_send.at[step, 0], xm_recv.at[y, 0], along(step)),
+            remote(lx_mid.at[to], lx_last.at[y], xm_send.at[step, 1], xm_recv.at[y, 1], along(step)),
+        ]
+
+    def xm_arrivals(step):
+        origin = (y + step) % NY
+        return [
+            remote(x_mid.at[0], x_last.at[origin], xm_send.at[step, 0], xm_recv.at[origin, 0], across),
+            remote(lx_mid.at[0], lx_last.at[origin], xm_send.at[step, 1], xm_recv.at[origin, 1], across),
+        ]
+
+    ym_copies = [
+        remote(y_mid.at[1 - side], y_last, ym_send.at[0], ym_recv.at[0], across),
+        remote(ly_mid.at[1 - side], ly_last, ym_send.at[1], ym_recv.at[1], across),
+    ]
+
+    for copy in x_copies:
+        copy.start()
+    for step in (1, 3, 2):
+        for copy in y_copies(step):
+            copy.start()
+
+    def weigh(logs):
+        top = jnp.max(logs, axis=0)
+        shares = jnp.exp2(logs - top[None])
+        total = jnp.sum(shares, axis=0)
+        shares = (shares / total[None]).reshape(-1, HD)
+        turned = jnp.transpose(jnp.concatenate([shares] * (HD // shares.shape[0]), axis=0))
+        return turned[:PIECE], top + jnp.log2(total)
+
+    def mix(turned, columns, pieces):
+        total = jnp.zeros((PIECE, HD), jnp.float32)
+        for column, piece in zip(columns, pieces):
+            total = total + piece.astype(jnp.float32) * turned[:, column:column + 1]
+        return total.astype(jnp.bfloat16)
+
     for copy in keep:
         copy.wait()
-
-    def wait_lse(step, carry):
-        s = (held + step) % 8
-        remote(lse.at[0, 0], l_in.at[s], l_send.at[step], l_recv.at[s], combiner(s)).wait_recv()
-        return carry
-
-    lax.fori_loop(1, 8, wait_lse, 0)
-    logs = l_in[...]
-    shares = jnp.exp2(logs - jnp.max(logs, axis=0, keepdims=True))
-    shares = shares / jnp.sum(shares, axis=0, keepdims=True)
-    turned = jnp.transpose(shares.reshape(HD, HD))
+    for copy in x_copies:
+        copy.wait_recv()
+    turned, logs = weigh(lx_in[...].reshape(2, NY * 8, HD))
+    lx_mid[...] = logs.reshape(NY, 8, HD)
+    for piece in range(NY):
+        for i in range(8):
+            column = piece * 8 + i
+            x_mid[piece, i] = mix(turned, (column, 32 + column), (x_in[0, i, piece], x_in[1, i, piece]))
+    x_keep = [
+        pltpu.make_async_copy(x_mid.at[y], x_last.at[y], local_sem.at[10]),
+        pltpu.make_async_copy(lx_mid.at[y], lx_last.at[y], local_sem.at[11]),
+    ]
+    for copy in x_keep:
+        copy.start()
+    for step in (1, 3, 2):
+        for copy in xm_copies(step):
+            copy.start()
+
+    for step in (1, 3, 2):
+        for copy in y_arrivals(step):
+            copy.wait_recv()
+    turned, logs = weigh(ly_in[...].reshape(NY, 16, HD))
+    ly_mid[...] = logs.reshape(2, 8, HD)
+    for i in range(16):
+        y_mid[i // 8, i % 8] = mix(turned, [s * 16 + i for s in range(NY)], [y_in[s, i] for s in range(NY)])
+    for copy in ym_copies:
+        copy.start()
 
     def row_copy(i, h):
         return remote(
@@ -470,18 +526,21 @@
         return own_target & (i == wide % 8)
 
     for h in range(2):
-        def wait_part(step, carry):
-            s = (held + step) % 8
-            remote(share(s, h), p_in.at[s, h], p_send.at[step, h], p_recv.at[s, h], combiner(s)).wait_recv()
-            return carry
-
-        lax.fori_loop(1, 8, wait_part, 0)
-        for i in range(8):
-            total = jnp.zeros((PIECE, HD), jnp.float32)
-            for s in range(8):
-                column = s * 16 + i // 2 * 4 + h * 2 + i % 2
-                total = total + p_in[s, h, i].astype(jnp.float32) * turned[:PIECE, column:column + 1]
-            rows_out[h, i] = total.astype(jnp.bfloat16)
+        if h == 0:
+            for copy in x_keep:
+                copy.wait()
+            for step in (1, 3, 2):
+                for copy in xm_arrivals(step):
+                    copy.wait_recv()
+            turned, logs = weigh(lx_last[...])
+            for i in range(8):
+                rows_out[h, i] = mix(turned, [s * 8 + i for s in range(NY)], [x_last[s, i] for s in range(NY)])
+        else:
+            for copy in ym_copies:
+                copy.wait_recv()
+            turned, logs = weigh(jnp.stack([ly_mid[side], ly_last[...]]))
+            for i in range(8):
+                rows_out[h, i] = mix(turned, (i, 8 + i), (y_mid[side, i], y_last[i]))
 
         def start_row(i, carry):
             @pl.when(local(i))
@@ -564,13 +623,11 @@
         total = total + product(1 - core, h)
     result[...] = total.astype(jnp.bfloat16)
 
-    def drain(step, carry):
-        lse_copy(step).wait_send()
-        for h in range(2):
-            part_copy(step, h).wait_send()
-        return carry
-
-    lax.fori_loop(1, 8, drain, 0)
+    for copy in (*x_copies, *ym_copies):
+        copy.wait_send()
+    for step in range(1, NY):
+        for copy in (*y_copies(step), *xm_copies(step)):
+            copy.wait_send()
     for h in range(2):
         def drain_row(i, carry):
             @pl.when(jnp.logical_not(local(i)))
@@ -596,14 +653,24 @@
         in_specs=[anywhere] * 3,
         out_specs=pl.BlockSpec(memory_space=pltpu.VMEM),
         scratch_shapes=[
-            pltpu.VMEM((8, 2, 8, PIECE, HD), jnp.bfloat16),
-            pltpu.VMEM((8, 16, HD), jnp.float32),
+            pltpu.VMEM((2, 8, NY, PIECE, HD), jnp.bfloat16),
+            pltpu.VMEM((NY, 16, PIECE, HD), jnp.bfloat16),
+            pltpu.VMEM((NY, 8, PIECE, HD), jnp.bfloat16),
+            pltpu.VMEM((2, 8, PIECE, HD), jnp.bfloat16),
+            pltpu.VMEM((NY, 8, PIECE, HD), jnp.bfloat16),
+            pltpu.VMEM((8, PIECE, HD), jnp.bfloat16),
+            pltpu.VMEM((2, NY, 8, HD), jnp.float32),
+            pltpu.VMEM((NY, 2, 8, HD), jnp.float32),
+            pltpu.VMEM((NY, 8, HD), jnp.float32),
+            pltpu.VMEM((2, 8, HD), jnp.float32),
+            pltpu.VMEM((NY, 8, HD), jnp.float32),
+            pltpu.VMEM((8, HD), jnp.float32),
             pltpu.VMEM((4, KVH, HD, 512), jnp.bfloat16),
             pltpu.VMEM((2, 8, PIECE, HD), jnp.bfloat16),
             pltpu.VMEM((2, 2, NY, KVH, PIECE, HD), jnp.bfloat16),
-            dma((8, 2)), dma((8, 2)), dma((8,)), dma((8,)),
+            dma((2,)), dma((2,)), dma((NY, 2)), dma((NY, 2)), dma((NY, 2)), dma((NY, 2)), dma((2,)), dma((2,)),
             dma((8, 2)), dma((8, 2)), dma((2, 2)), dma((2, 2)), dma((2,)), dma((2,)),
-            dma((2, NY)), dma((2, NY)), dma((9,)),
+            dma((2, NY)), dma((2, NY)), dma((12,)),
         ],
         compiler_params=pltpu.CompilerParams(
             collective_id=1, has_side_effects=True, vmem_limit_bytes=56 * MIB

time: 132 us -> 126 us (0.955)
  Pallas kernels: 114 us -> 96.6 us
  waiting for transfers between devices: 0.76 us -> 12.5 us
    all_gather x1, waiting for transfers between devices: 0.05 us -> 11.8 us  [shards(): weight = lax.all_gather(out_weight, 'wide', axis=0, tiled=True)]
    pallas_call x1, Pallas kernels: 58.6 us -> 50.6 us  [finish(): pl.pallas_call(finish_kernel, out_shape=jax.ShapeDtypeStruct((HALF, 512),...]
    pallas_call x1, Pallas kernels: 22.3 us -> 16.5 us  [attend(): pl.pallas_call(attend_kernel, out_shape=[jax.ShapeDtypeStruct((2, NW, NY,...]
    pallas_call x1, Pallas kernels: 33.5 us -> 29.5 us  [spread(): pl.pallas_call(spread_kernel, out_shape=[shape(NW, HALF, 2 * HD), shape(K...]
  transfers between devices with their start and end apart: 1 -> 1, of which waited for: 1 -> 1; matrix products, arithmetic and copies ran while one was open for 1% -> 1% of each run, Pallas kernels for 42% -> 37%
where the time goes in v7:
time: 126 us; the launch traced here: 125 us
  Pallas kernels  96.6 us (77%)
  between operations  13.4 us (11%)
  waiting for transfers between devices  12.5 us (10%)
  local copies, waits for them, and re-layouts  3.01 us (2%)
    pallas_call x1, Pallas kernels, finish(): pl.pallas_call(finish_kernel, out_shape=jax.ShapeDtypeStruct((HALF, 512),...  50.6 us
    pallas_call x1, Pallas kernels, spread(): pl.pallas_call(spread_kernel, out_shape=[shape(NW, HALF, 2 * HD), shape(K...  29.5 us
    pallas_call x1, Pallas kernels, attend(): pl.pallas_call(attend_kernel, out_shape=[jax.ShapeDtypeStruct((2, NW, NY,...  16.5 us
    all_gather x1, waiting for transfers between devices, shards(): weight = lax.all_gather(out_weight, 'wide', axis=0, tiled=True)  11.8 us
    unnamed x2, local copies, waits for them, and re-layouts  3.01 us
  transfers between devices with their start and end apart: 1, of which 1 were waited for; matrix products, arithmetic and copies ran while one was open for 1% of the time, Pallas kernels for 37%

profile of v7, /device:TPU:1, one launch (start us, length us, event | category | flops | bytes accessed | tf_op | source)
XLA Modules:
  0.0 125.5 jit_solution(9907346164695856111)
XLA Ops:
  6.5 0.0 all-gather.2.cloned.1.call-start
  6.5 0.7 all-gather.2.cloned.1.call-update
  7.3 1.3 %copy.8.chosen = s32[8,3]{1,0:T(8,128)} copy(s32[8,3]{0,1:T(4,128)} %param.12) | data formatting | bytes 192 | tf_op args[5]
  8.6 29.5 %shard_map.73 = (bf16[16,256,256]{2,1,0:T(8,128)(2,1)}, bf16[4096,128]{1,0:T(8,128)(2,1)}, bf16[4096,128]{1,0:T(8,128)(2,1)}, bf16[2,2,4,64,128]{4,3,2,1,0:T(8,128)(2,1)}) custom-call(bf16[256,4096]{1,0:T(8,128)(2,1)} %queries.1, bf16[256,1024]{1,0:T(8,128)(2,1)} %span_k.1, bf16[256,1024]{1,0:T(8,128)(2,1)} %span_v.1, bf16[4096,128]{1,0:T(8,128)(2,1)} %k_own.1, ...), custom_call_target="tpu_custom_call" | custom-call | tf_op jit(solution)/shard_map/pallas_call | solution.py:222
  38.1 16.5 %shard_map.74 = (bf16[2,16,4,64,128]{4,3,2,1,0:T(8,128)(2,1)}, f32[2,4,2,8,128]{4,3,2,1,0:T(8,128)}) custom-call(s32[8,3]{1,0:T(8,128)} %copy.8.chosen, bf16[16,256,256]{2,1,0:T(8,128)(2,1)} %get-tuple-element.11.q, bf16[4096,128]{1,0:T(8,128)(2,1)} %k_own.1, bf16[4096,128]{1,0:T(8,128)(2,1)} %v_own.1, bf16[4096,128]{1,0:T(8,128)(2,1)} %get-tuple-element.12.k_pair, ...), custom_call_target="tpu_custom_call" | custom-call | flops 14000000000 | bytes 10485760 | tf_op jit(solution)/shard_map/pallas_call | solution.py:361
  54.6 11.8 %all-gather.2.cloned.1.call-done = bf16[4096,512]{1,0:T(8,128)(2,1)} async-done(((bf16[256,512]{1,0:T(8,128)(2,1)}), bf16[4096,512]{1,0:T(8,128)(2,1)}) %all-gather.2.cloned.1.call-update) | async-done | bytes 4194320 | tf_op jit(solution)/shard_map/all_gather | solution.py:682
  66.4 50.6 %shard_map.75 = bf16[256,512]{1,0:T(8,128)(2,1)} custom-call(bf16[2,16,4,64,128]{4,3,2,1,0:T(8,128)(2,1)} %get-tuple-element.15.part, f32[2,4,2,8,128]{4,3,2,1,0:T(8,128)} %get-tuple-element.16.lse, bf16[8,4,128,512]{3,2,1,0:T(8,128)(2,1)} %bitcast.1), custom_call_target="tpu_custom_call" | custom-call | tf_op jit(solution)/shard_map/pallas_call | solution.py:650
  117.0 1.7 %copy.10 = bf16[256,512]{1,0:T(8,128)(2,1)} copy(bf16[256,512]{1,0:T(8,128)(2,1)} %shard_map.75) | data formatting | bytes 524288
Async XLA Ops:
  6.5 59.9 %all-gather.2.cloned.1.call-start = ((), (), s32[]{:S(2)}) async-start(), calls=%async_computation | async-start | bytes 4456448 | tf_op jit(solution)/shard_map/all_gather | solution.py:682
Sparse Core Ops, SparseCore 0:
  9.5 56.8 all-gather.1

commit v8 on v7

--- a/solution.py
+++ b/solution.py
@@ -300,7 +300,7 @@
         hits = []
         for i in range(2):
             c = first + jnp.where(core == 0, i, 1 - i)
-            hits.append((chosen[b, 0] == c) | (chosen[b, 1] == c) | (chosen[b, 2] == c))
+            hits.append((chosen[0, b] == c) | (chosen[1, b] == c) | (chosen[2, b] == c))
         used = hits[0] | hits[1] | (step == 0)
 
         @pl.when(used & (step != 0))
@@ -525,7 +525,7 @@
     def local(i):
         return own_target & (i == wide % 8)
 
-    for h in range(2):
+    for h in (1, 0):
         if h == 0:
             for copy in x_keep:
                 copy.wait()
@@ -575,7 +575,7 @@
             f_send.at[h, piece], f_recv.at[h, piece], (wide, buddy),
         )
 
-    for h in range(2):
+    for h in (1, 0):
         def wait_row(k, carry):
             mine = own_target & (k == kv)
 
@@ -596,7 +596,7 @@
             ring_copy(h, direction, y).start()
         forward(h, y, core).start()
 
-    for h in range(2):
+    for h in (1, 0):
         ring_copy(h, h, behind[h]).wait_recv()
         on_copy(h, behind[h]).start()
         forward(h, behind[h], core).start()
@@ -611,13 +611,13 @@
         )
 
     total = jnp.zeros((HALF, 512), jnp.float32)
-    for h in range(2):
+    for h in (1, 0):
         ring_copy(h, 1 - h, behind[1 - h]).wait_recv()
         forward(h, behind[1 - h], core).start()
         on_copy(h, (y + 2) % NY).wait_recv()
         forward(h, (y + 2) % NY, core).start()
         total = total + product(core, h)
-    for h in range(2):
+    for h in (1, 0):
         for piece in range(NY):
             forward(h, piece, 1 - core).wait_recv()
         total = total + product(1 - core, h)
@@ -681,7 +681,7 @@
 def shards(queries, span_keys, span_values, cache_keys, cache_values, chosen, out_weight):
     weight = lax.all_gather(out_weight, "wide", axis=0, tiled=True)
     q, k_pair, v_pair, span = spread(queries, span_keys, span_values, cache_keys, cache_values)
-    part, lse = attend(chosen, q, cache_keys, cache_values, k_pair, v_pair, span)
+    part, lse = attend(chosen.T, q, cache_keys, cache_values, k_pair, v_pair, span)
     return finish(part, lse, weight)
 
 

time: 126 us -> 123 us (0.976)
  waiting for transfers between devices: 12.5 us -> 7.02 us
  Pallas kernels: 96.6 us -> 100 us
  local copies, waits for them, and re-layouts: 3.01 us -> 1.67 us
    pallas_call x1, Pallas kernels: 16.5 us -> 22.1 us  [attend(): pl.pallas_call(attend_kernel, out_shape=[jax.ShapeDtypeStruct((2, NW, NY,...]
    all_gather x1, waiting for transfers between devices: 11.8 us -> 6.31 us  [shards(): weight = lax.all_gather(out_weight, 'wide', axis=0, tiled=True)]
    pallas_call x1, Pallas kernels: 50.6 us -> 48.5 us  [finish(): pl.pallas_call(finish_kernel, out_shape=jax.ShapeDtypeStruct((HALF, 512),...]
    unnamed x2 -> x1, local copies, waits for them, and re-layouts: 3.01 us -> 1.67 us
  transfers between devices with their start and end apart: 1 -> 1, of which waited for: 1 -> 1; matrix products, arithmetic and copies ran while one was open for 1% -> 0% of each run, Pallas kernels for 37% -> 42%
where the time goes in v8:
time: 123 us
  Pallas kernels  100 us (81%)
  between operations  13.4 us (11%)
  waiting for transfers between devices  7.02 us (6%)
  local copies, waits for them, and re-layouts  1.67 us (1%)
    pallas_call x1, Pallas kernels, finish(): pl.pallas_call(finish_kernel, out_shape=jax.ShapeDtypeStruct((HALF, 512),...  48.5 us
    pallas_call x1, Pallas kernels, spread(): pl.pallas_call(spread_kernel, out_shape=[shape(NW, HALF, 2 * HD), shape(K...  29.8 us
    pallas_call x1, Pallas kernels, attend(): pl.pallas_call(attend_kernel, out_shape=[jax.ShapeDtypeStruct((2, NW, NY,...  22.1 us
    all_gather x1, waiting for transfers between devices, shards(): weight = lax.all_gather(out_weight, 'wide', axis=0, tiled=True)  6.31 us
  transfers between devices with their start and end apart: 1, of which 1 were waited for; matrix products, arithmetic and copies ran while one was open for 0% of the time, Pallas kernels for 42%

profile of v8, /device:TPU:1, one launch (start us, length us, event | category | flops | bytes accessed | tf_op | source)
XLA Modules:
  0.0 122.5 jit_solution(3730999964299515200)
XLA Ops:
  6.5 0.0 all-gather.2.cloned.1.call-start
  6.5 0.7 all-gather.2.cloned.1.call-update
  7.3 29.8 %shard_map.73 = (bf16[16,256,256]{2,1,0:T(8,128)(2,1)}, bf16[4096,128]{1,0:T(8,128)(2,1)}, bf16[4096,128]{1,0:T(8,128)(2,1)}, bf16[2,2,4,64,128]{4,3,2,1,0:T(8,128)(2,1)}) custom-call(bf16[256,4096]{1,0:T(8,128)(2,1)} %queries.1, bf16[256,1024]{1,0:T(8,128)(2,1)} %span_k.1, bf16[256,1024]{1,0:T(8,128)(2,1)} %span_v.1, bf16[4096,128]{1,0:T(8,128)(2,1)} %k_own.1, ...), custom_call_target="tpu_custom_call" | custom-call | tf_op jit(solution)/shard_map/pallas_call | solution.py:222
  37.1 22.1 %shard_map.74 = (bf16[2,16,4,64,128]{4,3,2,1,0:T(8,128)(2,1)}, f32[2,4,2,8,128]{4,3,2,1,0:T(8,128)}) custom-call(s32[3,8]{1,0:T(4,128)} %bitcast.3, bf16[16,256,256]{2,1,0:T(8,128)(2,1)} %get-tuple-element.11.q, bf16[4096,128]{1,0:T(8,128)(2,1)} %k_own.1, bf16[4096,128]{1,0:T(8,128)(2,1)} %v_own.1, bf16[4096,128]{1,0:T(8,128)(2,1)} %get-tuple-element.12.k_pair, ...), custom_call_target="tpu_custom_call" | custom-call | flops 14000000000 | bytes 10485760 | tf_op jit(solution)/shard_map/pallas_call | solution.py:361
  59.2 6.3 %all-gather.2.cloned.1.call-done = bf16[4096,512]{1,0:T(8,128)(2,1)} async-done(((bf16[256,512]{1,0:T(8,128)(2,1)}), bf16[4096,512]{1,0:T(8,128)(2,1)}) %all-gather.2.cloned.1.call-update) | async-done | bytes 4194320 | tf_op jit(solution)/shard_map/all_gather | solution.py:682
  65.5 48.5 %shard_map.75 = bf16[256,512]{1,0:T(8,128)(2,1)} custom-call(bf16[2,16,4,64,128]{4,3,2,1,0:T(8,128)(2,1)} %get-tuple-element.15.part, f32[2,4,2,8,128]{4,3,2,1,0:T(8,128)} %get-tuple-element.16.lse, bf16[8,4,128,512]{3,2,1,0:T(8,128)(2,1)} %bitcast.2), custom_call_target="tpu_custom_call" | custom-call | tf_op jit(solution)/shard_map/pallas_call | solution.py:650
  114.0 1.7 %copy.9 = bf16[256,512]{1,0:T(8,128)(2,1)} copy(bf16[256,512]{1,0:T(8,128)(2,1)} %shard_map.75) | data formatting | bytes 524288
Async XLA Ops:
  6.5 59.0 %all-gather.2.cloned.1.call-start = ((), (), s32[]{:S(2)}) async-start(), calls=%async_computation | async-start | bytes 4456448 | tf_op jit(solution)/shard_map/all_gather | solution.py:682
Sparse Core Ops, SparseCore 0:
  9.5 55.9 all-gather.1

commit v9 on v8

--- a/solution.py
+++ b/solution.py
@@ -388,13 +388,11 @@
     x_in, y_in, x_mid, y_mid, x_last, y_last, lx_in, ly_in, lx_mid, ly_mid, lx_last, ly_last,
     w_in, rows_out, rows_in,
     x_send, x_recv, y_send, y_recv, xm_send, xm_recv, ym_send, ym_recv,
-    a_send, a_recv, ring_send, ring_recv, on_send, on_recv, f_send, f_recv, local_sem,
+    a_send, a_recv, f_send, f_recv, local_sem,
 ):
     wide, narrow, y, core = place()
     buddy = y * 2 + 1 - core
     kv, side = wide // 2, wide % 2
-    ring = [(y + 1) % NY, (y + NY - 1) % NY]
-    behind = ring[::-1]
     own_target = wide // 8 == side
     barrier = pltpu.get_barrier_semaphore()
 
@@ -415,16 +413,20 @@
     for device in (across, *(along(step) for step in range(1, NY))):
         pl.semaphore_signal(barrier, inc=1, device_id=device, device_id_type=MESH)
 
-    def greet_source(s, carry):
-        @pl.when(jnp.logical_not(own_target & (s == kv)))
+    def greet_source(n, carry):
+        s, step = n // NY, n % NY
+
+        @pl.when(jnp.logical_not(own_target & (s == kv) & (step == 0)))
         def _():
-            pl.semaphore_signal(barrier, inc=1, device_id=(s * 2 + wide // 8, narrow), device_id_type=MESH)
+            pl.semaphore_signal(
+                barrier, inc=1, device_id=(s * 2 + wide // 8, (y + step) % NY * 2 + core), device_id_type=MESH
+            )
 
         return carry
 
-    lax.fori_loop(0, 8, greet_source, 0)
+    lax.fori_loop(0, 8 * NY, greet_source, 0)
     pl.semaphore_signal(barrier, inc=1, device_id=(wide, buddy), device_id_type=MESH)
-    pl.semaphore_wait(barrier, 13 - own_target.astype(jnp.int32))
+    pl.semaphore_wait(barrier, 37 - own_target.astype(jnp.int32))
 
     x_copies = [
         remote(part.at[0, pl.ds((1 - side) * 8, 8)], x_in.at[1], x_send.at[0], x_recv.at[0], across),
@@ -514,16 +516,18 @@
     for copy in ym_copies:
         copy.start()
 
-    def row_copy(i, h):
+    def row_copy(n, h):
+        i, step = n // NY, n % NY
         return remote(
-            rows_out.at[h, i], rows_in.at[core, h, y, kv], a_send.at[i, h], a_recv.at[kv, h], (side * 8 + i, narrow)
+            rows_out.at[h, i], rows_in.at[core, h, y, kv], a_send.at[n, h], a_recv.at[y, kv, h],
+            (side * 8 + i, (y + step) % NY * 2 + core),
         )
 
     def own_copy(h):
         return pltpu.make_async_copy(rows_out.at[h, wide % 8], rows_in.at[core, h, y, kv], local_sem.at[7 + h])
 
-    def local(i):
-        return own_target & (i == wide % 8)
+    def local(n):
+        return own_target & (n == wide % 8 * NY)
 
     for h in (1, 0):
         if h == 0:
@@ -553,21 +557,10 @@
 
             return carry
 
-        lax.fori_loop(0, 8, start_row, 0)
+        lax.fori_loop(0, 8 * NY, start_row, 0)
 
     def batch(side_core, h, piece):
         return rows_in.at[side_core, h, piece]
-
-    def ring_copy(h, direction, piece):
-        return remote(
-            batch(core, h, piece), batch(core, h, piece),
-            ring_send.at[h, direction], ring_recv.at[h, direction], (wide, ring[direction] * 2 + core),
-        )
-
-    def on_copy(h, piece):
-        return remote(
-            batch(core, h, piece), batch(core, h, piece), on_send.at[h], on_recv.at[h], (wide, ring[h] * 2 + core)
-        )
 
     def forward(h, piece, side_core):
         return remote(
@@ -575,32 +568,6 @@
             f_send.at[h, piece], f_recv.at[h, piece], (wide, buddy),
         )
 
-    for h in (1, 0):
-        def wait_row(k, carry):
-            mine = own_target & (k == kv)
-
-            @pl.when(mine)
-            def _():
-                own_copy(h).wait()
-
-            @pl.when(jnp.logical_not(mine))
-            def _():
-                remote(
-                    rows_out.at[h, 0], rows_in.at[core, h, y, k], a_send.at[0, h], a_recv.at[k, h], (wide, buddy)
-                ).wait_recv()
-
-            return carry
-
-        lax.fori_loop(0, 8, wait_row, 0)
-        for direction in range(2):
-            ring_copy(h, direction, y).start()
-        forward(h, y, core).start()
-
-    for h in (1, 0):
-        ring_copy(h, h, behind[h]).wait_recv()
-        on_copy(h, behind[h]).start()
-        forward(h, behind[h], core).start()
-
     for copy in fetches:
         copy.wait()
 
@@ -612,10 +579,27 @@
 
     total = jnp.zeros((HALF, 512), jnp.float32)
     for h in (1, 0):
-        ring_copy(h, 1 - h, behind[1 - h]).wait_recv()
-        forward(h, behind[1 - h], core).start()
-        on_copy(h, (y + 2) % NY).wait_recv()
-        forward(h, (y + 2) % NY, core).start()
+        for step in (0, 1, 3, 2):
+            piece = (y + step) % NY
+
+            def wait_row(k, carry):
+                mine = own_target & (k == kv) & (step == 0)
+
+                @pl.when(mine)
+                def _():
+                    own_copy(h).wait()
+
+                @pl.when(jnp.logical_not(mine))
+                def _():
+                    remote(
+                        rows_out.at[h, 0], rows_in.at[core, h, piece, k],
+                        a_send.at[0, h], a_recv.at[piece, k, h], (wide, buddy),
+                    ).wait_recv()
+
+                return carry
+
+            lax.fori_loop(0, 8, wait_row, 0)
+            forward(h, piece, core).start()
         total = total + product(core, h)
     for h in (1, 0):
         for piece in range(NY):
@@ -636,10 +620,7 @@
 
             return carry
 
-        lax.fori_loop(0, 8, drain_row, 0)
-        for direction in range(2):
-            ring_copy(h, direction, y).wait_send()
-        on_copy(h, behind[h]).wait_send()
+        lax.fori_loop(0, 8 * NY, drain_row, 0)
         for piece in range(NY):
             forward(h, piece, core).wait_send()
 
@@ -669,7 +650,7 @@
             pltpu.VMEM((2, 8, PIECE, HD), jnp.bfloat16),
             pltpu.VMEM((2, 2, NY, KVH, PIECE, HD), jnp.bfloat16),
             dma((2,)), dma((2,)), dma((NY, 2)), dma((NY, 2)), dma((NY, 2)), dma((NY, 2)), dma((2,)), dma((2,)),
-            dma((8, 2)), dma((8, 2)), dma((2, 2)), dma((2, 2)), dma((2,)), dma((2,)),
+            dma((8 * NY, 2)), dma((NY, KVH, 2)),
             dma((2, NY)), dma((2, NY)), dma((12,)),
         ],
         compiler_params=pltpu.CompilerParams(

time: 123 us -> 130 us (1.057)
  waiting for transfers between devices: 7.02 us -> 12.7 us
  Pallas kernels: 100 us -> 102 us
    pallas_call x1, Pallas kernels: 48.5 us -> 56 us  [finish(): pl.pallas_call(finish_kernel, out_shape=jax.ShapeDtypeStruct((HALF, 512),...]
    all_gather x1, waiting for transfers between devices: 6.31 us -> 11.9 us  [shards(): weight = lax.all_gather(out_weight, 'wide', axis=0, tiled=True)]
    pallas_call x1, Pallas kernels: 22.1 us -> 16.5 us  [attend(): pl.pallas_call(attend_kernel, out_shape=[jax.ShapeDtypeStruct((2, NW, NY,...]
  transfers between devices with their start and end apart: 1 -> 1, of which waited for: 1 -> 1; matrix products, arithmetic and copies ran while one was open for 0% -> 0% of each run, Pallas kernels for 42% -> 36%
where the time goes in v9:
time: 130 us
  Pallas kernels  102 us (78%)
  between operations  13.4 us (10%)
  waiting for transfers between devices  12.7 us (10%)
  local copies, waits for them, and re-layouts  1.67 us (1%)
    pallas_call x1, Pallas kernels, finish(): pl.pallas_call(finish_kernel, out_shape=jax.ShapeDtypeStruct((HALF, 512),...  56 us
    pallas_call x1, Pallas kernels, spread(): pl.pallas_call(spread_kernel, out_shape=[shape(NW, HALF, 2 * HD), shape(K...  29.8 us
    pallas_call x1, Pallas kernels, attend(): pl.pallas_call(attend_kernel, out_shape=[jax.ShapeDtypeStruct((2, NW, NY,...  16.5 us
    all_gather x1, waiting for transfers between devices, shards(): weight = lax.all_gather(out_weight, 'wide', axis=0, tiled=True)  11.9 us
  transfers between devices with their start and end apart: 1, of which 1 were waited for; matrix products, arithmetic and copies ran while one was open for 0% of the time, Pallas kernels for 36%

profile of v9, /device:TPU:1, one launch (start us, length us, event | category | flops | bytes accessed | tf_op | source)
XLA Modules:
  0.0 130.1 jit_solution(9104732327761175489)
XLA Ops:
  6.5 0.0 all-gather.2.cloned.1.call-start
  6.5 0.7 all-gather.2.cloned.1.call-update
  7.3 29.8 %shard_map.73 = (bf16[16,256,256]{2,1,0:T(8,128)(2,1)}, bf16[4096,128]{1,0:T(8,128)(2,1)}, bf16[4096,128]{1,0:T(8,128)(2,1)}, bf16[2,2,4,64,128]{4,3,2,1,0:T(8,128)(2,1)}) custom-call(bf16[256,4096]{1,0:T(8,128)(2,1)} %queries.1, bf16[256,1024]{1,0:T(8,128)(2,1)} %span_k.1, bf16[256,1024]{1,0:T(8,128)(2,1)} %span_v.1, bf16[4096,128]{1,0:T(8,128)(2,1)} %k_own.1, ...), custom_call_target="tpu_custom_call" | custom-call | tf_op jit(solution)/shard_map/pallas_call | solution.py:222
  37.1 16.5 %shard_map.74 = (bf16[2,16,4,64,128]{4,3,2,1,0:T(8,128)(2,1)}, f32[2,4,2,8,128]{4,3,2,1,0:T(8,128)}) custom-call(s32[3,8]{1,0:T(4,128)} %bitcast.3, bf16[16,256,256]{2,1,0:T(8,128)(2,1)} %get-tuple-element.11.q, bf16[4096,128]{1,0:T(8,128)(2,1)} %k_own.1, bf16[4096,128]{1,0:T(8,128)(2,1)} %v_own.1, bf16[4096,128]{1,0:T(8,128)(2,1)} %get-tuple-element.12.k_pair, ...), custom_call_target="tpu_custom_call" | custom-call | flops 14000000000 | bytes 10485760 | tf_op jit(solution)/shard_map/pallas_call | solution.py:361
  53.6 11.9 %all-gather.2.cloned.1.call-done = bf16[4096,512]{1,0:T(8,128)(2,1)} async-done(((bf16[256,512]{1,0:T(8,128)(2,1)}), bf16[4096,512]{1,0:T(8,128)(2,1)}) %all-gather.2.cloned.1.call-update) | async-done | bytes 4194320 | tf_op jit(solution)/shard_map/all_gather | solution.py:663
  65.5 56.0 %shard_map.75 = bf16[256,512]{1,0:T(8,128)(2,1)} custom-call(bf16[2,16,4,64,128]{4,3,2,1,0:T(8,128)(2,1)} %get-tuple-element.15.part, f32[2,4,2,8,128]{4,3,2,1,0:T(8,128)} %get-tuple-element.16.lse, bf16[8,4,128,512]{3,2,1,0:T(8,128)(2,1)} %bitcast.2), custom_call_target="tpu_custom_call" | custom-call | tf_op jit(solution)/shard_map/pallas_call | solution.py:631
  121.6 1.7 %copy.9 = bf16[256,512]{1,0:T(8,128)(2,1)} copy(bf16[256,512]{1,0:T(8,128)(2,1)} %shard_map.75) | data formatting | bytes 524288
Async XLA Ops:
  6.5 59.0 %all-gather.2.cloned.1.call-start = ((), (), s32[]{:S(2)}) async-start(), calls=%async_computation | async-start | bytes 4456448 | tf_op jit(solution)/shard_map/all_gather | solution.py:663
Sparse Core Ops, SparseCore 0:
  9.5 55.9 all-gather.1

commit v10 on v8

--- a/solution.py
+++ b/solution.py
@@ -616,12 +616,13 @@
         forward(h, behind[1 - h], core).start()
         on_copy(h, (y + 2) % NY).wait_recv()
         forward(h, (y + 2) % NY, core).start()
+    for h in (1, 0):
         total = total + product(core, h)
     for h in (1, 0):
         for piece in range(NY):
             forward(h, piece, 1 - core).wait_recv()
         total = total + product(1 - core, h)
-    result[...] = total.astype(jnp.bfloat16)
+    result[...] = total
 
     for copy in (*x_copies, *ym_copies):
         copy.wait_send()
@@ -649,7 +650,7 @@
     dma = pltpu.SemaphoreType.DMA
     return pl.pallas_call(
         finish_kernel,
-        out_shape=jax.ShapeDtypeStruct((HALF, 512), jnp.bfloat16),
+        out_shape=jax.ShapeDtypeStruct((HALF, 512), jnp.float32),
         in_specs=[anywhere] * 3,
         out_specs=pl.BlockSpec(memory_space=pltpu.VMEM),
         scratch_shapes=[
@@ -682,7 +683,7 @@
     weight = lax.all_gather(out_weight, "wide", axis=0, tiled=True)
     q, k_pair, v_pair, span = spread(queries, span_keys, span_values, cache_keys, cache_values)
     part, lse = attend(chosen.T, q, cache_keys, cache_values, k_pair, v_pair, span)
-    return finish(part, lse, weight)
+    return finish(part, lse, weight).astype(jnp.bfloat16)
 
 
 def solution(mesh):

time: 123 us -> 129 us (1.049)
  waiting for transfers between devices: 7.02 us -> 12.7 us
  other arithmetic: 0 us -> 1.78 us
  local copies, waits for them, and re-layouts: 1.67 us -> 0 us
    pallas_call x1, Pallas kernels: 48.5 us -> 55.1 us  [finish(): pl.pallas_call(finish_kernel, out_shape=jax.ShapeDtypeStruct((HALF, 512),...]
    all_gather x1, waiting for transfers between devices: 6.31 us -> 11.9 us  [shards(): weight = lax.all_gather(out_weight, 'wide', axis=0, tiled=True)]
    pallas_call x1, Pallas kernels: 22.1 us -> 16.5 us  [attend(): pl.pallas_call(attend_kernel, out_shape=[jax.ShapeDtypeStruct((2, NW, NY,...]
    convert_element_type x0 -> x1, other arithmetic: none -> 1.78 us  [shards(): return finish(part, lse, weight).astype(jnp.bfloat16)]
    unnamed x1 -> x0, local copies, waits for them, and re-layouts: 1.67 us -> none
  transfers between devices with their start and end apart: 1 -> 1, of which waited for: 1 -> 1; matrix products, arithmetic and copies ran while one was open for 0% -> 0% of each run, Pallas kernels for 42% -> 36%
where the time goes in v10:
time: 129 us
  Pallas kernels  101 us (78%)
  between operations  13.4 us (10%)
  waiting for transfers between devices  12.7 us (10%)
  other arithmetic  1.78 us (1%)
    pallas_call x1, Pallas kernels, finish(): pl.pallas_call(finish_kernel, out_shape=jax.ShapeDtypeStruct((HALF, 512),...  55.1 us
    pallas_call x1, Pallas kernels, spread(): pl.pallas_call(spread_kernel, out_shape=[shape(NW, HALF, 2 * HD), shape(K...  29.8 us
    pallas_call x1, Pallas kernels, attend(): pl.pallas_call(attend_kernel, out_shape=[jax.ShapeDtypeStruct((2, NW, NY,...  16.5 us
    all_gather x1, waiting for transfers between devices, shards(): weight = lax.all_gather(out_weight, 'wide', axis=0, tiled=True)  11.9 us
  transfers between devices with their start and end apart: 1, of which 1 were waited for; matrix products, arithmetic and copies ran while one was open for 0% of the time, Pallas kernels for 36%

profile of v10, /device:TPU:1, one launch (start us, length us, event | category | flops | bytes accessed | tf_op | source)
XLA Modules:
  0.0 129.2 jit_solution(6344154488495356042)
XLA Ops:
  6.5 0.0 all-gather.2.cloned.1.call-start
  6.5 0.7 all-gather.2.cloned.1.call-update
  7.3 29.8 %shard_map.73 = (bf16[16,256,256]{2,1,0:T(8,128)(2,1)}, bf16[4096,128]{1,0:T(8,128)(2,1)}, bf16[4096,128]{1,0:T(8,128)(2,1)}, bf16[2,2,4,64,128]{4,3,2,1,0:T(8,128)(2,1)}) custom-call(bf16[256,4096]{1,0:T(8,128)(2,1)} %queries.1, bf16[256,1024]{1,0:T(8,128)(2,1)} %span_k.1, bf16[256,1024]{1,0:T(8,128)(2,1)} %span_v.1, bf16[4096,128]{1,0:T(8,128)(2,1)} %k_own.1, ...), custom_call_target="tpu_custom_call" | custom-call | tf_op jit(solution)/shard_map/pallas_call | solution.py:222
  37.1 16.5 %shard_map.74 = (bf16[2,16,4,64,128]{4,3,2,1,0:T(8,128)(2,1)}, f32[2,4,2,8,128]{4,3,2,1,0:T(8,128)}) custom-call(s32[3,8]{1,0:T(4,128)} %bitcast.3, bf16[16,256,256]{2,1,0:T(8,128)(2,1)} %get-tuple-element.11.q, bf16[4096,128]{1,0:T(8,128)(2,1)} %k_own.1, bf16[4096,128]{1,0:T(8,128)(2,1)} %v_own.1, bf16[4096,128]{1,0:T(8,128)(2,1)} %get-tuple-element.12.k_pair, ...), custom_call_target="tpu_custom_call" | custom-call | flops 14000000000 | bytes 10485760 | tf_op jit(solution)/shard_map/pallas_call | solution.py:361
  53.6 11.9 %all-gather.2.cloned.1.call-done = bf16[4096,512]{1,0:T(8,128)(2,1)} async-done(((bf16[256,512]{1,0:T(8,128)(2,1)}), bf16[4096,512]{1,0:T(8,128)(2,1)}) %all-gather.2.cloned.1.call-update) | async-done | bytes 4194320 | tf_op jit(solution)/shard_map/all_gather | solution.py:683
  65.5 55.1 %shard_map.75 = f32[256,512]{1,0:T(8,128)} custom-call(bf16[2,16,4,64,128]{4,3,2,1,0:T(8,128)(2,1)} %get-tuple-element.15.part, f32[2,4,2,8,128]{4,3,2,1,0:T(8,128)} %get-tuple-element.16.lse, bf16[8,4,128,512]{3,2,1,0:T(8,128)(2,1)} %bitcast.2), custom_call_target="tpu_custom_call" | custom-call | tf_op jit(solution)/shard_map/pallas_call | solution.py:651
  120.6 1.8 %convert_element_type.3 = bf16[256,512]{1,0:T(8,128)(2,1)} convert(f32[256,512]{1,0:T(8,128)} %shard_map.75) | non-fusion elementwise | flops 131072 | bytes 786432 | tf_op jit(solution)/shard_map/convert_element_type | solution.py:686
Async XLA Ops:
  6.5 59.0 %all-gather.2.cloned.1.call-start = ((), (), s32[]{:S(2)}) async-start(), calls=%async_computation | async-start | bytes 4456448 | tf_op jit(solution)/shard_map/all_gather | solution.py:683
Sparse Core Ops, SparseCore 0:
  9.5 55.9 all-gather.1

commit v11 on v8

--- a/solution.py
+++ b/solution.py
@@ -616,6 +616,7 @@
         forward(h, behind[1 - h], core).start()
         on_copy(h, (y + 2) % NY).wait_recv()
         forward(h, (y + 2) % NY, core).start()
+    for h in (1, 0):
         total = total + product(core, h)
     for h in (1, 0):
         for piece in range(NY):

time: 123 us -> 128 us (1.041); the launches traced: 123 us -> 129 us
  waiting for transfers between devices: 7.02 us -> 12.7 us
    pallas_call x1, Pallas kernels: 48.5 us -> 55 us  [finish(): pl.pallas_call(finish_kernel, out_shape=jax.ShapeDtypeStruct((HALF, 512),...]
    all_gather x1, waiting for transfers between devices: 6.31 us -> 11.9 us  [shards(): weight = lax.all_gather(out_weight, 'wide', axis=0, tiled=True)]
    pallas_call x1, Pallas kernels: 22.1 us -> 16.5 us  [attend(): pl.pallas_call(attend_kernel, out_shape=[jax.ShapeDtypeStruct((2, NW, NY,...]
  transfers between devices with their start and end apart: 1 -> 1, of which waited for: 1 -> 1; matrix products, arithmetic and copies ran while one was open for 0% -> 0% of each run, Pallas kernels for 42% -> 36%
where the time goes in v11:
time: 128 us; the launch traced here: 129 us
  Pallas kernels  101 us (79%)
  between operations  13.4 us (10%)
  waiting for transfers between devices  12.7 us (10%)
  local copies, waits for them, and re-layouts  1.67 us (1%)
    pallas_call x1, Pallas kernels, finish(): pl.pallas_call(finish_kernel, out_shape=jax.ShapeDtypeStruct((HALF, 512),...  55 us
    pallas_call x1, Pallas kernels, spread(): pl.pallas_call(spread_kernel, out_shape=[shape(NW, HALF, 2 * HD), shape(K...  29.8 us
    pallas_call x1, Pallas kernels, attend(): pl.pallas_call(attend_kernel, out_shape=[jax.ShapeDtypeStruct((2, NW, NY,...  16.5 us
    all_gather x1, waiting for transfers between devices, shards(): weight = lax.all_gather(out_weight, 'wide', axis=0, tiled=True)  11.9 us
  transfers between devices with their start and end apart: 1, of which 1 were waited for; matrix products, arithmetic and copies ran while one was open for 0% of the time, Pallas kernels for 36%

profile of v11, /device:TPU:1, one launch (start us, length us, event | category | flops | bytes accessed | tf_op | source)
XLA Modules:
  0.0 129.0 jit_solution(16534406335086130198)
XLA Ops:
  6.5 0.0 all-gather.2.cloned.1.call-start
  6.5 0.7 all-gather.2.cloned.1.call-update
  7.3 29.8 %shard_map.73 = (bf16[16,256,256]{2,1,0:T(8,128)(2,1)}, bf16[4096,128]{1,0:T(8,128)(2,1)}, bf16[4096,128]{1,0:T(8,128)(2,1)}, bf16[2,2,4,64,128]{4,3,2,1,0:T(8,128)(2,1)}) custom-call(bf16[256,4096]{1,0:T(8,128)(2,1)} %queries.1, bf16[256,1024]{1,0:T(8,128)(2,1)} %span_k.1, bf16[256,1024]{1,0:T(8,128)(2,1)} %span_v.1, bf16[4096,128]{1,0:T(8,128)(2,1)} %k_own.1, ...), custom_call_target="tpu_custom_call" | custom-call | tf_op jit(solution)/shard_map/pallas_call | solution.py:222
  37.1 16.5 %shard_map.74 = (bf16[2,16,4,64,128]{4,3,2,1,0:T(8,128)(2,1)}, f32[2,4,2,8,128]{4,3,2,1,0:T(8,128)}) custom-call(s32[3,8]{1,0:T(4,128)} %bitcast.3, bf16[16,256,256]{2,1,0:T(8,128)(2,1)} %get-tuple-element.11.q, bf16[4096,128]{1,0:T(8,128)(2,1)} %k_own.1, bf16[4096,128]{1,0:T(8,128)(2,1)} %v_own.1, bf16[4096,128]{1,0:T(8,128)(2,1)} %get-tuple-element.12.k_pair, ...), custom_call_target="tpu_custom_call" | custom-call | flops 14000000000 | bytes 10485760 | tf_op jit(solution)/shard_map/pallas_call | solution.py:361
  53.6 11.9 %all-gather.2.cloned.1.call-done = bf16[4096,512]{1,0:T(8,128)(2,1)} async-done(((bf16[256,512]{1,0:T(8,128)(2,1)}), bf16[4096,512]{1,0:T(8,128)(2,1)}) %all-gather.2.cloned.1.call-update) | async-done | bytes 4194320 | tf_op jit(solution)/shard_map/all_gather | solution.py:683
  65.5 55.0 %shard_map.75 = bf16[256,512]{1,0:T(8,128)(2,1)} custom-call(bf16[2,16,4,64,128]{4,3,2,1,0:T(8,128)(2,1)} %get-tuple-element.15.part, f32[2,4,2,8,128]{4,3,2,1,0:T(8,128)} %get-tuple-element.16.lse, bf16[8,4,128,512]{3,2,1,0:T(8,128)(2,1)} %bitcast.2), custom_call_target="tpu_custom_call" | custom-call | tf_op jit(solution)/shard_map/pallas_call | solution.py:651
  120.5 1.7 %copy.9 = bf16[256,512]{1,0:T(8,128)(2,1)} copy(bf16[256,512]{1,0:T(8,128)(2,1)} %shard_map.75) | data formatting | bytes 524288
Async XLA Ops:
  6.5 59.0 %all-gather.2.cloned.1.call-start = ((), (), s32[]{:S(2)}) async-start(), calls=%async_computation | async-start | bytes 4456448 | tf_op jit(solution)/shard_map/all_gather | solution.py:683
Sparse Core Ops, SparseCore 0:
  9.5 55.9 all-gather.1
